TPU v7x, 512 devices: a whole 4x4x16 slice. The times are simulated.
512 devices in a mesh: band: 8 (over y, x_hi), pw: 64 (over z, x_lo, core).
Axes of the slice: x: 4 (x_hi: 2, x_lo: 2; x = x_hi * 2 + x_lo), y: 4, z: 16, core: 2. Of those that a mesh axis runs over, the one named last changes fastest.
Arguments:
- block: bfloat16 [64, 2, 2560, 128], P('band', None, 'pw'), may hold values from -6 to 6
- bands: bfloat16 [256, 2, 2560, 128], P('band', None, 'pw'), may hold values from -0.01953125 to 0.01953125
- potential: float32 [128, 128, 128], P('pw'), may hold values from -4 to 1
- stick_cells: int32 [2560], P('pw'), may hold values from 0 to 16383, as said below
- sphere_mask: int32 [2560, 128], P('pw'), may hold values from 0 to 1, as said below
Outputs:
- applied: bfloat16 [64, 2, 2560, 128], P('band', None, 'pw')
- correlation: float32 [2, 256, 64], P(None, 'band')
- subspace: float32 [2, 256, 64], P(None, 'band')
Inputs may be any that keep to these rules, and one draw needn't show every extreme that they name: `stick_cells`: the 2560 distinct columns with the smallest g(x)^2 + g(y)^2, ties in random order, placed in random order over the sticks. `sphere_mask`: 1 exactly where g(cx)^2 + g(cy)^2 + g(k)^2 <= 32^2 for stick s's column (cx, cy) and index k, else 0.
All inputs are finite; a program needn't handle non-finite values.
Results may differ from a plain program's by a relative error of at most 0.002.
Values may be sent and summed in bfloat16 or wider, within the bound.
No kernel may reach another device: no remote copies, remote signals or barrier semaphores. Data moves between devices by JAX's collectives and lax.ppermute only.
A program may use at most 128 MiB of HBM per device.

v0:
```python
import math

import jax
import jax.numpy as jnp
from jax import lax
from jax.sharding import PartitionSpec as P


def signed_frequency(index, period):
    return jnp.where(index < period // 2, index, index - period)


def phase_table(first, second, period, sign, factor):
    turns = jnp.mod(first[:, None] * second[None, :], period).astype(jnp.float32)
    angle = turns * (2.0 * math.pi / period)
    cosine = jnp.cos(angle) * factor
    sine = jnp.sin(angle) * factor * sign
    upper = jnp.stack([cosine, sine], axis=1)
    lower = jnp.stack([-sine, cosine], axis=1)
    return jnp.stack([upper, lower], axis=0)


def inner_products(left, right):
    left_rows = left.shape[0]
    right_rows = right.shape[0]
    turned = jnp.stack([right[:, 1], -right[:, 0]], axis=1)
    joined = jnp.concatenate([right, turned], axis=0).reshape(2 * right_rows, -1)
    result = jnp.dot(left.reshape(left_rows, -1), joined.T, preferred_element_type=jnp.float32)
    return jnp.transpose(result.reshape(left_rows, 2, right_rows), (1, 0, 2))


def per_device(block, bands, potential, stick_cells, sphere_mask):
    highest = lax.Precision.HIGHEST
    extent = block.shape[3]
    radius = extent // 4
    window = extent // 2
    planes_dev = potential.shape[0]
    padded = planes_dev * lax.axis_size("pw")
    volume = float(extent) ** 3
    all_cells = lax.all_gather(stick_cells, "pw", axis=0, tiled=True)
    window_x = signed_frequency(all_cells // extent, extent) + radius
    place = window_x * extent + all_cells % extent
    own_x = signed_frequency(stick_cells // extent, extent)
    own_y = signed_frequency(stick_cells % extent, extent)
    depth = signed_frequency(jnp.arange(extent, dtype=jnp.int32), extent)
    squares = (own_x * own_x + own_y * own_y)[:, None] + (depth * depth)[None, :]
    kinetic = 2.0 / (radius * radius) * squares.astype(jnp.float32)
    weights = sphere_mask.astype(jnp.float32)
    masked = block * sphere_mask.astype(jnp.bfloat16)[None, None]
    frequencies = jnp.arange(extent, dtype=jnp.int32)
    slots = jnp.arange(padded, dtype=jnp.int32)
    live = (slots < extent).astype(jnp.float32)
    window_freq = jnp.arange(window, dtype=jnp.int32) - radius
    depth_inverse = phase_table(frequencies, slots, extent, 1.0, live[None, :] / volume)
    depth_forward = phase_table(slots, frequencies, extent, -1.0, live[:, None])
    across_inverse = phase_table(frequencies, frequencies, extent, 1.0, 1.0)
    across_forward = phase_table(frequencies, frequencies, extent, -1.0, 1.0)
    down_inverse = phase_table(window_freq, frequencies, extent, 1.0, 1.0)
    down_forward = phase_table(frequencies, window_freq, extent, -1.0, 1.0)
    masked_values = masked.astype(jnp.float32)
    stick_field = jnp.einsum("bpsk,pkqz->zbqs", masked_values, depth_inverse, precision=highest)
    portion = lax.all_to_all(stick_field, "pw", split_axis=0, concat_axis=3, tiled=True)
    items = portion.shape[1]
    grid = jnp.zeros((planes_dev, items, 2, window * extent), jnp.float32)
    grid = grid.at[:, :, :, place].set(portion).reshape(planes_dev, items, 2, window, extent)
    across = jnp.einsum("zbpxk,pkqy->zbqxy", grid, across_inverse, precision=highest)
    field = jnp.einsum("zbpwy,pwqx->zbqxy", across, down_inverse, precision=highest)
    field = field * potential[:, None, None]
    folded = jnp.einsum("zbpxy,pxqw->zbqwy", field, down_forward, precision=highest)
    spectrum = jnp.einsum("zbpwy,pyqk->zbqwk", folded, across_forward, precision=highest)
    picked = spectrum.reshape(planes_dev, items, 2, window * extent)[:, :, :, place]
    returned = lax.all_to_all(picked, "pw", split_axis=3, concat_axis=0, tiled=True)
    product = jnp.einsum("zbps,pzqk->bqsk", returned, depth_forward, precision=highest)
    applied = (weights * (kinetic * masked_values + product)).astype(jnp.bfloat16)
    paired = jnp.stack([masked, applied])
    portion = lax.all_gather(paired, "band", axis=1, tiled=True)
    partial_terms = jnp.stack(
        [inner_products(bands, portion[0]), inner_products(bands, portion[1])]
    )
    summed = lax.psum(partial_terms, "pw")
    correlation = summed[0]
    subspace = summed[1]
    return (applied, correlation, subspace)


def solution(mesh):
    return jax.shard_map(
        per_device,
        mesh=mesh,
        in_specs=(
            P("band", None, "pw", None),
            P("band", None, "pw", None),
            P("pw", None, None),
            P("pw"),
            P("pw", None),
        ),
        out_specs=(P("band", None, "pw", None), P(None, "band", None), P(None, "band", None)),
        check_vma=False,
    )
```

profile of v0, /device:TPU:1, one launch (start us, length us, event | category | flops | bytes accessed | tf_op | source)
XLA Modules:
  0.0 919.3 jit_solution(13066634721573757280)
XLA Ops:
  7.2 0.3 broadcast_multiply_fusion
  7.5 1.4 fusion.85
  8.9 1.2 convolution_bitcast_fusion.3
  10.2 0.5 copy.71
  10.6 1.7 reshape.623
  12.3 18.1 %all-to-all-start = ((f32[64,1,1280]{2,1,0:T(1,128)}), f32[64,1,1280]{2,1,0:T(1,128)S(1)}, u32[]{:S(2)}, u32[]{:S(2)}) async-start(f32[64,1,1280]{2,1,0:T(1,128)} %reshape.623), calls=%async_computation | async-start | bytes 655360 | tf_op jit(solution)/shard_map/all_to_all | solution.py:62
  30.4 0.3 broadcast_multiply_fusion.2
  30.7 0.3 fusion.56
  31.0 1.3 dynamic-slice
  32.9 0.3 dynamic-update-slice
  33.2 209.9 %all-reduce = s32[2560]{0:T(1024)S(1)} all-reduce(s32[2560]{0:T(1024)S(1)} %dynamic-update-slice), channel_id=1, replica_groups=mesh['band'=8,'pw'=64] {'pw'}, use_global_device_ids=true, to_apply=%add | all-reduce | flops 2560 | bytes 20480
  243.1 0.6 pad_clamp_fusion
  244.0 0.3 fusion.58
  244.2 0.3 fusion.61
  245.1 0.5 broadcast.940
  245.6 1.3 reduce
  246.9 0.8 reshape.624
  247.7 0.6 copy.72
  248.3 0.5 reshape.589
  248.9 4.9 copy.73
  253.7 6.0 broadcast_in_dim.4
  259.8 247.3 %scatter_fusion = f32[2,8,2,8192]{1,2,3,0:T(2,128)} fusion(f32[2,8,2,8192]{1,2,3,0:T(2,128)} %broadcast_in_dim.4, s32[2560]{0:T(1024)S(1)} %copy-done.4, f32[2560,2,8,2]{2,3,1,0:T(2,128)} %copy.73), kind=kCustom, calls=%fused_computation.1 | custom fusion | bytes 993280 | tf_op jit(solution)/shard_map/scatter | solution.py:65
  507.1 13.2 %copy.75 = f32[2,8,2,64,128]{4,3,2,1,0:T(8,128)S(1)} copy(f32[2,8,2,64,128]{1,2,4,3,0:T(2,128)} %bitcast.164) | data formatting | bytes 2097152 | tf_op jit(solution)/shard_map/reshape | solution.py:65
  520.3 1.0 convolution_bitcast_fusion.1
  521.3 1.9 fusion.4
  523.2 1.2 fusion.7
  524.4 1.0 convolution_bitcast_fusion
  525.4 11.2 %copy.114 = f32[2,8,2,64,128]{1,2,4,3,0:T(2,128)} copy(f32[2,8,2,64,128]{4,3,1,0,2:T(8,128)S(1)} %convolution_bitcast_fusion) | data formatting | bytes 2097152 | tf_op jit(solution)/shard_map/reshape | solution.py:71
  536.6 18.0 %gather_fusion = f32[2560,2,8,2]{2,3,1,0:T(2,128)} fusion(f32[2,8,2,8192]{1,2,3,0:T(2,128)} %bitcast.166, s32[3072]{0:T(1024)S(1)} %copy-done.6), kind=kCustom, calls=%fused_computation | custom fusion | bytes 665600 | tf_op jit(solution)/shard_map/gather | solution.py:71
  554.6 7.3 bitcast_bitcast_fusion
  561.9 9.4 %reshape.625 = f32[64,1,1280]{2,1,0:T(1,128)} reshape(f32[2560,2,2,8]{3,2,1,0:T(2,128)} %bitcast_bitcast_fusion) | data formatting | bytes 655360
  571.3 19.6 %all-to-all-start.1 = ((f32[64,1,1280]{2,1,0:T(1,128)}), f32[64,1,1280]{2,1,0:T(1,128)S(1)}, u32[]{:S(2)}, u32[]{:S(2)}) async-start(f32[64,1,1280]{2,1,0:T(1,128)} %reshape.625), calls=%async_computation.1 | async-start | bytes 655360 | tf_op jit(solution)/shard_map/all_to_all | solution.py:72
  590.9 0.3 multiply_multiply_fusion
  591.3 24.5 %all-to-all-done.1 = f32[64,1,1280]{2,1,0:T(1,128)S(1)} async-done(((f32[64,1,1280]{2,1,0:T(1,128)}), f32[64,1,1280]{2,1,0:T(1,128)S(1)}, u32[]{:S(2)}, u32[]{:S(2)}) %all-to-all-start.1) | async-done | bytes 327712 | tf_op jit(solution)/shard_map/all_to_all | solution.py:72
  615.9 1.3 reduce.1
  617.2 9.7 %reshape.626 = f32[2560,2,2,8]{3,2,1,0:T(2,128)} reshape(f32[64,1280]{1,0:T(8,128)S(1)} %reduce.1) | data formatting | bytes 655360
  627.0 5.6 copy.116
  632.6 0.5 copy.83
  633.0 0.4 fusion.12
  633.5 0.8 pad_maximum_fusion
  634.3 0.7 copy.90
  635.0 64.5 %all-gather.2.cloned.1.call-done = bf16[2,64,2,40,128]{4,3,1,2,0:T(8,128)(2,1)} async-done(((bf16[2,8,2,40,128]{4,3,1,2,0:T(8,128)(2,1)}), bf16[2,64,2,40,128]{4,3,1,2,0:T(8,128)(2,1)}) %all-gather.2.cloned.1.call-update) | async-done | bytes 2621456 | tf_op jit(solution)/shard_map/all_gather | solution.py:76
  699.5 2.2 slice_bitcast_fusion.1
  701.8 0.3 maximum_maximum_fusion
  702.1 1.0 fusion.13
  703.6 1.0 fusion.16
  704.7 207.1 %psum.7 = f32[2,2,32,64]{3,2,1,0:T(8,128)S(1)} all-reduce(f32[2,2,32,64]{3,2,1,0:T(8,128)S(1)} %pad_maximum_fusion.5), channel_id=1, replica_groups=mesh['band'=8,'pw'=64] {'pw'}, use_global_device_ids=true, to_apply=%region_1.2 | all-reduce | flops 8192 | bytes 65536 | tf_op jit(solution)/shard_map/psum | solution.py:80
  911.8 0.6 slice_bitcast_fusion.2
  (45 shorter events, 1.8 us)
Async XLA Ops:
  7.2 694.9 %copy-start = (bf16[32,2,40,128]{3,2,1,0:T(8,128)(2,1)S(1)}, bf16[32,2,40,128]{3,2,1,0:T(8,128)(2,1)}, u32[]{:S(2)}) copy-start(bf16[32,2,40,128]{3,2,1,0:T(8,128)(2,1)} %param.6) | copy-start | bytes 1966084
  7.2 25.7 %copy-start.7 = (s32[40]{0:T(128)S(1)}, s32[40]{0:T(128)}, u32[]{:S(2)}) copy-start(s32[40]{0:T(128)} %param.8) | copy-start | bytes 484
  12.3 232.7 %all-to-all-start = ((f32[64,1,1280]{2,1,0:T(1,128)}), f32[64,1,1280]{2,1,0:T(1,128)S(1)}, u32[]{:S(2)}, u32[]{:S(2)}) async-start(f32[64,1,1280]{2,1,0:T(1,128)} %reshape.623), calls=%async_computation | async-start | bytes 655360 | tf_op jit(solution)/shard_map/all_to_all | solution.py:62
  243.1 1.1 copy-start.3
  253.7 6.0 copy-start.4
  507.1 14.2 %copy-start.2 = (f32[2,128,128]{2,1,0:T(8,128)S(1)}, f32[2,128,128]{2,1,0:T(8,128)}, u32[]{:S(2)}) copy-start(f32[2,128,128]{2,1,0:T(8,128)} %param.7) | copy-start | bytes 393220
  525.4 11.2 %copy-start.6 = (s32[3072]{0:T(1024)S(1)}, s32[3072]{0:T(1024)}, u32[]{:S(2)}) copy-start(s32[3072]{0:T(1024)} %pad_clamp_fusion) | copy-start | bytes 36868
  561.9 29.4 %copy-start.1 = (bf16[8,2,40,128]{3,2,1,0:T(8,128)(2,1)S(1)}, bf16[8,2,40,128]{3,2,1,0:T(8,128)(2,1)}, u32[]{:S(2)}) copy-start(bf16[8,2,40,128]{3,2,1,0:T(8,128)(2,1)} %param.5) | copy-start | bytes 491524
  571.3 44.6 %all-to-all-start.1 = ((f32[64,1,1280]{2,1,0:T(1,128)}), f32[64,1,1280]{2,1,0:T(1,128)S(1)}, u32[]{:S(2)}, u32[]{:S(2)}) async-start(f32[64,1,1280]{2,1,0:T(1,128)} %reshape.625), calls=%async_computation.1 | async-start | bytes 655360 | tf_op jit(solution)/shard_map/all_to_all | solution.py:72
  590.8 108.6 %all-gather.2.cloned.1.call-start = ((), (), s32[]{:S(2)}) async-start(), calls=%async_computation.2 | async-start | bytes 2949120 | tf_op jit(solution)/shard_map/all_gather | solution.py:76
  627.0 6.1 copy-start.5
Sparse Core Ops, SparseCore 0:
  634.4 65.0 all-gather.1
where the time goes:
time: 934 us; the launch traced here: 919 us
  blocking collectives  417 us (45%)
  local copies, waits for them, and re-layouts  343 us (37%)
  waiting for transfers between devices  89.1 us (10%)
  starting transfers between devices  37.7 us (4%)
  between operations  15.1 us (2%)
    scatter x1, local copies, waits for them, and re-layouts, per_device(): grid.at[:, :, :, place].set(portion)  247 us
    unnamed x1, blocking collectives  210 us
    psum x1, blocking collectives, per_device(): summed = lax.psum(partial_terms, 'pw')  207 us
    all_gather x1, waiting for transfers between devices, per_device(): portion = lax.all_gather(paired, 'band', axis=1, tiled=True)  64.5 us
    unnamed x25, local copies, waits for them, and re-layouts  31.2 us
    all_to_all x1, waiting for transfers between devices, per_device(): lax.all_to_all(picked, 'pw', split_axis=3, concat_axis=0, tiled=True)  24.5 us
    all_to_all x1, starting transfers between devices, per_device(): lax.all_to_all(picked, 'pw', split_axis=3, concat_axis=0, tiled=True)  19.6 us
  transfers between devices with their start and end apart: 3, of which 2 were waited for; matrix products, arithmetic and copies ran while one was open for 1% of the time, Pallas kernels for 0%

commit v1 on v0

v1 whole, which is shorter than its diff:
```python
import jax
import jax.numpy as jnp
import ml_dtypes
import numpy as np
from jax import lax
from jax.experimental import pallas as pl
from jax.experimental.pallas import tpu as pltpu
from jax.sharding import PartitionSpec as P

NG = 128
RAD = 32
WIN = 64
GROUP = 4
RING = 16
BANDS = 2
STICKS = 160
ROWS = 48
ALL = STICKS * RING
F32 = jnp.float32
BF16 = jnp.bfloat16


def split_table(table):
    high = table.astype(ml_dtypes.bfloat16)
    low = (table - high.astype(np.float64)).astype(ml_dtypes.bfloat16)
    return high, low


def angle(first, second):
    return 2.0 * np.pi / NG * np.mod(np.outer(first, second), NG)


def depth_tables():
    k = np.arange(NG)
    theta = angle(np.arange(NG), k)
    inverse = np.zeros((RING, 2, 8, 2 * NG))
    theta = theta.reshape(RING, 8, NG)
    inverse[:, 0] = np.concatenate([np.cos(theta), -np.sin(theta)], axis=-1)
    inverse[:, 1] = np.concatenate([np.sin(theta), np.cos(theta)], axis=-1)
    forward = np.zeros((RING, 2, 8, 2 * NG))
    forward[:, 0] = np.concatenate([np.cos(theta), -np.sin(theta)], axis=-1)
    forward[:, 1] = np.concatenate([np.sin(theta), np.cos(theta)], axis=-1)
    return split_table(inverse.reshape(2 * NG, 2 * NG)), split_table(forward.reshape(2 * NG, 2 * NG))


def across_tables():
    y = np.arange(NG)
    j = np.arange(WIN)
    theta = angle(j, y)
    lower = np.sin(theta)
    lower[0] = np.where(y % 2 == 0, 1.0, -1.0)
    high, low = split_table(np.concatenate([np.cos(theta), lower], axis=0))
    stacked = np.concatenate([high, high, low, low], axis=0)
    wide = np.concatenate([high.T, low.T], axis=1)
    return stacked, wide


def down_tables():
    freq = np.arange(WIN) - RAD
    theta = angle(np.arange(NG), freq)
    cosine, sine = np.cos(theta) / NG**3, np.sin(theta) / NG**3
    inverse = np.block([[cosine, -sine], [sine, cosine]])
    cosine, sine = np.cos(theta).T, np.sin(theta).T
    forward = np.block([[cosine, sine], [-sine, cosine]])
    return split_table(inverse), split_table(forward)


def lane_order():
    order = np.concatenate([np.arange(WIN), [WIN], np.arange(NG - 1, WIN, -1)])
    matrix = np.zeros((NG, NG))
    matrix[order, np.arange(NG)] = 1.0
    return matrix.astype(ml_dtypes.bfloat16)


def split(value):
    high = value.astype(BF16)
    low = (value - high.astype(F32)).astype(BF16)
    return high, low


def dot(left, right, dims=((1,), (0,))):
    return lax.dot_general(left, right, (dims, ((), ())), preferred_element_type=F32)


def spread_kernel(part_ref, high_ref, low_ref, out_ref):
    for band in range(BANDS):
        real = part_ref[:, 2 * band].reshape(STICKS, NG)
        imag = part_ref[:, 2 * band + 1].reshape(STICKS, NG)
        both = jnp.concatenate([real, imag], axis=1)
        field = dot(high_ref[...], both, ((1,), (1,))) + dot(low_ref[...], both, ((1,), (1,)))
        out_ref[:, 16 * band : 16 * band + 16, :] = field[:, :NG].reshape(RING, 16, NG)
        rest = field[:, NG:].reshape(RING, 2, 8, STICKS - NG)
        for part in range(2):
            g = 2 * band + part
            out_ref[:, 32:40, 32 * g : 32 * g + 32] = rest[:, part]
    cells = part_ref[:, 2 * BANDS].reshape(STICKS, NG)
    lane = lax.broadcasted_iota(jnp.int32, (8, NG), 1)
    row = lax.broadcasted_iota(jnp.int32, (8, NG), 0)
    pick = jnp.where(row < 1, jnp.where(lane == 0, 128.0, jnp.where(lane == 1, 1.0, 0.0)), 0.0)
    flat = dot(pick.astype(BF16), cells, ((1,), (1,)))
    tail = jnp.concatenate([flat[0:1, NG:], jnp.zeros((1, 2 * NG - STICKS), F32)], axis=1)
    index = lax.broadcasted_iota(jnp.int32, (8, NG), 0)
    block = jnp.where(index == 0, flat[0:1, :NG], jnp.where(index == 1, tail, 0.0))
    out_ref[:, 40:48, :] = jnp.broadcast_to(block[None], (RING, 8, NG))


def plane_kernel(
    recv_ref, v_ref, stack_ref, wide_ref, xa_ref, xh_ref, fh_ref, fl_ref, order_ref,
    out_ref, val_ref, low_ref, cell_ref, onehot_ref, tall_ref, flat_ref, left_ref, mid_ref, lift_ref,
):
    for src in range(RING):
        val_ref[:, src * NG : (src + 1) * NG] = recv_ref[src, 0:32, :]
        cell_ref[:, src * NG : (src + 1) * NG] = jnp.broadcast_to(recv_ref[src, 40:41, :], (8, NG))
        start = RING * NG + 32 * src
        for g in range(4):
            val_ref[8 * g : 8 * g + 8, start : start + 32] = recv_ref[src, 32:40, 32 * g : 32 * g + 32]
        cell_ref[:, start : start + 32] = jnp.broadcast_to(recv_ref[src, 41:42, 0:32], (8, 32))

    cells = cell_ref[...].astype(jnp.int32)
    x_index = jnp.bitwise_and(lax.shift_right_logical(cells, 7) + RAD, NG - 1)
    y_index = jnp.bitwise_and(cells, NG - 1)
    x_row, y_row = x_index[0:1], y_index[0:1]
    onehot_ref[...] = jnp.where(
        lax.broadcasted_iota(jnp.int32, (WIN, ALL), 0) == x_row, 1.0, 0.0
    ).astype(BF16)
    pick_y = jnp.where(lax.broadcasted_iota(jnp.int32, (NG, ALL), 0) == y_row, 1.0, 0.0).astype(BF16)
    flat_ref[...] = dot(stack_ref[...], pick_y).astype(BF16)
    tall_ref[...] = dot(pick_y, wide_ref[...], ((0,), (0,))).astype(BF16)

    rounded = val_ref[...].astype(BF16).astype(F32)
    low_ref[...] = val_ref[...] - rounded
    val_ref[...] = rounded

    lane = lax.broadcasted_iota(jnp.int32, (WIN, NG), 1)
    first = jnp.bitwise_and(lane, WIN - 1) == 0
    lower = lane < WIN

    @pl.loop(0, 8)
    def _(z):
        for g in range(4):
            for part, ref in enumerate((val_ref, low_ref)):
                row = ref[pl.ds(8 * g + z, 1), :]
                spread = jnp.broadcast_to(row, (WIN, ALL)).astype(BF16)
                at = (2 * g + part) * WIN
                left_ref[at : at + WIN, :] = spread * onehot_ref[...]
        full = dot(left_ref[...], tall_ref[...])
        full = full[:, :NG] + full[:, NG:]
        parts = [full[2 * g * WIN : (2 * g + 1) * WIN] + full[(2 * g + 1) * WIN : (2 * g + 2) * WIN] for g in range(4)]
        for band in range(BANDS):
            real, imag = parts[2 * band], parts[2 * band + 1]
            real_turn, imag_turn = pltpu.roll(real, WIN, 1), pltpu.roll(imag, WIN, 1)
            new_real = jnp.where(first, real, jnp.where(lower, real - imag_turn, real_turn + imag))
            new_imag = jnp.where(first, imag, jnp.where(lower, imag + real_turn, imag_turn - real))
            mid_ref[z, 0:WIN, band * NG : (band + 1) * NG] = new_real
            mid_ref[z, WIN:, band * NG : (band + 1) * NG] = new_imag

    for owner in range(GROUP):
        for i in range(2):
            z = 2 * owner + i
            potential = dot(v_ref[owner, 0, i], order_ref[...]) + dot(v_ref[owner, 1, i], order_ref[...])
            high, low = split(mid_ref[z])
            field = dot(xa_ref[...], jnp.concatenate([high, high], axis=0)) + dot(xh_ref[...], low)
            wide = jnp.concatenate([potential, potential], axis=1)
            weighted = field * jnp.concatenate([wide, wide], axis=0)
            high, low = split(weighted)
            folded = dot(fh_ref[...], high) + dot(fh_ref[...], low) + dot(fl_ref[...], high)
            for band in range(BANDS):
                real = folded[:WIN, band * NG : (band + 1) * NG]
                imag = folded[WIN:, band * NG : (band + 1) * NG]
                real_turn, imag_turn = pltpu.roll(real, WIN, 1), pltpu.roll(imag, WIN, 1)
                left_real = jnp.where(first, real, jnp.where(lower, real + real_turn, imag_turn - imag))
                left_imag = jnp.where(first, imag, jnp.where(lower, imag + imag_turn, real - real_turn))
                for part, value in enumerate((left_real, left_imag)):
                    high, low = split(value)
                    lift_ref[2 * band + part, z, :, 0:NG] = high
                    lift_ref[2 * band + part, z, :, NG:] = low

    @pl.loop(0, ALL // 256)
    def _(t):
        cols = pl.ds(pl.multiple_of(t * 256, 256), 256)
        select = onehot_ref[:, cols].astype(F32)[None]
        for g in range(4):
            rows = lift_ref[g].reshape(8 * WIN, 2 * NG)
            full = dot(rows, flat_ref[0:256, cols]) + dot(rows, flat_ref[256:512, cols])
            val_ref[8 * g : 8 * g + 8, cols] = jnp.sum(full.reshape(8, WIN, 256) * select, axis=1)

    for src in range(RING):
        out_ref[src, 0:32, :] = val_ref[:, src * NG : (src + 1) * NG]
        start = RING * NG + 32 * src
        for g in range(4):
            out_ref[src, 32:40, 32 * g : 32 * g + 32] = val_ref[8 * g : 8 * g + 8, start : start + 32]
        out_ref[src, 40:48, :] = jnp.zeros((8, NG), F32)


def finish_kernel(recv_ref, part_ref, high_ref, low_ref, out_ref, copies_ref, line_ref, pack_ref):
    squares = part_ref[:, 2 * BANDS].reshape(STICKS, NG).astype(F32)
    signed = jnp.where(squares < NG // 2, squares, squares - NG)
    across = signed * signed
    across = across[:, 0:1] + across[:, 1:2]
    k = lax.broadcasted_iota(jnp.int32, (STICKS, NG), 1)
    k = jnp.where(k < NG // 2, k, k - NG)
    total = across + (k * k).astype(F32)
    weight = jnp.where(total <= RAD * RAD, 1.0, 0.0)
    kinetic = 2.0 / (RAD * RAD) * total
    for band in range(BANDS):
        line_ref[:, 0:NG] = recv_ref[:, 16 * band : 16 * band + 16, :].reshape(2 * NG, NG)
        for src in range(RING):
            for part in range(2):
                g = 2 * band + part
                at = 16 * src + 8 * part
                line_ref[at : at + 8, NG : NG + 32] = recv_ref[src, 32:40, 32 * g : 32 * g + 32]
        high, low = split(jnp.transpose(line_ref[...])[:STICKS])
        product = dot(high, high_ref[...]) + dot(low, high_ref[...]) + dot(high, low_ref[...])
        for part in range(2):
            masked = part_ref[:, 2 * band + part].reshape(STICKS, NG).astype(F32)
            value = weight * (kinetic * masked + product[:, part * NG : (part + 1) * NG])
            value = value.reshape(GROUP, STICKS // GROUP, NG)
            out_ref[:, 2 * band + part] = value.astype(BF16)
            half = STICKS // GROUP // 2
            for src in range(GROUP):
                at = ((2 * band + part) * GROUP + src) * half
                turned = pltpu.roll(value[src, half:], NG // 2, 1)
                pack_ref[at : at + half, :] = value[src, :half] + turned
    packed = pack_ref[...].astype(BF16)
    for copy in range(copies_ref.shape[0]):
        copies_ref[copy] = packed


def vmem_call(kernel, out_shape, inputs, scratch=()):
    vmem = pl.BlockSpec(memory_space=pltpu.VMEM)
    return pl.pallas_call(
        kernel,
        out_shape=out_shape,
        in_specs=[vmem] * len(inputs),
        out_specs=jax.tree.map(lambda _: vmem, out_shape),
        scratch_shapes=list(scratch),
        compiler_params=pltpu.CompilerParams(vmem_limit_bytes=56 * 1024 * 1024),
    )(*inputs)


def spread(part):
    (high, low), _ = depth_tables()
    shape = jax.ShapeDtypeStruct((RING, ROWS, NG), F32)
    return vmem_call(spread_kernel, shape, (part, high, low))


def planes(recv, potentials):
    stack, wide = across_tables()
    (xh, xl), (fh, fl) = down_tables()
    xa = np.concatenate([xh, xl], axis=1)
    shape = jax.ShapeDtypeStruct((RING, ROWS, NG), F32)
    scratch = (
        pltpu.VMEM((32, ALL), F32),
        pltpu.VMEM((32, ALL), F32),
        pltpu.VMEM((8, ALL), F32),
        pltpu.VMEM((WIN, ALL), BF16),
        pltpu.VMEM((ALL, 2 * NG), BF16),
        pltpu.VMEM((4 * NG, ALL), BF16),
        pltpu.VMEM((8 * WIN, ALL), BF16),
        pltpu.VMEM((8, 2 * WIN, 2 * NG), F32),
        pltpu.VMEM((4, 8, WIN, 2 * NG), BF16),
    )
    inputs = (recv, potentials, stack, wide, xa, xh, fh, fl, lane_order())
    return vmem_call(plane_kernel, shape, inputs, scratch)


def finish(recv, part, copies):
    _, (high, low) = depth_tables()
    rows = BANDS * STICKS
    shape = (
        jax.ShapeDtypeStruct((GROUP, 2 * BANDS, STICKS // GROUP, NG), BF16),
        jax.ShapeDtypeStruct((copies, rows, NG), BF16),
    )
    scratch = (pltpu.VMEM((2 * NG, 2 * NG), F32), pltpu.VMEM((rows, NG), F32))
    return vmem_call(finish_kernel, shape, (recv, part, high, low), scratch)


def pack(value):
    half = value.shape[2] // 2
    return value[:, :, :half] + jnp.roll(value[:, :, half:], NG // 2, axis=3)


def pairing(bands, vectors):
    full = lax.dot_general(
        bands, vectors, (((0, 3, 4), (3, 4, 5)), ((), ())), preferred_element_type=F32
    )
    real = full[:, 0, :, :, 0] + full[:, 1, :, :, 1]
    imag = full[:, 0, :, :, 1] - full[:, 1, :, :, 0]
    return jnp.stack([real, imag])


def exchange(value, axis, groups=None):
    return lax.all_to_all(value, axis, 0, 0, axis_index_groups=groups, tiled=True)


def to_all(value, axis, count, groups=None):
    return exchange(jnp.broadcast_to(value[None], (count, *value.shape)), axis, groups)


def per_device(block, bands, potential, stick_cells, sphere_mask):
    size = lax.axis_size("pw")
    teams = lax.axis_size("band")
    own, sticks, rows = block.shape[0], block.shape[2], bands.shape[0]
    fours = [[i * GROUP + j for j in range(GROUP)] for i in range(size // GROUP)]
    rings = [[i * GROUP + j for i in range(size // GROUP)] for j in range(GROUP)]

    inside = sphere_mask.astype(BF16)[None, None]
    masked = block * inside
    lane = jnp.arange(NG, dtype=jnp.int32)[None, :]
    column = jnp.where(lane == 0, stick_cells[:, None] // NG, jnp.where(lane == 1, stick_cells[:, None] % NG, 0))
    grouped = masked.reshape(GROUP, 2 * BANDS, sticks, NG)
    column = jnp.broadcast_to(column.astype(BF16)[None, None], (GROUP, 1, sticks, NG))
    part = exchange(jnp.concatenate([grouped, column], axis=1), "pw", fours)
    sent = spread(part)
    recv = exchange(sent, "pw", rings)

    bands_rows = pack(bands * inside).reshape(-1, NG)
    v_high = lax.reduce_precision(potential, 8, 7)
    v_low = (potential - v_high).astype(BF16)
    potential_rows = jnp.stack([v_high.astype(BF16), v_low]).reshape(-1, NG)
    side = to_all(jnp.concatenate([bands_rows, potential_rows], axis=0), "pw", GROUP, fours)
    split_at = bands_rows.shape[0]
    bands_all = side[:, :split_at].reshape(GROUP, rows, 2, sticks // 2, NG)
    potentials = side[:, split_at:].reshape(GROUP, 2, potential.shape[0], NG, NG)
    shape = (teams, BANDS, 2, GROUP, sticks // 2, NG)
    packed = jnp.transpose(pack(part[:, : 2 * BANDS]), (1, 0, 2, 3)).reshape(-1, NG)
    masked_all = to_all(packed, "band", teams).reshape(shape)

    back = exchange(planes(recv, potentials), "pw", rings)
    result, copies = finish(back, part, teams)
    applied_all = exchange(copies, "band").reshape(shape)
    applied = exchange(result, "pw", fours).reshape(own, 2, sticks, NG)

    terms = jnp.stack([pairing(bands_all, masked_all), pairing(bands_all, applied_all)])
    total = jnp.sum(to_all(terms.reshape(-1, NG), "pw", size // GROUP, rings), axis=0)
    total = to_all(total, "pw", GROUP, fours).reshape(GROUP, 2, 2, rows, teams, BANDS)
    total = jnp.transpose(total, (1, 2, 3, 4, 0, 5)).reshape(2, 2, rows, teams * own)
    return (applied, total[0], total[1])


def solution(mesh):
    return jax.shard_map(
        per_device,
        mesh=mesh,
        in_specs=(
            P("band", None, "pw", None),
            P("band", None, "pw", None),
            P("pw", None, None),
            P("pw"),
            P("pw", None),
        ),
        out_specs=(P("band", None, "pw", None), P(None, "band", None), P(None, "band", None)),
        check_vma=False,
    )
```

time: 934 us -> 204 us (0.22); the launches traced: 919 us -> 203 us
  blocking collectives: 417 us -> 26.7 us
  local copies, waits for them, and re-layouts: 343 us -> 17.4 us
  Pallas kernels: 0 us -> 26 us
  waiting for transfers between devices: 89.1 us -> 66.5 us
  starting transfers between devices: 37.7 us -> 59.5 us
  between operations: 15.1 us -> 0.88 us
    scatter x1 -> x0, local copies, waits for them, and re-layouts: 247 us -> none  [per_device(): grid.at[:, :, :, place].set(portion)]
    unnamed x1 -> x0, blocking collectives: 210 us -> none
    psum x1 -> x0, blocking collectives: 207 us -> none  [per_device(): summed = lax.psum(partial_terms, 'pw')]
    all_gather x1 -> x0, waiting for transfers between devices: 64.5 us -> none  [per_device(): portion = lax.all_gather(paired, 'band', axis=1, tiled=True)]
    all_to_all x2 -> x8, waiting for transfers between devices: 24.6 us -> 66.5 us  [exchange(): lax.all_to_all(value, axis, 0, 0, axis_index_groups=groups, tiled=True)]
    unnamed x25 -> x17, local copies, waits for them, and re-layouts: 31.2 us -> 3.33 us
    all_to_all x0 -> x1, blocking collectives: none -> 26.7 us  [exchange(): lax.all_to_all(value, axis, 0, 0, axis_index_groups=groups, tiled=True)]
    pallas_call x0 -> x3, Pallas kernels: none -> 26 us  [vmem_call(): pl.pallas_call(kernel, out_shape=out_shape, in_specs=[vmem] * len(inputs)...]
  transfers between devices with their start and end apart: 3 -> 8, of which waited for: 2 -> 7; matrix products, arithmetic and copies ran while one was open for 1% -> 5% of each run, Pallas kernels for 0% -> 12%
where the time goes in v1:
time: 204 us; the launch traced here: 203 us
  waiting for transfers between devices  66.5 us (33%)
  starting transfers between devices  59.5 us (29%)
  blocking collectives  26.7 us (13%)
  Pallas kernels  26 us (13%)
  local copies, waits for them, and re-layouts  17.4 us (9%)
  other arithmetic  3.76 us (2%)
  matrix products  2.28 us (1%)
    all_to_all x8, waiting for transfers between devices, exchange(): lax.all_to_all(value, axis, 0, 0, axis_index_groups=groups, tiled=True)  66.5 us
    all_to_all x8, starting transfers between devices, exchange(): lax.all_to_all(value, axis, 0, 0, axis_index_groups=groups, tiled=True)  59.5 us
    all_to_all x1, blocking collectives, exchange(): lax.all_to_all(value, axis, 0, 0, axis_index_groups=groups, tiled=True)  26.7 us
    pallas_call x3, Pallas kernels, vmem_call(): pl.pallas_call(kernel, out_shape=out_shape, in_specs=[vmem] * len(inputs)...  26 us
    slice x2, local copies, waits for them, and re-layouts, per_device(): bands_all = side[:, :split_at].reshape(GROUP, rows, 2, sticks // 2, NG)  6.2 us
  transfers between devices with their start and end apart: 8, of which 7 were waited for; matrix products, arithmetic and copies ran while one was open for 5% of the time, Pallas kernels for 12%

profile of v1, /device:TPU:1, one launch (start us, length us, event | category | flops | bytes accessed | tf_op | source)
XLA Modules:
  0.0 202.9 jit_solution(10239506515332325608)
XLA Ops:
  0.7 0.8 convert_element_type.16
  1.4 0.7 and_select_fusion.1
  2.1 0.9 broadcast_multiply_fusion.1
  3.1 0.7 pad_maximum_fusion.1
  3.9 10.2 %all-to-all-start = ((bf16[4,5,40,128]{3,2,1,0:T(8,128)(2,1)}), bf16[4,5,40,128]{3,2,1,0:T(8,128)(2,1)S(1)}, u32[]{:S(2)}, u32[]{:S(2)}) async-start(bf16[4,5,40,128]{3,2,1,0:T(8,128)(2,1)} %pad_maximum_fusion.1), calls=%async_computation | async-start | bytes 409600 | tf_op jit(solution)/shard_map/all_to_all | solution.py:293
  14.1 0.3 fusion.21
  14.4 0.3 slice_add_fusion
  14.8 0.5 copy-done.6
  15.4 3.2 %all-to-all-done.part_ref = bf16[4,5,40,128]{3,2,1,0:T(8,128)(2,1)S(1)} async-done(((bf16[4,5,40,128]{3,2,1,0:T(8,128)(2,1)}), bf16[4,5,40,128]{3,2,1,0:T(8,128)(2,1)S(1)}, u32[]{:S(2)}, u32[]{:S(2)}) %all-to-all-start) | async-done | bytes 204832 | tf_op jit(solution)/shard_map/all_to_all | solution.py:293
  18.6 1.5 broadcast_in_dim.78
  20.1 4.4 %all-to-all-start.2 = ((bf16[4,1792,128]{2,1,0:T(8,128)(2,1)}), bf16[4,1792,128]{2,1,0:T(8,128)(2,1)S(1)}, u32[]{:S(2)}, u32[]{:S(2)}) async-start(bf16[4,1792,128]{2,1,0:T(8,128)(2,1)} %broadcast_in_dim.78), calls=%async_computation.2 | async-start | bytes 3670016 | tf_op jit(solution)/shard_map/all_to_all | solution.py:293
  24.5 2.2 %shard_map.175 = f32[16,48,128]{2,1,0:T(8,128)} custom-call(bf16[4,5,40,128]{3,2,1,0:T(8,128)(2,1)} %copy-done, bf16[256,256]{1,0:T(8,128)(2,1)} %constant.51.clone.high_ref, bf16[256,256]{1,0:T(8,128)(2,1)} %constant.52.clone.low_ref), custom_call_target="tpu_custom_call" | custom-call | tf_op jit(solution)/shard_map/pallas_call | solution.py:231
  26.8 19.8 %all-to-all-done.2 = bf16[4,1792,128]{2,1,0:T(8,128)(2,1)S(1)} async-done(((bf16[4,1792,128]{2,1,0:T(8,128)(2,1)}), bf16[4,1792,128]{2,1,0:T(8,128)(2,1)S(1)}, u32[]{:S(2)}, u32[]{:S(2)}) %all-to-all-start.2) | async-done | bytes 1835040 | tf_op jit(solution)/shard_map/all_to_all | solution.py:293
  46.6 9.5 %all-to-all-start.1 = ((f32[16,48,128]{2,1,0:T(8,128)}), f32[16,48,128]{2,1,0:T(8,128)S(1)}, u32[]{:S(2)}, u32[]{:S(2)}) async-start(f32[16,48,128]{2,1,0:T(8,128)} %shard_map.175), calls=%async_computation.1 | async-start | bytes 786432 | tf_op jit(solution)/shard_map/all_to_all | solution.py:293
  56.1 0.1 fusion.22
  56.2 0.1 fusion.12
  56.4 17.8 %all-to-all-done.1.recv_ref = f32[16,48,128]{2,1,0:T(8,128)S(1)} async-done(((f32[16,48,128]{2,1,0:T(8,128)}), f32[16,48,128]{2,1,0:T(8,128)S(1)}, u32[]{:S(2)}, u32[]{:S(2)}) %all-to-all-start.1) | async-done | bytes 393248 | tf_op jit(solution)/shard_map/all_to_all | solution.py:293
  74.2 1.0 broadcast_in_dim.80
  75.2 6.7 %all-to-all-start.5 = ((bf16[8,320,128]{2,1,0:T(8,128)(2,1)}), bf16[8,320,128]{2,1,0:T(8,128)(2,1)S(1)}, u32[]{:S(2)}, u32[]{:S(2)}) async-start(bf16[8,320,128]{2,1,0:T(8,128)(2,1)} %broadcast_in_dim.80), calls=%async_computation.5 | async-start | bytes 1310720 | tf_op jit(solution)/shard_map/all_to_all | solution.py:293
  81.8 0.8 slice.90
  82.7 21.2 %shard_map.176 = f32[16,48,128]{2,1,0:T(8,128)} custom-call(f32[16,48,128]{2,1,0:T(8,128)} %copy-done.2, bf16[4,2,2,128,128]{4,3,2,1,0:T(8,128)(2,1)} %bitcast.61, bf16[512,128]{1,0:T(8,128)(2,1)} %constant.53.clone.stack_ref, bf16[128,256]{1,0:T(8,128)(2,1)} %constant.54.clone.wide_ref, bf16[256,256]{1,0:T(8,128)(2,1)} %constant.55.clone.xa_ref, ...), custom_call_target="tpu_custom_call" | custom-call | tf_op jit(solution)/shard_map/pallas_call | solution.py:231
  103.8 11.5 %all-to-all-start.3 = ((f32[16,48,128]{2,1,0:T(8,128)}), f32[16,48,128]{2,1,0:T(8,128)S(1)}, u32[]{:S(2)}, u32[]{:S(2)}) async-start(f32[16,48,128]{2,1,0:T(8,128)} %shard_map.176), calls=%async_computation.3 | async-start | bytes 786432 | tf_op jit(solution)/shard_map/all_to_all | solution.py:293
  115.3 1.3 copy.62
  116.6 0.1 slice.91
  116.7 6.1 %copy.60 = bf16[4,1280,128]{2,0,1:T(4,128)(2,1)S(1)} copy(bf16[4,1280,128]{2,1,0:T(8,128)(2,1)S(1)} %slice.91) | data formatting | bytes 2621440 | tf_op jit(solution)/shard_map/slice | solution.py:323
  122.8 10.1 %all-to-all-done.3.recv_ref = f32[16,48,128]{2,1,0:T(8,128)S(1)} async-done(((f32[16,48,128]{2,1,0:T(8,128)}), f32[16,48,128]{2,1,0:T(8,128)S(1)}, u32[]{:S(2)}, u32[]{:S(2)}) %all-to-all-start.3) | async-done | bytes 393248 | tf_op jit(solution)/shard_map/all_to_all | solution.py:293
  132.9 0.7 copy-done.3
  133.7 2.7 %shard_map.177 = (bf16[4,4,40,128]{3,2,1,0:T(8,128)(2,1)}, bf16[8,320,128]{2,1,0:T(8,128)(2,1)}) custom-call(f32[16,48,128]{2,1,0:T(8,128)} %copy-done.3, bf16[4,5,40,128]{3,2,1,0:T(8,128)(2,1)} %copy-done, bf16[256,256]{1,0:T(8,128)(2,1)} %constant.51.clone.high_ref, bf16[256,256]{1,0:T(8,128)(2,1)} %constant.52.clone.low_ref), custom_call_target="tpu_custom_call" | custom-call | tf_op jit(solution)/shard_map/pallas_call | solution.py:231
  136.4 5.4 %all-to-all-start.6 = ((bf16[8,320,128]{2,1,0:T(8,128)(2,1)}), bf16[8,320,128]{2,1,0:T(8,128)(2,1)S(1)}, u32[]{:S(2)}, u32[]{:S(2)}) async-start(bf16[8,320,128]{2,1,0:T(8,128)(2,1)} %get-tuple-element.6), calls=%async_computation.6 | async-start | bytes 1310720 | tf_op jit(solution)/shard_map/all_to_all | solution.py:293
  141.7 1.1 fusion.4
  142.9 8.6 %all-to-all-done.6 = bf16[8,320,128]{2,1,0:T(8,128)(2,1)S(1)} async-done(((bf16[8,320,128]{2,1,0:T(8,128)(2,1)}), bf16[8,320,128]{2,1,0:T(8,128)(2,1)S(1)}, u32[]{:S(2)}, u32[]{:S(2)}) %all-to-all-start.6) | async-done | bytes 655392 | tf_op jit(solution)/shard_map/all_to_all | solution.py:293
  151.5 0.4 copy.66
  151.9 1.1 fusion.7
  153.1 0.3 copy.72
  153.4 0.3 broadcast_in_dim.81
  153.7 26.7 %all_to_all.45 = f32[16,16,128]{2,1,0:T(8,128)S(1)} all-to-all(f32[16,16,128]{2,1,0:T(8,128)S(1)} %broadcast_in_dim.82), channel_id=1, replica_groups={{0,4,8,12,16,20,24,28,32,36,40,44,48,52,56,60},{1,5,9,13,17,21,25,29,33..., dimensions={0} | all-to-all | bytes 262144 | tf_op jit(solution)/shard_map/all_to_all | solution.py:293
  180.3 7.4 %all-to-all-start.4 = ((bf16[4,4,40,128]{3,2,1,0:T(8,128)(2,1)}), bf16[4,4,40,128]{3,2,1,0:T(8,128)(2,1)S(1)}, u32[]{:S(2)}, u32[]{:S(2)}) async-start(bf16[4,4,40,128]{3,2,1,0:T(8,128)(2,1)} %get-tuple-element.5), calls=%async_computation.4 | async-start | bytes 327680 | tf_op jit(solution)/shard_map/all_to_all | solution.py:293
  187.8 3.8 %all-to-all-done.4 = bf16[4,4,40,128]{3,2,1,0:T(8,128)(2,1)S(1)} async-done(((bf16[4,4,40,128]{3,2,1,0:T(8,128)(2,1)}), bf16[4,4,40,128]{3,2,1,0:T(8,128)(2,1)S(1)}, u32[]{:S(2)}, u32[]{:S(2)}) %all-to-all-start.4) | async-done | bytes 163872 | tf_op jit(solution)/shard_map/all_to_all | solution.py:293
  191.6 0.6 broadcast_in_dim.83
  192.2 4.4 %all-to-all-start.8 = ((f32[4,16,128]{2,1,0:T(8,128)}), f32[4,16,128]{2,1,0:T(8,128)S(1)}, u32[]{:S(2)}, u32[]{:S(2)}) async-start(f32[4,16,128]{2,1,0:T(8,128)} %broadcast_in_dim.83), calls=%async_computation.8 | async-start | bytes 65536 | tf_op jit(solution)/shard_map/all_to_all | solution.py:293
  196.6 3.2 %all-to-all-done.8 = f32[4,16,128]{2,1,0:T(8,128)S(1)} async-done(((f32[4,16,128]{2,1,0:T(8,128)}), f32[4,16,128]{2,1,0:T(8,128)S(1)}, u32[]{:S(2)}, u32[]{:S(2)}) %all-to-all-start.8) | async-done | bytes 32800 | tf_op jit(solution)/shard_map/all_to_all | solution.py:293
  199.8 0.4 copy.73
  200.1 0.1 fusion.20
  200.2 0.3 copy.74
  200.5 0.7 copy.76
  201.2 0.3 copy.75
  201.6 0.7 copy.77
  202.3 0.7 copy.104
  (31 shorter events, 0.4 us)
Async XLA Ops:
  0.6 13.4 %copy-start.4 = (bf16[32,2,40,128]{3,2,1,0:T(8,128)(2,1)S(1)}, bf16[32,2,40,128]{3,2,1,0:T(8,128)(2,1)}, u32[]{:S(2)}) copy-start(bf16[32,2,40,128]{3,2,1,0:T(8,128)(2,1)} %param.17) | copy-start | bytes 1966084
  3.9 14.8 %all-to-all-start = ((bf16[4,5,40,128]{3,2,1,0:T(8,128)(2,1)}), bf16[4,5,40,128]{3,2,1,0:T(8,128)(2,1)S(1)}, u32[]{:S(2)}, u32[]{:S(2)}) async-start(bf16[4,5,40,128]{3,2,1,0:T(8,128)(2,1)} %pad_maximum_fusion.1), calls=%async_computation | async-start | bytes 409600 | tf_op jit(solution)/shard_map/all_to_all | solution.py:293
  14.4 0.9 copy-start.6
  18.6 1.5 copy-start
  20.1 26.4 %all-to-all-start.2 = ((bf16[4,1792,128]{2,1,0:T(8,128)(2,1)}), bf16[4,1792,128]{2,1,0:T(8,128)(2,1)S(1)}, u32[]{:S(2)}, u32[]{:S(2)}) async-start(bf16[4,1792,128]{2,1,0:T(8,128)(2,1)} %broadcast_in_dim.78), calls=%async_computation.2 | async-start | bytes 3670016 | tf_op jit(solution)/shard_map/all_to_all | solution.py:293
  24.5 31.6 %copy-start.1 = (bf16[4,5,40,128]{3,2,1,0:T(8,128)(2,1)S(1)}, bf16[4,5,40,128]{3,2,1,0:T(8,128)(2,1)}, u32[]{:S(2)}) copy-start(bf16[4,5,40,128]{3,2,1,0:T(8,128)(2,1)} %copy-done) | copy-start | bytes 614404
  46.6 27.6 %all-to-all-start.1 = ((f32[16,48,128]{2,1,0:T(8,128)}), f32[16,48,128]{2,1,0:T(8,128)S(1)}, u32[]{:S(2)}, u32[]{:S(2)}) async-start(f32[16,48,128]{2,1,0:T(8,128)} %shard_map.175), calls=%async_computation.1 | async-start | bytes 786432 | tf_op jit(solution)/shard_map/all_to_all | solution.py:293
  74.2 8.5 %copy-start.2 = (f32[16,48,128]{2,1,0:T(8,128)}, f32[16,48,128]{2,1,0:T(8,128)S(1)}, u32[]{:S(2)}) copy-start(f32[16,48,128]{2,1,0:T(8,128)S(1)} %all-to-all-done.1.recv_ref) | copy-start | bytes 1179652
  75.2 28.7 %all-to-all-start.5 = ((bf16[8,320,128]{2,1,0:T(8,128)(2,1)}), bf16[8,320,128]{2,1,0:T(8,128)(2,1)S(1)}, u32[]{:S(2)}, u32[]{:S(2)}) async-start(bf16[8,320,128]{2,1,0:T(8,128)(2,1)} %broadcast_in_dim.80), calls=%async_computation.5 | async-start | bytes 1310720 | tf_op jit(solution)/shard_map/all_to_all | solution.py:293
  103.8 29.1 %all-to-all-start.3 = ((f32[16,48,128]{2,1,0:T(8,128)}), f32[16,48,128]{2,1,0:T(8,128)S(1)}, u32[]{:S(2)}, u32[]{:S(2)}) async-start(f32[16,48,128]{2,1,0:T(8,128)} %shard_map.176), calls=%async_computation.3 | async-start | bytes 786432 | tf_op jit(solution)/shard_map/all_to_all | solution.py:293
  122.8 18.9 %copy-start.5 = (bf16[8,320,128]{2,0,1:T(8,128)(2,1)S(1)}, bf16[8,320,128]{2,0,1:T(8,128)(2,1)}, u32[]{:S(2)}) copy-start(bf16[8,320,128]{2,0,1:T(8,128)(2,1)} %copy.62) | copy-start | bytes 1966084
  132.9 0.7 copy-start.3
  136.4 15.1 %all-to-all-start.6 = ((bf16[8,320,128]{2,1,0:T(8,128)(2,1)}), bf16[8,320,128]{2,1,0:T(8,128)(2,1)S(1)}, u32[]{:S(2)}, u32[]{:S(2)}) async-start(bf16[8,320,128]{2,1,0:T(8,128)(2,1)} %get-tuple-element.6), calls=%async_computation.6 | async-start | bytes 1310720 | tf_op jit(solution)/shard_map/all_to_all | solution.py:293
  180.3 11.2 %all-to-all-start.4 = ((bf16[4,4,40,128]{3,2,1,0:T(8,128)(2,1)}), bf16[4,4,40,128]{3,2,1,0:T(8,128)(2,1)S(1)}, u32[]{:S(2)}, u32[]{:S(2)}) async-start(bf16[4,4,40,128]{3,2,1,0:T(8,128)(2,1)} %get-tuple-element.5), calls=%async_computation.4 | async-start | bytes 327680 | tf_op jit(solution)/shard_map/all_to_all | solution.py:293
  192.2 7.5 %all-to-all-start.8 = ((f32[4,16,128]{2,1,0:T(8,128)}), f32[4,16,128]{2,1,0:T(8,128)S(1)}, u32[]{:S(2)}, u32[]{:S(2)}) async-start(f32[4,16,128]{2,1,0:T(8,128)} %broadcast_in_dim.83), calls=%async_computation.8 | async-start | bytes 65536 | tf_op jit(solution)/shard_map/all_to_all | solution.py:293

commit v2 on v1

--- a/solution.py
+++ b/solution.py
@@ -82,54 +82,83 @@
     return lax.dot_general(left, right, (dims, ((), ())), preferred_element_type=F32)
 
 
+def exponent(peak):
+    return jnp.ceil(jnp.log2(jnp.maximum(peak, 1e-30)))
+
+
+def encode_scale(power):
+    return jnp.exp2(15.0 - power) * 0.999
+
+
+def decode_scale(power):
+    return jnp.exp2(power - 15.0) * (1.0 / 0.999)
+
+
+def to_short(value):
+    return jnp.floor(value + 0.5).astype(jnp.int32).astype(jnp.int16)
+
+
+def from_short(value):
+    return value.astype(jnp.int32).astype(F32)
+
+
 def spread_kernel(part_ref, high_ref, low_ref, out_ref):
+    powers, tails = [], []
     for band in range(BANDS):
         real = part_ref[:, 2 * band].reshape(STICKS, NG)
         imag = part_ref[:, 2 * band + 1].reshape(STICKS, NG)
         both = jnp.concatenate([real, imag], axis=1)
         field = dot(high_ref[...], both, ((1,), (1,))) + dot(low_ref[...], both, ((1,), (1,)))
-        out_ref[:, 16 * band : 16 * band + 16, :] = field[:, :NG].reshape(RING, 16, NG)
+        power = exponent(jnp.max(jnp.abs(field), axis=0, keepdims=True))
+        field = field * encode_scale(power)
+        out_ref[:, 16 * band : 16 * band + 16, :] = to_short(field[:, :NG]).reshape(RING, 16, NG)
         rest = field[:, NG:].reshape(RING, 2, 8, STICKS - NG)
-        for part in range(2):
-            g = 2 * band + part
-            out_ref[:, 32:40, 32 * g : 32 * g + 32] = rest[:, part]
+        tails += [rest[:, 0], rest[:, 1]]
+        powers.append(power)
     cells = part_ref[:, 2 * BANDS].reshape(STICKS, NG)
     lane = lax.broadcasted_iota(jnp.int32, (8, NG), 1)
-    row = lax.broadcasted_iota(jnp.int32, (8, NG), 0)
-    pick = jnp.where(row < 1, jnp.where(lane == 0, 128.0, jnp.where(lane == 1, 1.0, 0.0)), 0.0)
-    flat = dot(pick.astype(BF16), cells, ((1,), (1,)))
-    tail = jnp.concatenate([flat[0:1, NG:], jnp.zeros((1, 2 * NG - STICKS), F32)], axis=1)
+    pick = jnp.where(lane == 0, 128.0, jnp.where(lane == 1, 1.0, 0.0))
+    flat = dot(pick.astype(BF16), cells, ((1,), (1,)))[0:1]
     index = lax.broadcasted_iota(jnp.int32, (8, NG), 0)
-    block = jnp.where(index == 0, flat[0:1, :NG], jnp.where(index == 1, tail, 0.0))
-    out_ref[:, 40:48, :] = jnp.broadcast_to(block[None], (RING, 8, NG))
+    notes = jnp.zeros((8, NG), F32)
+    for place, line in enumerate((flat, *powers)):
+        tail = jnp.concatenate([line[:, NG:], jnp.zeros((1, 2 * NG - STICKS), F32)], axis=1)
+        notes = jnp.where(index == 2 * place, line[:, :NG], jnp.where(index == 2 * place + 1, tail, notes))
+    notes = jnp.broadcast_to(notes[None], (RING, 8, NG))
+    last = jnp.concatenate([jnp.concatenate(tails, axis=2), notes], axis=1)
+    out_ref[:, 32:48, :] = to_short(last)
 
 
 def plane_kernel(
-    recv_ref, v_ref, stack_ref, wide_ref, xa_ref, xh_ref, fh_ref, fl_ref, order_ref,
-    out_ref, val_ref, low_ref, cell_ref, onehot_ref, tall_ref, flat_ref, left_ref, mid_ref, lift_ref,
+    me_ref, recv_ref, v0_ref, v1_ref, v2_ref, v3_ref, stack_ref, wide_ref, xa_ref, xh_ref, fh_ref, fl_ref, order_ref,
+    out_ref, val_ref, low_ref, cell_ref, onehot_ref, tall_ref, flat_ref, left_ref, mid_ref, lift_ref, tail_ref,
 ):
     for src in range(RING):
-        val_ref[:, src * NG : (src + 1) * NG] = recv_ref[src, 0:32, :]
-        cell_ref[:, src * NG : (src + 1) * NG] = jnp.broadcast_to(recv_ref[src, 40:41, :], (8, NG))
+        val_ref[:, src * NG : (src + 1) * NG] = from_short(recv_ref[src, 0:32, :])
+        last = from_short(recv_ref[src, 32:48, :])
         start = RING * NG + 32 * src
         for g in range(4):
-            val_ref[8 * g : 8 * g + 8, start : start + 32] = recv_ref[src, 32:40, 32 * g : 32 * g + 32]
-        cell_ref[:, start : start + 32] = jnp.broadcast_to(recv_ref[src, 41:42, 0:32], (8, 32))
-
-    cells = cell_ref[...].astype(jnp.int32)
+            val_ref[8 * g : 8 * g + 8, start : start + 32] = last[:8, 32 * g : 32 * g + 32]
+        for place in range(3):
+            cell_ref[place : place + 1, src * NG : (src + 1) * NG] = last[8 + 2 * place : 9 + 2 * place]
+            cell_ref[place : place + 1, start : start + 32] = last[9 + 2 * place : 10 + 2 * place, 0:32]
+
+    cells = cell_ref[0:1, :].astype(jnp.int32)
     x_index = jnp.bitwise_and(lax.shift_right_logical(cells, 7) + RAD, NG - 1)
     y_index = jnp.bitwise_and(cells, NG - 1)
-    x_row, y_row = x_index[0:1], y_index[0:1]
     onehot_ref[...] = jnp.where(
-        lax.broadcasted_iota(jnp.int32, (WIN, ALL), 0) == x_row, 1.0, 0.0
+        lax.broadcasted_iota(jnp.int32, (WIN, ALL), 0) == x_index, 1.0, 0.0
     ).astype(BF16)
-    pick_y = jnp.where(lax.broadcasted_iota(jnp.int32, (NG, ALL), 0) == y_row, 1.0, 0.0).astype(BF16)
+    pick_y = jnp.where(lax.broadcasted_iota(jnp.int32, (NG, ALL), 0) == y_index, 1.0, 0.0).astype(BF16)
     flat_ref[...] = dot(stack_ref[...], pick_y).astype(BF16)
     tall_ref[...] = dot(pick_y, wide_ref[...], ((0,), (0,))).astype(BF16)
 
-    rounded = val_ref[...].astype(BF16).astype(F32)
-    low_ref[...] = val_ref[...] - rounded
-    val_ref[...] = rounded
+    for band in range(BANDS):
+        half = slice(16 * band, 16 * band + 16)
+        value = val_ref[half, :] * decode_scale(cell_ref[1 + band : 2 + band, :])
+        rounded = value.astype(BF16).astype(F32)
+        low_ref[half, :] = value - rounded
+        val_ref[half, :] = rounded
 
     lane = lax.broadcasted_iota(jnp.int32, (WIN, NG), 1)
     first = jnp.bitwise_and(lane, WIN - 1) == 0
@@ -140,7 +169,8 @@
         for g in range(4):
             for part, ref in enumerate((val_ref, low_ref)):
                 row = ref[pl.ds(8 * g + z, 1), :]
-                spread = jnp.broadcast_to(row, (WIN, ALL)).astype(BF16)
+                spread = jnp.broadcast_to(row, (16, ALL)).astype(BF16)
+                spread = jnp.concatenate([spread] * (WIN // 16), axis=0)
                 at = (2 * g + part) * WIN
                 left_ref[at : at + WIN, :] = spread * onehot_ref[...]
         full = dot(left_ref[...], tall_ref[...])
@@ -154,10 +184,11 @@
             mid_ref[z, 0:WIN, band * NG : (band + 1) * NG] = new_real
             mid_ref[z, WIN:, band * NG : (band + 1) * NG] = new_imag
 
-    for owner in range(GROUP):
+    me = me_ref[0]
+    for turn, v_ref in enumerate((v0_ref, v1_ref, v2_ref, v3_ref)):
         for i in range(2):
-            z = 2 * owner + i
-            potential = dot(v_ref[owner, 0, i], order_ref[...]) + dot(v_ref[owner, 1, i], order_ref[...])
+            z = 2 * jnp.bitwise_xor(me, turn) + i
+            potential = dot(v_ref[0, i], order_ref[...]) + dot(v_ref[1, i], order_ref[...])
             high, low = split(mid_ref[z])
             field = dot(xa_ref[...], jnp.concatenate([high, high], axis=0)) + dot(xh_ref[...], low)
             wide = jnp.concatenate([potential, potential], axis=1)
@@ -184,12 +215,21 @@
             full = dot(rows, flat_ref[0:256, cols]) + dot(rows, flat_ref[256:512, cols])
             val_ref[8 * g : 8 * g + 8, cols] = jnp.sum(full.reshape(8, WIN, 256) * select, axis=1)
 
+    for band in range(BANDS):
+        half = slice(16 * band, 16 * band + 16)
+        power = exponent(jnp.max(jnp.abs(val_ref[half, :]), axis=0, keepdims=True))
+        cell_ref[1 + band : 2 + band, :] = power
+        val_ref[half, :] = val_ref[half, :] * encode_scale(power)
+    tail_ref[...] = jnp.zeros((RING, 16, NG), F32)
     for src in range(RING):
-        out_ref[src, 0:32, :] = val_ref[:, src * NG : (src + 1) * NG]
+        out_ref[src, 0:32, :] = to_short(val_ref[:, src * NG : (src + 1) * NG])
         start = RING * NG + 32 * src
         for g in range(4):
-            out_ref[src, 32:40, 32 * g : 32 * g + 32] = val_ref[8 * g : 8 * g + 8, start : start + 32]
-        out_ref[src, 40:48, :] = jnp.zeros((8, NG), F32)
+            tail_ref[src, 0:8, 32 * g : 32 * g + 32] = val_ref[8 * g : 8 * g + 8, start : start + 32]
+        for place in range(1, 3):
+            tail_ref[src, 8 + 2 * place : 9 + 2 * place, :] = cell_ref[place : place + 1, src * NG : (src + 1) * NG]
+            tail_ref[src, 9 + 2 * place : 10 + 2 * place, 0:32] = cell_ref[place : place + 1, start : start + 32]
+    out_ref[:, 32:48, :] = to_short(tail_ref[...])
 
 
 def finish_kernel(recv_ref, part_ref, high_ref, low_ref, out_ref, copies_ref, line_ref, pack_ref):
@@ -203,12 +243,15 @@
     weight = jnp.where(total <= RAD * RAD, 1.0, 0.0)
     kinetic = 2.0 / (RAD * RAD) * total
     for band in range(BANDS):
-        line_ref[:, 0:NG] = recv_ref[:, 16 * band : 16 * band + 16, :].reshape(2 * NG, NG)
         for src in range(RING):
+            last = from_short(recv_ref[src, 32:48, :])
+            main = from_short(recv_ref[src, 16 * band : 16 * band + 16, :])
+            scale = decode_scale(last[10 + 2 * band : 12 + 2 * band])
+            line_ref[16 * src : 16 * src + 16, 0:NG] = main * scale[0:1]
             for part in range(2):
                 g = 2 * band + part
                 at = 16 * src + 8 * part
-                line_ref[at : at + 8, NG : NG + 32] = recv_ref[src, 32:40, 32 * g : 32 * g + 32]
+                line_ref[at : at + 8, NG : NG + 32] = last[:8, 32 * g : 32 * g + 32] * scale[1:2, 0:32]
         high, low = split(jnp.transpose(line_ref[...])[:STICKS])
         product = dot(high, high_ref[...]) + dot(low, high_ref[...]) + dot(high, low_ref[...])
         for part in range(2):
@@ -226,12 +269,13 @@
         copies_ref[copy] = packed
 
 
-def vmem_call(kernel, out_shape, inputs, scratch=()):
+def vmem_call(kernel, out_shape, inputs, scratch=(), scalars=0):
     vmem = pl.BlockSpec(memory_space=pltpu.VMEM)
+    smem = pl.BlockSpec(memory_space=pltpu.SMEM)
     return pl.pallas_call(
         kernel,
         out_shape=out_shape,
-        in_specs=[vmem] * len(inputs),
+        in_specs=[smem] * scalars + [vmem] * (len(inputs) - scalars),
         out_specs=jax.tree.map(lambda _: vmem, out_shape),
         scratch_shapes=list(scratch),
         compiler_params=pltpu.CompilerParams(vmem_limit_bytes=56 * 1024 * 1024),
@@ -240,15 +284,15 @@
 
 def spread(part):
     (high, low), _ = depth_tables()
-    shape = jax.ShapeDtypeStruct((RING, ROWS, NG), F32)
+    shape = jax.ShapeDtypeStruct((RING, ROWS, NG), jnp.int16)
     return vmem_call(spread_kernel, shape, (part, high, low))
 
 
-def planes(recv, potentials):
+def planes(me, recv, potentials):
     stack, wide = across_tables()
     (xh, xl), (fh, fl) = down_tables()
     xa = np.concatenate([xh, xl], axis=1)
-    shape = jax.ShapeDtypeStruct((RING, ROWS, NG), F32)
+    shape = jax.ShapeDtypeStruct((RING, ROWS, NG), jnp.int16)
     scratch = (
         pltpu.VMEM((32, ALL), F32),
         pltpu.VMEM((32, ALL), F32),
@@ -259,9 +303,10 @@
         pltpu.VMEM((8 * WIN, ALL), BF16),
         pltpu.VMEM((8, 2 * WIN, 2 * NG), F32),
         pltpu.VMEM((4, 8, WIN, 2 * NG), BF16),
+        pltpu.VMEM((RING, 16, NG), F32),
     )
-    inputs = (recv, potentials, stack, wide, xa, xh, fh, fl, lane_order())
-    return vmem_call(plane_kernel, shape, inputs, scratch)
+    inputs = (me, recv, *potentials, stack, wide, xa, xh, fh, fl, lane_order())
+    return vmem_call(plane_kernel, shape, inputs, scratch, 1)
 
 
 def finish(recv, part, copies):
@@ -280,15 +325,24 @@
     return value[:, :, :half] + jnp.roll(value[:, :, half:], NG // 2, axis=3)
 
 
-def pairing(bands, vectors):
-    full = lax.dot_general(
-        bands, vectors, (((0, 3, 4), (3, 4, 5)), ((), ())), preferred_element_type=F32
-    )
+def pairing(bands, vectors, labels):
+    full = jnp.einsum("snprl," + labels + "->npgbq", bands, vectors, preferred_element_type=F32)
     real = full[:, 0, :, :, 0] + full[:, 1, :, :, 1]
     imag = full[:, 0, :, :, 1] - full[:, 1, :, :, 0]
     return jnp.stack([real, imag])
 
 
+def partner(value, turn, size):
+    return lax.ppermute(value, "pw", [(i, i ^ turn) for i in range(size)])
+
+
+def place(pieces, me):
+    result = jnp.zeros((GROUP, *pieces[0].shape), pieces[0].dtype)
+    for turn, piece in enumerate(pieces):
+        result = lax.dynamic_update_index_in_dim(result, piece, jnp.bitwise_xor(me, turn), 0)
+    return result
+
+
 def exchange(value, axis, groups=None):
     return lax.all_to_all(value, axis, 0, 0, axis_index_groups=groups, tiled=True)
 
@@ -300,6 +354,7 @@
 def per_device(block, bands, potential, stick_cells, sphere_mask):
     size = lax.axis_size("pw")
     teams = lax.axis_size("band")
+    me = jnp.bitwise_and(lax.axis_index("pw"), GROUP - 1)
     own, sticks, rows = block.shape[0], block.shape[2], bands.shape[0]
     fours = [[i * GROUP + j for j in range(GROUP)] for i in range(size // GROUP)]
     rings = [[i * GROUP + j for i in range(size // GROUP)] for j in range(GROUP)]
@@ -318,20 +373,26 @@
     v_high = lax.reduce_precision(potential, 8, 7)
     v_low = (potential - v_high).astype(BF16)
     potential_rows = jnp.stack([v_high.astype(BF16), v_low]).reshape(-1, NG)
-    side = to_all(jnp.concatenate([bands_rows, potential_rows], axis=0), "pw", GROUP, fours)
+    side = jnp.concatenate([bands_rows, potential_rows], axis=0)
+    sides = [side] + [partner(side, turn, size) for turn in range(1, GROUP)]
     split_at = bands_rows.shape[0]
-    bands_all = side[:, :split_at].reshape(GROUP, rows, 2, sticks // 2, NG)
-    potentials = side[:, split_at:].reshape(GROUP, 2, potential.shape[0], NG, NG)
-    shape = (teams, BANDS, 2, GROUP, sticks // 2, NG)
-    packed = jnp.transpose(pack(part[:, : 2 * BANDS]), (1, 0, 2, 3)).reshape(-1, NG)
-    masked_all = to_all(packed, "band", teams).reshape(shape)
-
-    back = exchange(planes(recv, potentials), "pw", rings)
+    bands_all = place([piece[:split_at] for piece in sides], me).reshape(GROUP, rows, 2, sticks // 2, NG)
+    potentials = [piece[split_at:].reshape(2, potential.shape[0], NG, NG) for piece in sides]
+    vectors = part[:, : 2 * BANDS].reshape(GROUP * BANDS, 2, sticks, NG)
+    masked_all = lax.all_gather(jnp.stack([vectors, vectors]), "band", axis=1, tiled=True)[0]
+    masked_all = pack(masked_all.reshape(teams * GROUP * BANDS, 2, sticks, NG))
+    masked_all = masked_all.reshape(teams, GROUP, BANDS, 2, sticks // 2, NG)
+
+    back = exchange(planes(me.reshape(1), recv, potentials), "pw", rings)
     result, copies = finish(back, part, teams)
-    applied_all = exchange(copies, "band").reshape(shape)
-    applied = exchange(result, "pw", fours).reshape(own, 2, sticks, NG)
-
-    terms = jnp.stack([pairing(bands_all, masked_all), pairing(bands_all, applied_all)])
+    applied_all = exchange(copies, "band").reshape(teams, BANDS, 2, GROUP, sticks // 2, NG)
+    pieces = [lax.dynamic_index_in_dim(result, jnp.bitwise_xor(me, turn), 0, False) for turn in range(GROUP)]
+    pieces = pieces[:1] + [partner(pieces[turn], turn, size) for turn in range(1, GROUP)]
+    applied = place(pieces, me).reshape(own, 2, sticks, NG)
+
+    terms = jnp.stack(
+        [pairing(bands_all, masked_all, "gsbqrl"), pairing(bands_all, applied_all, "gbqsrl")]
+    )
     total = jnp.sum(to_all(terms.reshape(-1, NG), "pw", size // GROUP, rings), axis=0)
     total = to_all(total, "pw", GROUP, fours).reshape(GROUP, 2, 2, rows, teams, BANDS)
     total = jnp.transpose(total, (1, 2, 3, 4, 0, 5)).reshape(2, 2, rows, teams * own)

time: 204 us -> 234 us (1.15); the launches traced: 203 us -> 230 us
  local copies, waits for them, and re-layouts: 17.4 us -> 91.9 us
  waiting for transfers between devices: 66.5 us -> 16.2 us
  between operations: 0.88 us -> 14.5 us
  blocking collectives: 26.7 us -> 14 us
    dynamic_update_slice x0 -> x7, local copies, waits for them, and re-layouts: none -> 63.6 us  [place(): lax.dynamic_update_index_in_dim(result, piece, jnp.bitwise_xor(me, turn), 0)]
    all_to_all x8 -> x5, waiting for transfers between devices: 66.5 us -> 11.3 us  [exchange(): lax.all_to_all(value, axis, 0, 0, axis_index_groups=groups, tiled=True)]
    ppermute x0 -> x6, starting transfers between devices: none -> 20.4 us  [partner(): return lax.ppermute(value, 'pw', [(i, i ^ turn) for i in range(size)])]
    all_to_all x8 -> x5, starting transfers between devices: 59.5 us -> 40.1 us  [exchange(): lax.all_to_all(value, axis, 0, 0, axis_index_groups=groups, tiled=True)]
    broadcast_in_dim x0 -> x9, local copies, waits for them, and re-layouts: none -> 17 us  [the longest x7 16.6 us: place(): lax.dynamic_update_index_in_dim(result, piece, jnp.bitwise_xor(me, turn), 0)]
    all_to_all x1, blocking collectives: 26.7 us -> 14 us  [exchange(): lax.all_to_all(value, axis, 0, 0, axis_index_groups=groups, tiled=True)]
    ppermute x0 -> x6, waiting for transfers between devices: none -> 4.82 us  [partner(): return lax.ppermute(value, 'pw', [(i, i ^ turn) for i in range(size)])]
    slice x3 -> x4, local copies, waits for them, and re-layouts: 7.05 us -> 2.97 us  [the longest x3 2.95 us: per_device(): piece[split_at:].reshape(2, potential.shape[0], NG, NG)]
  transfers between devices with their start and end apart: 8 -> 12, of which waited for: 7 -> 4; matrix products, arithmetic and copies ran while one was open for 5% -> 40% of each run, Pallas kernels for 12% -> 11%
where the time goes in v2:
time: 234 us; the launch traced here: 230 us
  local copies, waits for them, and re-layouts  91.9 us (39%)
  starting transfers between devices  60.6 us (26%)
  Pallas kernels  26.3 us (11%)
  waiting for transfers between devices  16.2 us (7%)
  between operations  14.5 us (6%)
  blocking collectives  14 us (6%)
  other arithmetic  4.15 us (2%)
    dynamic_update_slice x7, local copies, waits for them, and re-layouts, place(): lax.dynamic_update_index_in_dim(result, piece, jnp.bitwise_xor(me, turn), 0)  63.6 us
    all_to_all x5, starting transfers between devices, exchange(): lax.all_to_all(value, axis, 0, 0, axis_index_groups=groups, tiled=True)  40.1 us
    pallas_call x3, Pallas kernels, vmem_call(): pl.pallas_call(kernel, out_shape=out_shape, in_specs=[smem] * scalars + [...  26.3 us
    ppermute x6, starting transfers between devices, partner(): return lax.ppermute(value, 'pw', [(i, i ^ turn) for i in range(size)])  20.4 us
    broadcast_in_dim x7, local copies, waits for them, and re-layouts, place(): lax.dynamic_update_index_in_dim(result, piece, jnp.bitwise_xor(me, turn), 0)  16.6 us
    all_to_all x1, blocking collectives, exchange(): lax.all_to_all(value, axis, 0, 0, axis_index_groups=groups, tiled=True)  14 us
    all_to_all x5, waiting for transfers between devices, exchange(): lax.all_to_all(value, axis, 0, 0, axis_index_groups=groups, tiled=True)  11.3 us
    ppermute x6, waiting for transfers between devices, partner(): return lax.ppermute(value, 'pw', [(i, i ^ turn) for i in range(size)])  4.82 us
  transfers between devices with their start and end apart: 12, of which 4 were waited for; matrix products, arithmetic and copies ran while one was open for 40% of the time, Pallas kernels for 11%

profile of v2, /device:TPU:1, one launch (start us, length us, event | category | flops | bytes accessed | tf_op | source)
XLA Modules:
  0.0 229.9 jit_solution(5900700310801829571)
XLA Ops:
  7.2 0.7 and_select_fusion.1
  7.9 0.7 convert_element_type.16
  8.6 1.0 broadcast_multiply_fusion.1
  9.7 14.0 %all_to_all.30.part_ref = bf16[4,5,40,128]{3,2,1,0:T(8,128)(2,1)S(1)} all-to-all(bf16[4,5,40,128]{3,2,1,0:T(8,128)(2,1)S(1)} %pad_maximum_fusion.2), channel_id=1, replica_groups={{0,1,2,3},{4,5,6,7},{8,9,10,11},{12,13,14,15},{16,17,18,19},{20,21,22,2..., dimensions={0} | all-to-all | bytes 409600 | tf_op jit(solution)/shard_map/all_to_all | solution.py:347
  23.8 0.8 pad_maximum_fusion.1
  25.3 2.3 shard_map.175
  27.6 9.7 %all-to-all-start.1 = ((s16[16,48,128]{2,1,0:T(8,128)(2,1)}), s16[16,48,128]{2,1,0:T(8,128)(2,1)S(1)}, u32[]{:S(2)}, u32[]{:S(2)}) async-start(s16[16,48,128]{2,1,0:T(8,128)(2,1)} %shard_map.175), calls=%async_computation.1 | async-start | bytes 393216 | tf_op jit(solution)/shard_map/all_to_all | solution.py:347
  37.5 3.0 %collective-permute-start = (bf16[1792,128]{1,0:T(8,128)(2,1)S(1)}, bf16[1792,128]{1,0:T(8,128)(2,1)S(1)}, u32[]{:S(2)}, u32[]{:S(2)}) collective-permute-start(bf16[1792,128]{1,0:T(8,128)(2,1)S(1)} %pad_maximum_fusion), channel_id=1, source_target_pairs={{0,1},{1,0},{2,3},{3,2},{4,5},{5,4},{6,7},{7,6},{8,9},{9,8},{10,11... | collective-permute-start | bytes 1376264 | tf_op jit(solution)/shard_map/ppermute | solution.py:336
  40.5 2.0 collective-permute-start.1
  42.5 3.5 %collective-permute-start.2 = (bf16[1792,128]{1,0:T(8,128)(2,1)S(1)}, bf16[1792,128]{1,0:T(8,128)(2,1)S(1)}, u32[]{:S(2)}, u32[]{:S(2)}) collective-permute-start(bf16[1792,128]{1,0:T(8,128)(2,1)S(1)} %pad_maximum_fusion), channel_id=1, source_target_pairs={{0,3},{1,2},{2,1},{3,0},{4,7},{5,6},{6,5},{7,4},{8,11},{9,10},{10,... | collective-permute-start | bytes 1376264 | tf_op jit(solution)/shard_map/ppermute | solution.py:336
  46.2 0.4 broadcast_in_dim.99
  46.6 13.9 %dynamic_update_slice.30 = bf16[4,1280,128]{2,0,1:T(4,128)(2,1)S(1)} dynamic-update-slice(bf16[4,1280,128]{2,0,1:T(4,128)(2,1)S(1)} %broadcast_in_dim.99, bf16[1,1280,128]{2,0,1:T(2,128)(2,1)S(1)} %broadcast_in_dim.107, s32[]{:T(128)S(6)} %select_n.57, s32[]{:T(128)} %constant.85.clone.1, s32[]{:T(128)} %constant.85.clone.1) | dynamic-update-slice | bytes 655364 | tf_op jit(solution)/shard_map/jit(dynamic_update_index_in_dim)/dynamic_update_slice | solution.py:342
  60.5 0.7 slice.111
  61.2 1.6 slice.112
  62.8 4.8 %collective-permute-done.2 = bf16[1792,128]{1,0:T(8,128)(2,1)S(1)} collective-permute-done((bf16[1792,128]{1,0:T(8,128)(2,1)S(1)}, bf16[1792,128]{1,0:T(8,128)(2,1)S(1)}, u32[]{:S(2)}, u32[]{:S(2)}) %collective-permute-start.2) | collective-permute-done | bytes 458784 | tf_op jit(solution)/shard_map/ppermute | solution.py:336
  67.6 0.7 slice.113
  68.3 0.7 copy-done.4
  69.0 21.3 %shard_map.176 = s16[16,48,128]{2,1,0:T(8,128)(2,1)} custom-call(s32[1]{0:T(128)} %bitcast.me_ref, s16[16,48,128]{2,1,0:T(8,128)(2,1)} %copy-done.4, bf16[2,2,128,128]{3,2,1,0:T(8,128)(2,1)} %copy-done.3, bf16[2,2,128,128]{3,2,1,0:T(8,128)(2,1)} %bitcast.90, bf16[2,2,128,128]{3,2,1,0:T(8,128)(2,1)} %bitcast.91, bf16[2,2,128,128]{3,2,1,0:T(8,128)(2,1)} %bitcast.92, ...), custom_call_target="tpu_custom_call" | custom-call | tf_op jit(solution)/shard_map/pallas_call | solution.py:275
  90.3 12.1 %all-to-all-start.2 = ((s16[16,48,128]{2,1,0:T(8,128)(2,1)}), s16[16,48,128]{2,1,0:T(8,128)(2,1)S(1)}, u32[]{:S(2)}, u32[]{:S(2)}) async-start(s16[16,48,128]{2,1,0:T(8,128)(2,1)} %shard_map.176), calls=%async_computation.2 | async-start | bytes 393216 | tf_op jit(solution)/shard_map/all_to_all | solution.py:347
  102.4 5.1 %copy.72 = bf16[1,1280,128]{2,0,1:T(2,128)(2,1)S(1)} copy(bf16[1,1280,128]{2,1,0:T(8,128)(2,1)S(1)} %slice_bitcast_fusion.3) | data formatting | bytes 655360 | tf_op jit(solution)/shard_map/jit(dynamic_update_index_in_dim)/broadcast_in_dim | solution.py:342
  107.5 1.0 slice_bitcast_fusion.2
  108.5 5.1 %copy.73 = bf16[1,1280,128]{2,0,1:T(2,128)(2,1)S(1)} copy(bf16[1,1280,128]{2,1,0:T(8,128)(2,1)S(1)} %slice_bitcast_fusion.2) | data formatting | bytes 655360 | tf_op jit(solution)/shard_map/jit(dynamic_update_index_in_dim)/broadcast_in_dim | solution.py:342
  113.6 1.6 all-to-all-done.2.recv_ref
  115.2 0.7 copy-done.5
  115.9 2.7 %shard_map.177 = (bf16[4,4,40,128]{3,2,1,0:T(8,128)(2,1)}, bf16[8,320,128]{2,1,0:T(8,128)(2,1)}) custom-call(s16[16,48,128]{2,1,0:T(8,128)(2,1)} %copy-done.5, bf16[4,5,40,128]{3,2,1,0:T(8,128)(2,1)} %copy-done, bf16[256,256]{1,0:T(8,128)(2,1)} %constant.94.clone.high_ref, bf16[256,256]{1,0:T(8,128)(2,1)} %constant.95.clone.low_ref), custom_call_target="tpu_custom_call" | custom-call | tf_op jit(solution)/shard_map/pallas_call | solution.py:275
  118.6 6.0 %all-to-all-start.3 = ((bf16[8,320,128]{2,1,0:T(8,128)(2,1)}), bf16[8,320,128]{2,1,0:T(8,128)(2,1)S(1)}, u32[]{:S(2)}, u32[]{:S(2)}) async-start(bf16[8,320,128]{2,1,0:T(8,128)(2,1)} %get-tuple-element.6), calls=%async_computation.3 | async-start | bytes 1310720 | tf_op jit(solution)/shard_map/all_to_all | solution.py:347
  124.7 5.1 %copy.74 = bf16[1,1280,128]{2,0,1:T(2,128)(2,1)S(1)} copy(bf16[1,1280,128]{2,1,0:T(8,128)(2,1)S(1)} %slice_bitcast_fusion.1) | data formatting | bytes 655360 | tf_op jit(solution)/shard_map/jit(dynamic_update_index_in_dim)/broadcast_in_dim | solution.py:342
  129.8 16.5 %dynamic_update_slice.31 = bf16[4,1280,128]{2,0,1:T(4,128)(2,1)} dynamic-update-slice(bf16[4,1280,128]{2,0,1:T(4,128)(2,1)} %copy-done.1, bf16[1,1280,128]{2,0,1:T(2,128)(2,1)S(1)} %copy.72, s32[]{:T(128)S(6)} %select_n.58, s32[]{:T(128)} %constant.85.clone.1, s32[]{:T(128)} %constant.85.clone.1) | dynamic-update-slice | bytes 655364 | tf_op jit(solution)/shard_map/jit(dynamic_update_index_in_dim)/dynamic_update_slice | solution.py:342
  146.4 16.6 %dynamic_update_slice.32 = bf16[4,1280,128]{2,0,1:T(4,128)(2,1)} dynamic-update-slice(bf16[4,1280,128]{2,0,1:T(4,128)(2,1)} %dynamic_update_slice.31, bf16[1,1280,128]{2,0,1:T(2,128)(2,1)S(1)} %copy.73, s32[]{:T(128)S(6)} %select_n.59, s32[]{:T(128)} %constant.85.clone.1, s32[]{:T(128)} %constant.85.clone.1) | dynamic-update-slice | bytes 655364 | tf_op jit(solution)/shard_map/jit(dynamic_update_index_in_dim)/dynamic_update_slice | solution.py:342
  162.9 16.5 %dynamic_update_slice.33 = bf16[4,1280,128]{2,0,1:T(4,128)(2,1)} dynamic-update-slice(bf16[4,1280,128]{2,0,1:T(4,128)(2,1)} %dynamic_update_slice.32, bf16[1,1280,128]{2,0,1:T(2,128)(2,1)S(1)} %copy.74, s32[]{:T(128)S(6)} %select_n.60, s32[]{:T(128)} %constant.85.clone.1, s32[]{:T(128)} %constant.85.clone.1) | dynamic-update-slice | bytes 655364 | tf_op jit(solution)/shard_map/jit(dynamic_update_index_in_dim)/dynamic_update_slice | solution.py:342
  179.5 6.3 %collective-permute-start.3 = (bf16[4,40,128]{2,1,0:T(8,128)(2,1)S(1)}, bf16[4,40,128]{2,1,0:T(8,128)(2,1)S(1)}, u32[]{:S(2)}, u32[]{:S(2)}) collective-permute-start(bf16[4,40,128]{2,1,0:T(8,128)(2,1)S(1)} %get-tuple-element.24), channel_id=1, source_target_pairs={{0,1},{1,0},{2,3},{3,2},{4,5},{5,4},{6,7},{7,6},{8,9},{9,8},{10,11... | collective-permute-start | bytes 122888 | tf_op jit(solution)/shard_map/ppermute | solution.py:336
  185.8 0.4 copy.81
  186.3 1.1 fusion.7
  187.4 1.4 slice_bitcast_fusion
  189.2 0.5 slice_add_fusion
  189.6 1.1 fusion.4
  191.4 0.7 broadcast_in_dim.105
  192.0 7.1 %all-to-all-start.4 = ((f32[16,16,128]{2,1,0:T(8,128)}), f32[16,16,128]{2,1,0:T(8,128)S(1)}, u32[]{:S(2)}, u32[]{:S(2)}) async-start(f32[16,16,128]{2,1,0:T(8,128)} %broadcast_in_dim.105), calls=%async_computation.4 | async-start | bytes 262144 | tf_op jit(solution)/shard_map/all_to_all | solution.py:347
  199.2 2.0 collective-permute-start.4
  201.2 3.8 %collective-permute-start.5 = (bf16[4,40,128]{2,1,0:T(8,128)(2,1)S(1)}, bf16[4,40,128]{2,1,0:T(8,128)(2,1)S(1)}, u32[]{:S(2)}, u32[]{:S(2)}) collective-permute-start(bf16[4,40,128]{2,1,0:T(8,128)(2,1)S(1)} %get-tuple-element.22), channel_id=1, source_target_pairs={{0,3},{1,2},{2,1},{3,0},{4,7},{5,6},{6,5},{7,4},{8,11},{9,10},{10,... | collective-permute-start | bytes 122888 | tf_op jit(solution)/shard_map/ppermute | solution.py:336
  205.0 6.6 %all-to-all-done.4 = f32[16,16,128]{2,1,0:T(8,128)S(1)} async-done(((f32[16,16,128]{2,1,0:T(8,128)}), f32[16,16,128]{2,1,0:T(8,128)S(1)}, u32[]{:S(2)}, u32[]{:S(2)}) %all-to-all-start.4) | async-done | bytes 131104 | tf_op jit(solution)/shard_map/all_to_all | solution.py:347
  211.6 0.6 broadcast_in_dim.106
  212.3 5.1 %all-to-all-start.5 = ((f32[4,16,128]{2,1,0:T(8,128)}), f32[4,16,128]{2,1,0:T(8,128)S(1)}, u32[]{:S(2)}, u32[]{:S(2)}) async-start(f32[4,16,128]{2,1,0:T(8,128)} %broadcast_in_dim.106), calls=%async_computation.5 | async-start | bytes 65536 | tf_op jit(solution)/shard_map/all_to_all | solution.py:347
  217.4 3.1 %all-to-all-done.5 = f32[4,16,128]{2,1,0:T(8,128)S(1)} async-done(((f32[4,16,128]{2,1,0:T(8,128)}), f32[4,16,128]{2,1,0:T(8,128)S(1)}, u32[]{:S(2)}, u32[]{:S(2)}) %all-to-all-start.5) | async-done | bytes 32800 | tf_op jit(solution)/shard_map/all_to_all | solution.py:347
  220.5 0.4 copy.89
  221.0 0.3 copy.90
  221.3 0.7 copy.92
  222.4 0.7 copy.93
  (61 shorter events, 2.8 us)
Async XLA Ops:
  7.2 180.3 %all-gather.2.cloned.1.call-start = ((), (), s32[]{:S(2)}) async-start(), calls=%async_computation.6 | async-start | bytes 2949120 | tf_op jit(solution)/shard_map/all_gather | solution.py:382
  8.6 16.0 %copy-start.9 = (f32[2,128,128]{2,1,0:T(8,128)S(1)}, f32[2,128,128]{2,1,0:T(8,128)}, u32[]{:S(2)}) copy-start(f32[2,128,128]{2,1,0:T(8,128)} %param.18) | copy-start | bytes 393220
  9.6 15.0 %copy-start.6 = (bf16[32,2,40,128]{3,2,1,0:T(8,128)(2,1)S(1)}, bf16[32,2,40,128]{3,2,1,0:T(8,128)(2,1)}, u32[]{:S(2)}) copy-start(bf16[32,2,40,128]{3,2,1,0:T(8,128)(2,1)} %param.17) | copy-start | bytes 1966084
  23.7 1.0 copy-start
  27.6 40.7 %all-to-all-start.1 = ((s16[16,48,128]{2,1,0:T(8,128)(2,1)}), s16[16,48,128]{2,1,0:T(8,128)(2,1)S(1)}, u32[]{:S(2)}, u32[]{:S(2)}) async-start(s16[16,48,128]{2,1,0:T(8,128)(2,1)} %shard_map.175), calls=%async_computation.1 | async-start | bytes 393216 | tf_op jit(solution)/shard_map/all_to_all | solution.py:347
  37.4 8.8 %copy-start.3 = (bf16[2,2,128,128]{3,2,1,0:T(8,128)(2,1)}, bf16[2,2,128,128]{3,2,1,0:T(8,128)(2,1)S(1)}, u32[]{:S(2)}) copy-start(bf16[2,2,128,128]{3,2,1,0:T(8,128)(2,1)S(1)} %pad_maximum_fusion.3.v0_ref) | copy-start | bytes 393220
  37.5 23.0 %collective-permute-start = (bf16[1792,128]{1,0:T(8,128)(2,1)S(1)}, bf16[1792,128]{1,0:T(8,128)(2,1)S(1)}, u32[]{:S(2)}, u32[]{:S(2)}) collective-permute-start(bf16[1792,128]{1,0:T(8,128)(2,1)S(1)} %pad_maximum_fusion), channel_id=1, source_target_pairs={{0,1},{1,0},{2,3},{3,2},{4,5},{5,4},{6,7},{7,6},{8,9},{9,8},{10,11... | collective-permute-start | bytes 1376264 | tf_op jit(solution)/shard_map/ppermute | solution.py:336
  40.5 20.7 %collective-permute-start.1 = (bf16[1792,128]{1,0:T(8,128)(2,1)S(1)}, bf16[1792,128]{1,0:T(8,128)(2,1)}, u32[]{:S(2)}, u32[]{:S(2)}) collective-permute-start(bf16[1792,128]{1,0:T(8,128)(2,1)S(1)} %pad_maximum_fusion), channel_id=1, source_target_pairs={{0,2},{1,3},{2,0},{3,1},{4,6},{5,7},{6,4},{7,5},{8,10},{9,11},{10,... | collective-permute-start | bytes 1376264 | tf_op jit(solution)/shard_map/ppermute | solution.py:336
  42.5 25.1 %collective-permute-start.2 = (bf16[1792,128]{1,0:T(8,128)(2,1)S(1)}, bf16[1792,128]{1,0:T(8,128)(2,1)S(1)}, u32[]{:S(2)}, u32[]{:S(2)}) collective-permute-start(bf16[1792,128]{1,0:T(8,128)(2,1)S(1)} %pad_maximum_fusion), channel_id=1, source_target_pairs={{0,3},{1,2},{2,1},{3,0},{4,7},{5,6},{6,5},{7,4},{8,11},{9,10},{10,... | collective-permute-start | bytes 1376264 | tf_op jit(solution)/shard_map/ppermute | solution.py:336
  60.5 29.8 %copy-start.1 = (bf16[4,1280,128]{2,0,1:T(4,128)(2,1)}, bf16[4,1280,128]{2,0,1:T(4,128)(2,1)S(1)}, u32[]{:S(2)}) copy-start(bf16[4,1280,128]{2,0,1:T(4,128)(2,1)S(1)} %dynamic_update_slice.30) | copy-start | bytes 3932164
  68.3 0.7 copy-start.4
  90.3 24.9 %all-to-all-start.2 = ((s16[16,48,128]{2,1,0:T(8,128)(2,1)}), s16[16,48,128]{2,1,0:T(8,128)(2,1)S(1)}, u32[]{:S(2)}, u32[]{:S(2)}) async-start(s16[16,48,128]{2,1,0:T(8,128)(2,1)} %shard_map.176), calls=%async_computation.2 | async-start | bytes 393216 | tf_op jit(solution)/shard_map/all_to_all | solution.py:347
  115.2 0.7 copy-start.5
  118.6 67.2 %all-to-all-start.3 = ((bf16[8,320,128]{2,1,0:T(8,128)(2,1)}), bf16[8,320,128]{2,1,0:T(8,128)(2,1)S(1)}, u32[]{:S(2)}, u32[]{:S(2)}) async-start(bf16[8,320,128]{2,1,0:T(8,128)(2,1)} %get-tuple-element.6), calls=%async_computation.3 | async-start | bytes 1310720 | tf_op jit(solution)/shard_map/all_to_all | solution.py:347
  146.4 33.1 %copy-start.7 = (bf16[4,4,40,128]{3,2,1,0:T(8,128)(2,1)S(1)}, bf16[4,4,40,128]{3,2,1,0:T(8,128)(2,1)}, u32[]{:S(2)}) copy-start(bf16[4,4,40,128]{3,2,1,0:T(8,128)(2,1)} %get-tuple-element.5) | copy-start | bytes 491524
  179.5 6.8 %copy-start.2 = (bf16[4,1280,128]{2,0,1:T(4,128)(2,1)S(1)}, bf16[4,1280,128]{2,0,1:T(4,128)(2,1)}, u32[]{:S(2)}) copy-start(bf16[4,1280,128]{2,0,1:T(4,128)(2,1)} %dynamic_update_slice.33) | copy-start | bytes 3932164
  179.5 25.4 %collective-permute-start.3 = (bf16[4,40,128]{2,1,0:T(8,128)(2,1)S(1)}, bf16[4,40,128]{2,1,0:T(8,128)(2,1)S(1)}, u32[]{:S(2)}, u32[]{:S(2)}) collective-permute-start(bf16[4,40,128]{2,1,0:T(8,128)(2,1)S(1)} %get-tuple-element.24), channel_id=1, source_target_pairs={{0,1},{1,0},{2,3},{3,2},{4,5},{5,4},{6,7},{7,6},{8,9},{9,8},{10,11... | collective-permute-start | bytes 122888 | tf_op jit(solution)/shard_map/ppermute | solution.py:336
  192.0 19.6 %all-to-all-start.4 = ((f32[16,16,128]{2,1,0:T(8,128)}), f32[16,16,128]{2,1,0:T(8,128)S(1)}, u32[]{:S(2)}, u32[]{:S(2)}) async-start(f32[16,16,128]{2,1,0:T(8,128)} %broadcast_in_dim.105), calls=%async_computation.4 | async-start | bytes 262144 | tf_op jit(solution)/shard_map/all_to_all | solution.py:347
  199.2 5.8 %collective-permute-start.4 = (bf16[4,40,128]{2,1,0:T(8,128)(2,1)S(1)}, bf16[4,40,128]{2,1,0:T(8,128)(2,1)S(1)}, u32[]{:S(2)}, u32[]{:S(2)}) collective-permute-start(bf16[4,40,128]{2,1,0:T(8,128)(2,1)S(1)} %get-tuple-element.23), channel_id=1, source_target_pairs={{0,2},{1,3},{2,0},{3,1},{4,6},{5,7},{6,4},{7,5},{8,10},{9,11},{10,... | collective-permute-start | bytes 122888 | tf_op jit(solution)/shard_map/ppermute | solution.py:336
  201.2 16.2 %collective-permute-start.5 = (bf16[4,40,128]{2,1,0:T(8,128)(2,1)S(1)}, bf16[4,40,128]{2,1,0:T(8,128)(2,1)S(1)}, u32[]{:S(2)}, u32[]{:S(2)}) collective-permute-start(bf16[4,40,128]{2,1,0:T(8,128)(2,1)S(1)} %get-tuple-element.22), channel_id=1, source_target_pairs={{0,3},{1,2},{2,1},{3,0},{4,7},{5,6},{6,5},{7,4},{8,11},{9,10},{10,... | collective-permute-start | bytes 122888 | tf_op jit(solution)/shard_map/ppermute | solution.py:336
  212.3 8.3 %all-to-all-start.5 = ((f32[4,16,128]{2,1,0:T(8,128)}), f32[4,16,128]{2,1,0:T(8,128)S(1)}, u32[]{:S(2)}, u32[]{:S(2)}) async-start(f32[4,16,128]{2,1,0:T(8,128)} %broadcast_in_dim.106), calls=%async_computation.5 | async-start | bytes 65536 | tf_op jit(solution)/shard_map/all_to_all | solution.py:347
  217.4 3.6 %copy-start.8 = (bf16[4,4,40,128]{3,2,1,0:T(8,128)(2,1)}, bf16[4,4,40,128]{3,2,1,0:T(8,128)(2,1)S(1)}, u32[]{:S(2)}) copy-start(bf16[4,4,40,128]{3,2,1,0:T(8,128)(2,1)S(1)} %bitcast_dynamic-update-slice_fusion) | copy-start | bytes 491524
Sparse Core Ops, SparseCore 0:
  24.7 76.5 all-gather.1

commit v3 on v2

--- a/solution.py
+++ b/solution.py
@@ -131,8 +131,15 @@
 
 def plane_kernel(
     me_ref, recv_ref, v0_ref, v1_ref, v2_ref, v3_ref, stack_ref, wide_ref, xa_ref, xh_ref, fh_ref, fl_ref, order_ref,
-    out_ref, val_ref, low_ref, cell_ref, onehot_ref, tall_ref, flat_ref, left_ref, mid_ref, lift_ref, tail_ref,
+    out_ref, val_ref, low_ref, cell_ref, onehot_ref, tall_ref, flat_ref, left_a_ref, left_b_ref, mid_ref, lift_ref, tail_ref, v_ref, v_sem,
 ):
+    copies = [
+        pltpu.make_async_copy(source.at[pl.ds(0, 4 * NG), :], v_ref.at[turn], v_sem.at[turn])
+        for turn, source in enumerate((v0_ref, v1_ref, v2_ref, v3_ref))
+    ]
+    for copy in copies:
+        copy.start()
+
     for src in range(RING):
         val_ref[:, src * NG : (src + 1) * NG] = from_short(recv_ref[src, 0:32, :])
         last = from_short(recv_ref[src, 32:48, :])
@@ -164,8 +171,7 @@
     first = jnp.bitwise_and(lane, WIN - 1) == 0
     lower = lane < WIN
 
-    @pl.loop(0, 8)
-    def _(z):
+    def across(z, left_ref):
         for g in range(4):
             for part, ref in enumerate((val_ref, low_ref)):
                 row = ref[pl.ds(8 * g + z, 1), :]
@@ -184,11 +190,20 @@
             mid_ref[z, 0:WIN, band * NG : (band + 1) * NG] = new_real
             mid_ref[z, WIN:, band * NG : (band + 1) * NG] = new_imag
 
+    @pl.loop(0, 4)
+    def _(pair):
+        across(2 * pair, left_a_ref)
+        across(2 * pair + 1, left_b_ref)
+
     me = me_ref[0]
-    for turn, v_ref in enumerate((v0_ref, v1_ref, v2_ref, v3_ref)):
+    for copy in copies:
+        copy.wait()
+    for turn in range(GROUP):
         for i in range(2):
             z = 2 * jnp.bitwise_xor(me, turn) + i
-            potential = dot(v_ref[0, i], order_ref[...]) + dot(v_ref[1, i], order_ref[...])
+            at = i * NG
+            potential = dot(v_ref[turn, at : at + NG, :], order_ref[...])
+            potential += dot(v_ref[turn, at + 2 * NG : at + 3 * NG, :], order_ref[...])
             high, low = split(mid_ref[z])
             field = dot(xa_ref[...], jnp.concatenate([high, high], axis=0)) + dot(xh_ref[...], low)
             wide = jnp.concatenate([potential, potential], axis=1)
@@ -269,13 +284,12 @@
         copies_ref[copy] = packed
 
 
-def vmem_call(kernel, out_shape, inputs, scratch=(), scalars=0):
+def vmem_call(kernel, out_shape, inputs, scratch=(), specs=None):
     vmem = pl.BlockSpec(memory_space=pltpu.VMEM)
-    smem = pl.BlockSpec(memory_space=pltpu.SMEM)
     return pl.pallas_call(
         kernel,
         out_shape=out_shape,
-        in_specs=[smem] * scalars + [vmem] * (len(inputs) - scalars),
+        in_specs=specs or [vmem] * len(inputs),
         out_specs=jax.tree.map(lambda _: vmem, out_shape),
         scratch_shapes=list(scratch),
         compiler_params=pltpu.CompilerParams(vmem_limit_bytes=56 * 1024 * 1024),
@@ -301,12 +315,18 @@
         pltpu.VMEM((ALL, 2 * NG), BF16),
         pltpu.VMEM((4 * NG, ALL), BF16),
         pltpu.VMEM((8 * WIN, ALL), BF16),
+        pltpu.VMEM((8 * WIN, ALL), BF16),
         pltpu.VMEM((8, 2 * WIN, 2 * NG), F32),
         pltpu.VMEM((4, 8, WIN, 2 * NG), BF16),
         pltpu.VMEM((RING, 16, NG), F32),
+        pltpu.VMEM((GROUP, 4 * NG, NG), BF16),
+        pltpu.SemaphoreType.DMA((GROUP,)),
     )
     inputs = (me, recv, *potentials, stack, wide, xa, xh, fh, fl, lane_order())
-    return vmem_call(plane_kernel, shape, inputs, scratch, 1)
+    whole = pl.BlockSpec(memory_space=pltpu.VMEM)
+    specs = [pl.BlockSpec(memory_space=pltpu.SMEM), whole] + [pl.BlockSpec(memory_space=pl.ANY)] * GROUP
+    specs += [whole] * (len(inputs) - 2 - GROUP)
+    return vmem_call(plane_kernel, shape, inputs, scratch, specs)
 
 
 def finish(recv, part, copies):
@@ -325,8 +345,12 @@
     return value[:, :, :half] + jnp.roll(value[:, :, half:], NG // 2, axis=3)
 
 
-def pairing(bands, vectors, labels):
-    full = jnp.einsum("snprl," + labels + "->npgbq", bands, vectors, preferred_element_type=F32)
+def pairing(bands, vectors, axis):
+    full = 0.0
+    for src, left in enumerate(bands):
+        right = lax.index_in_dim(vectors, src, axis, False)
+        full += jnp.einsum("rkl,gbqrl->kgbq", left, right, preferred_element_type=F32)
+    full = full.reshape(-1, 2, *full.shape[1:])
     real = full[:, 0, :, :, 0] + full[:, 1, :, :, 1]
     imag = full[:, 0, :, :, 1] - full[:, 1, :, :, 0]
     return jnp.stack([real, imag])
@@ -337,10 +361,10 @@
 
 
 def place(pieces, me):
-    result = jnp.zeros((GROUP, *pieces[0].shape), pieces[0].dtype)
-    for turn, piece in enumerate(pieces):
-        result = lax.dynamic_update_index_in_dim(result, piece, jnp.bitwise_xor(me, turn), 0)
-    return result
+    for bit in (1, 2):
+        odd = jnp.bitwise_and(me, bit) != 0
+        pieces = [jnp.where(odd, pieces[i ^ bit], pieces[i]) for i in range(GROUP)]
+    return pieces
 
 
 def exchange(value, axis, groups=None):
@@ -349,6 +373,12 @@
 
 def to_all(value, axis, count, groups=None):
     return exchange(jnp.broadcast_to(value[None], (count, *value.shape)), axis, groups)
+
+
+def two_steps(value, outer, inner):
+    value = value.reshape(GROUP, GROUP, *value.shape[1:])
+    value = jnp.swapaxes(exchange(value, "pw", outer), 0, 1)
+    return exchange(value, "pw", inner).reshape(RING, *value.shape[2:])
 
 
 def per_device(block, bands, potential, stick_cells, sphere_mask):
@@ -357,7 +387,8 @@
     me = jnp.bitwise_and(lax.axis_index("pw"), GROUP - 1)
     own, sticks, rows = block.shape[0], block.shape[2], bands.shape[0]
     fours = [[i * GROUP + j for j in range(GROUP)] for i in range(size // GROUP)]
-    rings = [[i * GROUP + j for i in range(size // GROUP)] for j in range(GROUP)]
+    far = [[i * 16 + j for i in range(GROUP)] for j in range(16)]
+    near = [[k * 16 + i * GROUP + j for i in range(GROUP)] for k in range(GROUP) for j in range(GROUP)]
 
     inside = sphere_mask.astype(BF16)[None, None]
     masked = block * inside
@@ -367,33 +398,31 @@
     column = jnp.broadcast_to(column.astype(BF16)[None, None], (GROUP, 1, sticks, NG))
     part = exchange(jnp.concatenate([grouped, column], axis=1), "pw", fours)
     sent = spread(part)
-    recv = exchange(sent, "pw", rings)
-
-    bands_rows = pack(bands * inside).reshape(-1, NG)
+    recv = two_steps(sent, far, near)
+
+    bands_rows = jnp.transpose(pack(bands * inside), (2, 0, 1, 3)).reshape(-1, NG)
     v_high = lax.reduce_precision(potential, 8, 7)
     v_low = (potential - v_high).astype(BF16)
     potential_rows = jnp.stack([v_high.astype(BF16), v_low]).reshape(-1, NG)
-    side = jnp.concatenate([bands_rows, potential_rows], axis=0)
+    side = jnp.concatenate([potential_rows, bands_rows], axis=0)
     sides = [side] + [partner(side, turn, size) for turn in range(1, GROUP)]
-    split_at = bands_rows.shape[0]
-    bands_all = place([piece[:split_at] for piece in sides], me).reshape(GROUP, rows, 2, sticks // 2, NG)
-    potentials = [piece[split_at:].reshape(2, potential.shape[0], NG, NG) for piece in sides]
+    bands_all = place([piece[potential_rows.shape[0] :] for piece in sides], me)
+    bands_all = [piece.reshape(sticks // 2, 2 * rows, NG) for piece in bands_all]
     vectors = part[:, : 2 * BANDS].reshape(GROUP * BANDS, 2, sticks, NG)
     masked_all = lax.all_gather(jnp.stack([vectors, vectors]), "band", axis=1, tiled=True)[0]
     masked_all = pack(masked_all.reshape(teams * GROUP * BANDS, 2, sticks, NG))
     masked_all = masked_all.reshape(teams, GROUP, BANDS, 2, sticks // 2, NG)
 
-    back = exchange(planes(me.reshape(1), recv, potentials), "pw", rings)
+    back = two_steps(planes(me.reshape(1), recv, sides), near, far)
     result, copies = finish(back, part, teams)
     applied_all = exchange(copies, "band").reshape(teams, BANDS, 2, GROUP, sticks // 2, NG)
     pieces = [lax.dynamic_index_in_dim(result, jnp.bitwise_xor(me, turn), 0, False) for turn in range(GROUP)]
     pieces = pieces[:1] + [partner(pieces[turn], turn, size) for turn in range(1, GROUP)]
-    applied = place(pieces, me).reshape(own, 2, sticks, NG)
-
-    terms = jnp.stack(
-        [pairing(bands_all, masked_all, "gsbqrl"), pairing(bands_all, applied_all, "gbqsrl")]
-    )
-    total = jnp.sum(to_all(terms.reshape(-1, NG), "pw", size // GROUP, rings), axis=0)
+    applied = jnp.stack(place(pieces, me)).reshape(own, 2, sticks, NG)
+
+    terms = jnp.stack([pairing(bands_all, masked_all, 1), pairing(bands_all, applied_all, 3)])
+    total = jnp.sum(to_all(terms.reshape(-1, NG), "pw", GROUP, near), axis=0)
+    total = jnp.sum(to_all(total, "pw", GROUP, far), axis=0)
     total = to_all(total, "pw", GROUP, fours).reshape(GROUP, 2, 2, rows, teams, BANDS)
     total = jnp.transpose(total, (1, 2, 3, 4, 0, 5)).reshape(2, 2, rows, teams * own)
     return (applied, total[0], total[1])

time: 234 us -> 221 us (0.944); the launches traced: 230 us -> 220 us
  local copies, waits for them, and re-layouts: 91.9 us -> 10.4 us
  waiting for transfers between devices: 16.2 us -> 60.9 us
  blocking collectives: 14 us -> 43.7 us
  starting transfers between devices: 60.6 us -> 57.9 us
    dynamic_update_slice x7 -> x0, local copies, waits for them, and re-layouts: 63.6 us -> none  [place(): lax.dynamic_update_index_in_dim(result, piece, jnp.bitwise_xor(me, turn), 0)]
    all_to_all x1 -> x3, blocking collectives: 14 us -> 43.7 us  [exchange(): lax.all_to_all(value, axis, 0, 0, axis_index_groups=groups, tiled=True)]
    all_to_all x5 -> x6, waiting for transfers between devices: 11.3 us -> 36.2 us  [exchange(): lax.all_to_all(value, axis, 0, 0, axis_index_groups=groups, tiled=True)]
    ppermute x6, waiting for transfers between devices: 4.82 us -> 24.7 us  [partner(): return lax.ppermute(value, 'pw', [(i, i ^ turn) for i in range(size)])]
    broadcast_in_dim x9 -> x0, local copies, waits for them, and re-layouts: 17 us -> none  [the longest x7 16.6 us: place(): lax.dynamic_update_index_in_dim(result, piece, jnp.bitwise_xor(me, turn), 0)]
    slice x3 -> x1, local copies, waits for them, and re-layouts: 2.95 us -> 0.45 us  [pairing(): right = lax.index_in_dim(vectors, src, axis, False)]
    all_to_all x5 -> x6, starting transfers between devices: 40.1 us -> 37.9 us  [exchange(): lax.all_to_all(value, axis, 0, 0, axis_index_groups=groups, tiled=True)]
  transfers between devices with their start and end apart: 12 -> 13, of which waited for: 4 -> 6; matrix products, arithmetic and copies ran while one was open for 40% -> 3% of each run, Pallas kernels for 11% -> 11%
where the time goes in v3:
time: 221 us; the launch traced here: 220 us
  waiting for transfers between devices  60.9 us (28%)
  starting transfers between devices  57.9 us (26%)
  blocking collectives  43.7 us (20%)
  Pallas kernels  25.2 us (11%)
  between operations  14.4 us (7%)
  local copies, waits for them, and re-layouts  10.4 us (5%)
  other arithmetic  6.1 us (3%)
    all_to_all x3, blocking collectives, exchange(): lax.all_to_all(value, axis, 0, 0, axis_index_groups=groups, tiled=True)  43.7 us
    all_to_all x6, starting transfers between devices, exchange(): lax.all_to_all(value, axis, 0, 0, axis_index_groups=groups, tiled=True)  37.9 us
    all_to_all x6, waiting for transfers between devices, exchange(): lax.all_to_all(value, axis, 0, 0, axis_index_groups=groups, tiled=True)  36.2 us
    pallas_call x3, Pallas kernels, vmem_call(): pl.pallas_call(kernel, out_shape=out_shape, in_specs=specs or [vmem] * le...  25.2 us
    ppermute x6, waiting for transfers between devices, partner(): return lax.ppermute(value, 'pw', [(i, i ^ turn) for i in range(size)])  24.7 us
    ppermute x6, starting transfers between devices, partner(): return lax.ppermute(value, 'pw', [(i, i ^ turn) for i in range(size)])  20 us
  transfers between devices with their start and end apart: 13, of which 6 were waited for; matrix products, arithmetic and copies ran while one was open for 3% of the time, Pallas kernels for 11%

profile of v3, /device:TPU:1, one launch (start us, length us, event | category | flops | bytes accessed | tf_op | source)
XLA Modules:
  0.0 220.3 jit_solution(14563185441295296368)
XLA Ops:
  7.2 0.7 and_select_fusion.1
  7.9 0.7 convert_element_type.16
  8.6 1.0 broadcast_multiply_fusion.1
  9.7 13.9 %all_to_all.45.part_ref = bf16[4,5,40,128]{3,2,1,0:T(8,128)(2,1)S(1)} all-to-all(bf16[4,5,40,128]{3,2,1,0:T(8,128)(2,1)S(1)} %pad_maximum_fusion.2), channel_id=1, replica_groups={{0,1,2,3},{4,5,6,7},{8,9,10,11},{12,13,14,15},{16,17,18,19},{20,21,22,2..., dimensions={0} | all-to-all | bytes 409600 | tf_op jit(solution)/shard_map/all_to_all | solution.py:371
  23.7 0.7 pad_maximum_fusion.1
  24.5 0.3 fusion.13
  24.9 2.2 %shard_map.175 = s16[16,48,128]{2,1,0:T(8,128)(2,1)} custom-call(bf16[4,5,40,128]{3,2,1,0:T(8,128)(2,1)} %copy-done, bf16[256,256]{1,0:T(8,128)(2,1)} %constant.71.clone.high_ref, bf16[256,256]{1,0:T(8,128)(2,1)} %constant.72.clone.low_ref), custom_call_target="tpu_custom_call" | custom-call | tf_op jit(solution)/shard_map/pallas_call | solution.py:289
  27.1 9.8 %all-to-all-start.1 = ((s16[4,4,48,128]{3,2,1,0:T(8,128)(2,1)}), s16[4,4,48,128]{3,2,1,0:T(8,128)(2,1)S(1)}, u32[]{:S(2)}, u32[]{:S(2)}) async-start(s16[4,4,48,128]{3,2,1,0:T(8,128)(2,1)} %bitcast.180), calls=%async_computation.1 | async-start | bytes 393216 | tf_op jit(solution)/shard_map/all_to_all | solution.py:371
  37.2 0.3 copy.112
  37.5 12.0 %all-to-all-done.1 = s16[4,4,48,128]{3,2,1,0:T(8,128)(2,1)S(1)} async-done(((s16[4,4,48,128]{3,2,1,0:T(8,128)(2,1)}), s16[4,4,48,128]{3,2,1,0:T(8,128)(2,1)S(1)}, u32[]{:S(2)}, u32[]{:S(2)}) %all-to-all-start.1) | async-done | bytes 196640 | tf_op jit(solution)/shard_map/all_to_all | solution.py:371
  49.6 0.7 copy.111
  50.3 6.5 %all-to-all-start.2 = ((s16[4,4,48,128]{3,2,1,0:T(8,128)(2,1)}), s16[4,4,48,128]{3,2,1,0:T(8,128)(2,1)S(1)}, u32[]{:S(2)}, u32[]{:S(2)}) async-start(s16[4,4,48,128]{3,2,1,0:T(8,128)(2,1)} %copy.111), calls=%async_computation.2 | async-start | bytes 393216 | tf_op jit(solution)/shard_map/all_to_all | solution.py:371
  56.8 5.0 %collective-permute-start.2 = (bf16[1792,128]{1,0:T(8,128)(2,1)S(1)}, bf16[1792,128]{1,0:T(8,128)(2,1)S(1)}, u32[]{:S(2)}, u32[]{:S(2)}) collective-permute-start(bf16[1792,128]{1,0:T(8,128)(2,1)S(1)} %pad_maximum_fusion.v0_ref), channel_id=1, source_target_pairs={{0,3},{1,2},{2,1},{3,0},{4,7},{5,6},{6,5},{7,4},{8,11},{9,10},{10,... | collective-permute-start | bytes 1376264 | tf_op jit(solution)/shard_map/ppermute | solution.py:360
  61.8 3.1 %collective-permute-start.1 = (bf16[1792,128]{1,0:T(8,128)(2,1)S(1)}, bf16[1792,128]{1,0:T(8,128)(2,1)S(1)}, u32[]{:S(2)}, u32[]{:S(2)}) collective-permute-start(bf16[1792,128]{1,0:T(8,128)(2,1)S(1)} %pad_maximum_fusion.v0_ref), channel_id=1, source_target_pairs={{0,2},{1,3},{2,0},{3,1},{4,6},{5,7},{6,4},{7,5},{8,10},{9,11},{10,... | collective-permute-start | bytes 1376264 | tf_op jit(solution)/shard_map/ppermute | solution.py:360
  64.9 1.9 collective-permute-start
  66.9 5.4 %collective-permute-done.2.v3_ref = bf16[1792,128]{1,0:T(8,128)(2,1)S(1)} collective-permute-done((bf16[1792,128]{1,0:T(8,128)(2,1)S(1)}, bf16[1792,128]{1,0:T(8,128)(2,1)S(1)}, u32[]{:S(2)}, u32[]{:S(2)}) %collective-permute-start.2) | collective-permute-done | bytes 458784 | tf_op jit(solution)/shard_map/ppermute | solution.py:360
  72.3 19.3 %collective-permute-done.1.v2_ref = bf16[1792,128]{1,0:T(8,128)(2,1)S(1)} collective-permute-done((bf16[1792,128]{1,0:T(8,128)(2,1)S(1)}, bf16[1792,128]{1,0:T(8,128)(2,1)S(1)}, u32[]{:S(2)}, u32[]{:S(2)}) %collective-permute-start.1) | collective-permute-done | bytes 458784 | tf_op jit(solution)/shard_map/ppermute | solution.py:360
  91.6 0.7 copy-done.4
  92.5 20.2 %shard_map.176 = s16[16,48,128]{2,1,0:T(8,128)(2,1)} custom-call(s32[1]{0:T(128)} %bitcast.me_ref, s16[16,48,128]{2,1,0:T(8,128)(2,1)} %bitcast.176, bf16[1792,128]{1,0:T(8,128)(2,1)} %copy-done.1, bf16[1792,128]{1,0:T(8,128)(2,1)} %copy-done.6, bf16[1792,128]{1,0:T(8,128)(2,1)} %copy-done.4, bf16[1792,128]{1,0:T(8,128)(2,1)} %copy-done.2, ...), custom_call_target="tpu_custom_call" | custom-call | tf_op jit(solution)/shard_map/pallas_call | solution.py:289
  112.8 13.1 %all_to_all.46 = s16[4,4,48,128]{3,2,1,0:T(8,128)(2,1)S(1)} all-to-all(s16[4,4,48,128]{3,2,1,0:T(8,128)(2,1)} %bitcast.177), channel_id=1, replica_groups={{0,4,8,12},{1,5,9,13},{2,6,10,14},{3,7,11,15},{16,20,24,28},{17,21,25,2..., dimensions={0} | all-to-all | bytes 393216 | tf_op jit(solution)/shard_map/all_to_all | solution.py:371
  125.9 16.7 %all_to_all.47 = s16[4,4,48,128]{3,2,1,0:T(8,128)(2,1)} all-to-all(s16[4,4,48,128]{3,2,1,0:T(8,128)(2,1)S(1)} %copy.113), channel_id=1, replica_groups={{0,16,32,48},{1,17,33,49},{2,18,34,50},{3,19,35,51},{4,20,36,52},{5,21,..., dimensions={0} | all-to-all | bytes 393216 | tf_op jit(solution)/shard_map/all_to_all | solution.py:371
  142.6 2.7 %shard_map.177 = (bf16[4,4,40,128]{3,2,1,0:T(8,128)(2,1)}, bf16[8,320,128]{2,1,0:T(8,128)(2,1)}) custom-call(s16[16,48,128]{2,1,0:T(8,128)(2,1)} %bitcast.181, bf16[4,5,40,128]{3,2,1,0:T(8,128)(2,1)} %copy-done, bf16[256,256]{1,0:T(8,128)(2,1)} %constant.71.clone.high_ref, bf16[256,256]{1,0:T(8,128)(2,1)} %constant.72.clone.low_ref), custom_call_target="tpu_custom_call" | custom-call | tf_op jit(solution)/shard_map/pallas_call | solution.py:289
  145.3 8.5 %all-to-all-start.5 = ((bf16[8,320,128]{2,1,0:T(8,128)(2,1)}), bf16[8,320,128]{2,1,0:T(8,128)(2,1)S(1)}, u32[]{:S(2)}, u32[]{:S(2)}) async-start(bf16[8,320,128]{2,1,0:T(8,128)(2,1)} %get-tuple-element.6), calls=%async_computation.5 | async-start | bytes 1310720 | tf_op jit(solution)/shard_map/all_to_all | solution.py:371
  153.9 1.1 broadcast_select_fusion.4
  155.0 10.2 %all-to-all-done.5 = bf16[8,320,128]{2,1,0:T(8,128)(2,1)S(1)} async-done(((bf16[8,320,128]{2,1,0:T(8,128)(2,1)}), bf16[8,320,128]{2,1,0:T(8,128)(2,1)S(1)}, u32[]{:S(2)}, u32[]{:S(2)}) %all-to-all-start.5) | async-done | bytes 655392 | tf_op jit(solution)/shard_map/all_to_all | solution.py:371
  165.2 0.4 copy.123
  166.8 1.4 slice_bitcast_fusion
  168.3 0.3 fusion.10
  168.6 0.5 slice_add_fusion
  169.0 0.5 fusion.12
  170.7 0.3 copy.131
  171.3 0.6 broadcast_in_dim.72
  171.9 4.4 %all-to-all-start.6 = ((f32[4,16,128]{2,1,0:T(8,128)}), f32[4,16,128]{2,1,0:T(8,128)S(1)}, u32[]{:S(2)}, u32[]{:S(2)}) async-start(f32[4,16,128]{2,1,0:T(8,128)} %broadcast_in_dim.72), calls=%async_computation.6 | async-start | bytes 65536 | tf_op jit(solution)/shard_map/all_to_all | solution.py:371
  176.4 4.5 %collective-permute-start.5 = (bf16[4,40,128]{2,1,0:T(8,128)(2,1)S(1)}, bf16[4,40,128]{2,1,0:T(8,128)(2,1)S(1)}, u32[]{:S(2)}, u32[]{:S(2)}) collective-permute-start(bf16[4,40,128]{2,1,0:T(8,128)(2,1)S(1)} %get-tuple-element.37), channel_id=1, source_target_pairs={{0,1},{1,0},{2,3},{3,2},{4,5},{5,4},{6,7},{7,6},{8,9},{9,8},{10,11... | collective-permute-start | bytes 122888 | tf_op jit(solution)/shard_map/ppermute | solution.py:360
  180.9 1.9 collective-permute-start.4
  182.8 3.5 %collective-permute-start.3 = (bf16[4,40,128]{2,1,0:T(8,128)(2,1)S(1)}, bf16[4,40,128]{2,1,0:T(8,128)(2,1)S(1)}, u32[]{:S(2)}, u32[]{:S(2)}) collective-permute-start(bf16[4,40,128]{2,1,0:T(8,128)(2,1)S(1)} %get-tuple-element.39), channel_id=1, source_target_pairs={{0,3},{1,2},{2,1},{3,0},{4,7},{5,6},{6,5},{7,4},{8,11},{9,10},{10,... | collective-permute-start | bytes 122888 | tf_op jit(solution)/shard_map/ppermute | solution.py:360
  186.4 0.6 broadcast_in_dim.73
  187.0 3.6 %all-to-all-start.7 = ((f32[4,16,128]{2,1,0:T(8,128)}), f32[4,16,128]{2,1,0:T(8,128)S(1)}, u32[]{:S(2)}, u32[]{:S(2)}) async-start(f32[4,16,128]{2,1,0:T(8,128)} %broadcast_in_dim.73), calls=%async_computation.7 | async-start | bytes 65536 | tf_op jit(solution)/shard_map/all_to_all | solution.py:371
  190.7 11.5 %all-to-all-done.7 = f32[4,16,128]{2,1,0:T(8,128)S(1)} async-done(((f32[4,16,128]{2,1,0:T(8,128)}), f32[4,16,128]{2,1,0:T(8,128)S(1)}, u32[]{:S(2)}, u32[]{:S(2)}) %all-to-all-start.7) | async-done | bytes 32800 | tf_op jit(solution)/shard_map/all_to_all | solution.py:371
  202.1 0.6 broadcast_in_dim.74
  202.7 5.0 %all-to-all-start.8 = ((f32[4,16,128]{2,1,0:T(8,128)}), f32[4,16,128]{2,1,0:T(8,128)S(1)}, u32[]{:S(2)}, u32[]{:S(2)}) async-start(f32[4,16,128]{2,1,0:T(8,128)} %broadcast_in_dim.74), calls=%async_computation.8 | async-start | bytes 65536 | tf_op jit(solution)/shard_map/all_to_all | solution.py:371
  207.8 0.7 pad_maximum_fusion.3
  208.5 2.5 %all-to-all-done.8 = f32[4,16,128]{2,1,0:T(8,128)S(1)} async-done(((f32[4,16,128]{2,1,0:T(8,128)}), f32[4,16,128]{2,1,0:T(8,128)S(1)}, u32[]{:S(2)}, u32[]{:S(2)}) %all-to-all-start.8) | async-done | bytes 32800 | tf_op jit(solution)/shard_map/all_to_all | solution.py:371
  210.9 0.4 copy.132
  211.4 0.3 copy.134
  211.7 0.7 copy.136
  212.4 0.3 copy.133
  212.8 0.7 copy.135
  (67 shorter events, 3.6 us)
Async XLA Ops:
  7.2 159.7 %all-gather.2.cloned.1.call-start = ((), (), s32[]{:S(2)}) async-start(), calls=%async_computation.9 | async-start | bytes 2949120 | tf_op jit(solution)/shard_map/all_gather | solution.py:412
  8.6 15.8 %copy-start.8 = (bf16[32,2,40,128]{3,2,1,0:T(8,128)(2,1)S(1)}, bf16[32,2,40,128]{3,2,1,0:T(8,128)(2,1)}, u32[]{:S(2)}) copy-start(bf16[32,2,40,128]{3,2,1,0:T(8,128)(2,1)} %param.17) | copy-start | bytes 1966084
  23.6 0.9 copy-start
  27.1 10.4 %copy-start.10 = (f32[2,128,128]{2,1,0:T(8,128)S(1)}, f32[2,128,128]{2,1,0:T(8,128)}, u32[]{:S(2)}) copy-start(f32[2,128,128]{2,1,0:T(8,128)} %param.18) | copy-start | bytes 393220
  27.1 22.5 %all-to-all-start.1 = ((s16[4,4,48,128]{3,2,1,0:T(8,128)(2,1)}), s16[4,4,48,128]{3,2,1,0:T(8,128)(2,1)S(1)}, u32[]{:S(2)}, u32[]{:S(2)}) async-start(s16[4,4,48,128]{3,2,1,0:T(8,128)(2,1)} %bitcast.180), calls=%async_computation.1 | async-start | bytes 393216 | tf_op jit(solution)/shard_map/all_to_all | solution.py:371
  50.3 41.3 %all-to-all-start.2 = ((s16[4,4,48,128]{3,2,1,0:T(8,128)(2,1)}), s16[4,4,48,128]{3,2,1,0:T(8,128)(2,1)S(1)}, u32[]{:S(2)}, u32[]{:S(2)}) async-start(s16[4,4,48,128]{3,2,1,0:T(8,128)(2,1)} %copy.111), calls=%async_computation.2 | async-start | bytes 393216 | tf_op jit(solution)/shard_map/all_to_all | solution.py:371
  56.8 34.7 %copy-start.1 = (bf16[1792,128]{1,0:T(8,128)(2,1)}, bf16[1792,128]{1,0:T(8,128)(2,1)S(1)}, u32[]{:S(2)}) copy-start(bf16[1792,128]{1,0:T(8,128)(2,1)S(1)} %pad_maximum_fusion.v0_ref) | copy-start | bytes 1376260
  56.8 15.4 %collective-permute-start.2 = (bf16[1792,128]{1,0:T(8,128)(2,1)S(1)}, bf16[1792,128]{1,0:T(8,128)(2,1)S(1)}, u32[]{:S(2)}, u32[]{:S(2)}) collective-permute-start(bf16[1792,128]{1,0:T(8,128)(2,1)S(1)} %pad_maximum_fusion.v0_ref), channel_id=1, source_target_pairs={{0,3},{1,2},{2,1},{3,0},{4,7},{5,6},{6,5},{7,4},{8,11},{9,10},{10,... | collective-permute-start | bytes 1376264 | tf_op jit(solution)/shard_map/ppermute | solution.py:360
  61.8 29.7 %collective-permute-start.1 = (bf16[1792,128]{1,0:T(8,128)(2,1)S(1)}, bf16[1792,128]{1,0:T(8,128)(2,1)S(1)}, u32[]{:S(2)}, u32[]{:S(2)}) collective-permute-start(bf16[1792,128]{1,0:T(8,128)(2,1)S(1)} %pad_maximum_fusion.v0_ref), channel_id=1, source_target_pairs={{0,2},{1,3},{2,0},{3,1},{4,6},{5,7},{6,4},{7,5},{8,10},{9,11},{10,... | collective-permute-start | bytes 1376264 | tf_op jit(solution)/shard_map/ppermute | solution.py:360
  64.9 26.6 %collective-permute-start = (bf16[1792,128]{1,0:T(8,128)(2,1)S(1)}, bf16[1792,128]{1,0:T(8,128)(2,1)S(1)}, u32[]{:S(2)}, u32[]{:S(2)}) collective-permute-start(bf16[1792,128]{1,0:T(8,128)(2,1)S(1)} %pad_maximum_fusion.v0_ref), channel_id=1, source_target_pairs={{0,1},{1,0},{2,3},{3,2},{4,5},{5,4},{6,7},{7,6},{8,9},{9,8},{10,11... | collective-permute-start | bytes 1376264 | tf_op jit(solution)/shard_map/ppermute | solution.py:360
  72.3 19.3 %copy-start.2 = (bf16[1792,128]{1,0:T(8,128)(2,1)}, bf16[1792,128]{1,0:T(8,128)(2,1)S(1)}, u32[]{:S(2)}) copy-start(bf16[1792,128]{1,0:T(8,128)(2,1)S(1)} %collective-permute-done.2.v3_ref) | copy-start | bytes 1376260
  91.5 0.8 copy-start.4
  91.5 0.9 copy-start.6
  91.6 1.0 copy-start.7
  125.9 28.0 %copy-start.3 = (bf16[1792,128]{1,0:T(8,128)(2,1)S(1)}, bf16[1792,128]{1,0:T(8,128)(2,1)}, u32[]{:S(2)}) copy-start(bf16[1792,128]{1,0:T(8,128)(2,1)} %copy-done.2) | copy-start | bytes 1376260
  125.9 28.0 %copy-start.5 = (bf16[1792,128]{1,0:T(8,128)(2,1)S(1)}, bf16[1792,128]{1,0:T(8,128)(2,1)}, u32[]{:S(2)}) copy-start(bf16[1792,128]{1,0:T(8,128)(2,1)} %copy-done.4) | copy-start | bytes 1376260
  145.3 19.9 %all-to-all-start.5 = ((bf16[8,320,128]{2,1,0:T(8,128)(2,1)}), bf16[8,320,128]{2,1,0:T(8,128)(2,1)S(1)}, u32[]{:S(2)}, u32[]{:S(2)}) async-start(bf16[8,320,128]{2,1,0:T(8,128)(2,1)} %get-tuple-element.6), calls=%async_computation.5 | async-start | bytes 1310720 | tf_op jit(solution)/shard_map/all_to_all | solution.py:371
  169.9 6.4 %copy-start.9 = (bf16[4,4,40,128]{3,2,1,0:T(8,128)(2,1)S(1)}, bf16[4,4,40,128]{3,2,1,0:T(8,128)(2,1)}, u32[]{:S(2)}) copy-start(bf16[4,4,40,128]{3,2,1,0:T(8,128)(2,1)} %get-tuple-element.5) | copy-start | bytes 491524
  171.9 14.4 %all-to-all-start.6 = ((f32[4,16,128]{2,1,0:T(8,128)}), f32[4,16,128]{2,1,0:T(8,128)S(1)}, u32[]{:S(2)}, u32[]{:S(2)}) async-start(f32[4,16,128]{2,1,0:T(8,128)} %broadcast_in_dim.72), calls=%async_computation.6 | async-start | bytes 65536 | tf_op jit(solution)/shard_map/all_to_all | solution.py:371
  176.4 14.2 %collective-permute-start.5 = (bf16[4,40,128]{2,1,0:T(8,128)(2,1)S(1)}, bf16[4,40,128]{2,1,0:T(8,128)(2,1)S(1)}, u32[]{:S(2)}, u32[]{:S(2)}) collective-permute-start(bf16[4,40,128]{2,1,0:T(8,128)(2,1)S(1)} %get-tuple-element.37), channel_id=1, source_target_pairs={{0,1},{1,0},{2,3},{3,2},{4,5},{5,4},{6,7},{7,6},{8,9},{9,8},{10,11... | collective-permute-start | bytes 122888 | tf_op jit(solution)/shard_map/ppermute | solution.py:360
  180.9 9.8 %collective-permute-start.4 = (bf16[4,40,128]{2,1,0:T(8,128)(2,1)S(1)}, bf16[4,40,128]{2,1,0:T(8,128)(2,1)S(1)}, u32[]{:S(2)}, u32[]{:S(2)}) collective-permute-start(bf16[4,40,128]{2,1,0:T(8,128)(2,1)S(1)} %get-tuple-element.38), channel_id=1, source_target_pairs={{0,2},{1,3},{2,0},{3,1},{4,6},{5,7},{6,4},{7,5},{8,10},{9,11},{10,... | collective-permute-start | bytes 122888 | tf_op jit(solution)/shard_map/ppermute | solution.py:360
  182.8 7.8 %collective-permute-start.3 = (bf16[4,40,128]{2,1,0:T(8,128)(2,1)S(1)}, bf16[4,40,128]{2,1,0:T(8,128)(2,1)S(1)}, u32[]{:S(2)}, u32[]{:S(2)}) collective-permute-start(bf16[4,40,128]{2,1,0:T(8,128)(2,1)S(1)} %get-tuple-element.39), channel_id=1, source_target_pairs={{0,3},{1,2},{2,1},{3,0},{4,7},{5,6},{6,5},{7,4},{8,11},{9,10},{10,... | collective-permute-start | bytes 122888 | tf_op jit(solution)/shard_map/ppermute | solution.py:360
  187.0 15.1 %all-to-all-start.7 = ((f32[4,16,128]{2,1,0:T(8,128)}), f32[4,16,128]{2,1,0:T(8,128)S(1)}, u32[]{:S(2)}, u32[]{:S(2)}) async-start(f32[4,16,128]{2,1,0:T(8,128)} %broadcast_in_dim.73), calls=%async_computation.7 | async-start | bytes 65536 | tf_op jit(solution)/shard_map/all_to_all | solution.py:371
  202.7 8.2 %all-to-all-start.8 = ((f32[4,16,128]{2,1,0:T(8,128)}), f32[4,16,128]{2,1,0:T(8,128)S(1)}, u32[]{:S(2)}, u32[]{:S(2)}) async-start(f32[4,16,128]{2,1,0:T(8,128)} %broadcast_in_dim.74), calls=%async_computation.8 | async-start | bytes 65536 | tf_op jit(solution)/shard_map/all_to_all | solution.py:371
Sparse Core Ops, SparseCore 0:
  24.6 82.1 all-gather.1

commit v4 on v3

--- a/solution.py
+++ b/solution.py
@@ -130,11 +130,11 @@
 
 
 def plane_kernel(
-    me_ref, recv_ref, v0_ref, v1_ref, v2_ref, v3_ref, stack_ref, wide_ref, xa_ref, xh_ref, fh_ref, fl_ref, order_ref,
-    out_ref, val_ref, low_ref, cell_ref, onehot_ref, tall_ref, flat_ref, left_a_ref, left_b_ref, mid_ref, lift_ref, tail_ref, v_ref, v_sem,
+    me_ref, recv_ref, v0_ref, v1_ref, v2_ref, v3_ref, stack_ref, wide_ref, xa_ref, xh_ref, fh_ref, fl_ref, order_ref, rows_ref,
+    out_ref, same_rows_ref, val_ref, low_ref, cell_ref, onehot_ref, tall_ref, flat_ref, left_a_ref, left_b_ref, mid_ref, lift_ref, tail_ref, v_ref, v_sem,
 ):
     copies = [
-        pltpu.make_async_copy(source.at[pl.ds(0, 4 * NG), :], v_ref.at[turn], v_sem.at[turn])
+        pltpu.make_async_copy(source, v_ref.at[turn], v_sem.at[turn])
         for turn, source in enumerate((v0_ref, v1_ref, v2_ref, v3_ref))
     ]
     for copy in copies:
@@ -284,13 +284,14 @@
         copies_ref[copy] = packed
 
 
-def vmem_call(kernel, out_shape, inputs, scratch=(), specs=None):
+def vmem_call(kernel, out_shape, inputs, scratch=(), specs=None, outs=None, aliases=None):
     vmem = pl.BlockSpec(memory_space=pltpu.VMEM)
     return pl.pallas_call(
         kernel,
         out_shape=out_shape,
         in_specs=specs or [vmem] * len(inputs),
-        out_specs=jax.tree.map(lambda _: vmem, out_shape),
+        out_specs=outs or jax.tree.map(lambda _: vmem, out_shape),
+        input_output_aliases=aliases or {},
         scratch_shapes=list(scratch),
         compiler_params=pltpu.CompilerParams(vmem_limit_bytes=56 * 1024 * 1024),
     )(*inputs)
@@ -302,11 +303,11 @@
     return vmem_call(spread_kernel, shape, (part, high, low))
 
 
-def planes(me, recv, potentials):
+def planes(me, recv, potentials, rows):
     stack, wide = across_tables()
     (xh, xl), (fh, fl) = down_tables()
     xa = np.concatenate([xh, xl], axis=1)
-    shape = jax.ShapeDtypeStruct((RING, ROWS, NG), jnp.int16)
+    shape = (jax.ShapeDtypeStruct((RING, ROWS, NG), jnp.int16), jax.ShapeDtypeStruct(rows.shape, rows.dtype))
     scratch = (
         pltpu.VMEM((32, ALL), F32),
         pltpu.VMEM((32, ALL), F32),
@@ -322,11 +323,12 @@
         pltpu.VMEM((GROUP, 4 * NG, NG), BF16),
         pltpu.SemaphoreType.DMA((GROUP,)),
     )
-    inputs = (me, recv, *potentials, stack, wide, xa, xh, fh, fl, lane_order())
+    inputs = (me, recv, *potentials, stack, wide, xa, xh, fh, fl, lane_order(), rows)
     whole = pl.BlockSpec(memory_space=pltpu.VMEM)
     specs = [pl.BlockSpec(memory_space=pltpu.SMEM), whole] + [pl.BlockSpec(memory_space=pl.ANY)] * GROUP
-    specs += [whole] * (len(inputs) - 2 - GROUP)
-    return vmem_call(plane_kernel, shape, inputs, scratch, specs)
+    specs += [whole] * (len(inputs) - 3 - GROUP) + [pl.BlockSpec(memory_space=pl.ANY)]
+    outs = (whole, pl.BlockSpec(memory_space=pl.ANY))
+    return vmem_call(plane_kernel, shape, inputs, scratch, specs, outs, {len(inputs) - 1: 1})
 
 
 def finish(recv, part, copies):
@@ -375,20 +377,13 @@
     return exchange(jnp.broadcast_to(value[None], (count, *value.shape)), axis, groups)
 
 
-def two_steps(value, outer, inner):
-    value = value.reshape(GROUP, GROUP, *value.shape[1:])
-    value = jnp.swapaxes(exchange(value, "pw", outer), 0, 1)
-    return exchange(value, "pw", inner).reshape(RING, *value.shape[2:])
-
-
 def per_device(block, bands, potential, stick_cells, sphere_mask):
     size = lax.axis_size("pw")
     teams = lax.axis_size("band")
     me = jnp.bitwise_and(lax.axis_index("pw"), GROUP - 1)
     own, sticks, rows = block.shape[0], block.shape[2], bands.shape[0]
     fours = [[i * GROUP + j for j in range(GROUP)] for i in range(size // GROUP)]
-    far = [[i * 16 + j for i in range(GROUP)] for j in range(16)]
-    near = [[k * 16 + i * GROUP + j for i in range(GROUP)] for k in range(GROUP) for j in range(GROUP)]
+    rings = [[i * GROUP + j for i in range(size // GROUP)] for j in range(GROUP)]
 
     inside = sphere_mask.astype(BF16)[None, None]
     masked = block * inside
@@ -398,22 +393,22 @@
     column = jnp.broadcast_to(column.astype(BF16)[None, None], (GROUP, 1, sticks, NG))
     part = exchange(jnp.concatenate([grouped, column], axis=1), "pw", fours)
     sent = spread(part)
-    recv = two_steps(sent, far, near)
+    recv = exchange(sent, "pw", rings)
 
     bands_rows = jnp.transpose(pack(bands * inside), (2, 0, 1, 3)).reshape(-1, NG)
     v_high = lax.reduce_precision(potential, 8, 7)
     v_low = (potential - v_high).astype(BF16)
     potential_rows = jnp.stack([v_high.astype(BF16), v_low]).reshape(-1, NG)
-    side = jnp.concatenate([potential_rows, bands_rows], axis=0)
-    sides = [side] + [partner(side, turn, size) for turn in range(1, GROUP)]
-    bands_all = place([piece[potential_rows.shape[0] :] for piece in sides], me)
+    potentials = [potential_rows] + [partner(potential_rows, turn, size) for turn in range(1, GROUP)]
+    back, bands_rows = planes(me.reshape(1), recv, potentials, bands_rows)
+    back = exchange(back, "pw", rings)
+    bands_all = place([bands_rows] + [partner(bands_rows, turn, size) for turn in range(1, GROUP)], me)
     bands_all = [piece.reshape(sticks // 2, 2 * rows, NG) for piece in bands_all]
     vectors = part[:, : 2 * BANDS].reshape(GROUP * BANDS, 2, sticks, NG)
     masked_all = lax.all_gather(jnp.stack([vectors, vectors]), "band", axis=1, tiled=True)[0]
     masked_all = pack(masked_all.reshape(teams * GROUP * BANDS, 2, sticks, NG))
     masked_all = masked_all.reshape(teams, GROUP, BANDS, 2, sticks // 2, NG)
 
-    back = two_steps(planes(me.reshape(1), recv, sides), near, far)
     result, copies = finish(back, part, teams)
     applied_all = exchange(copies, "band").reshape(teams, BANDS, 2, GROUP, sticks // 2, NG)
     pieces = [lax.dynamic_index_in_dim(result, jnp.bitwise_xor(me, turn), 0, False) for turn in range(GROUP)]
@@ -421,8 +416,7 @@
     applied = jnp.stack(place(pieces, me)).reshape(own, 2, sticks, NG)
 
     terms = jnp.stack([pairing(bands_all, masked_all, 1), pairing(bands_all, applied_all, 3)])
-    total = jnp.sum(to_all(terms.reshape(-1, NG), "pw", GROUP, near), axis=0)
-    total = jnp.sum(to_all(total, "pw", GROUP, far), axis=0)
+    total = jnp.sum(to_all(terms.reshape(-1, NG), "pw", size // GROUP, rings), axis=0)
     total = to_all(total, "pw", GROUP, fours).reshape(GROUP, 2, 2, rows, teams, BANDS)
     total = jnp.transpose(total, (1, 2, 3, 4, 0, 5)).reshape(2, 2, rows, teams * own)
     return (applied, total[0], total[1])

time: 221 us -> 170 us (0.77)
  waiting for transfers between devices: 60.9 us -> 29.3 us
  blocking collectives: 43.7 us -> 13.9 us
  starting transfers between devices: 57.9 us -> 68.9 us
    all_to_all x3 -> x1, blocking collectives: 43.7 us -> 13.9 us  [exchange(): lax.all_to_all(value, axis, 0, 0, axis_index_groups=groups, tiled=True)]
    ppermute x6 -> x9, waiting for transfers between devices: 24.7 us -> 2.18 us  [partner(): return lax.ppermute(value, 'pw', [(i, i ^ turn) for i in range(size)])]
    all_to_all x6 -> x5, waiting for transfers between devices: 36.2 us -> 27.1 us  [exchange(): lax.all_to_all(value, axis, 0, 0, axis_index_groups=groups, tiled=True)]
    ppermute x6 -> x9, starting transfers between devices: 20 us -> 26 us  [partner(): return lax.ppermute(value, 'pw', [(i, i ^ turn) for i in range(size)])]
    all_to_all x6 -> x5, starting transfers between devices: 37.9 us -> 42.9 us  [exchange(): lax.all_to_all(value, axis, 0, 0, axis_index_groups=groups, tiled=True)]
  transfers between devices with their start and end apart: 13 -> 15, of which waited for: 6 -> 5; matrix products, arithmetic and copies ran while one was open for 3% -> 2% of each run, Pallas kernels for 11% -> 15%
where the time goes in v4:
time: 170 us; the launch traced here: 169 us
  starting transfers between devices  68.9 us (41%)
  waiting for transfers between devices  29.3 us (17%)
  Pallas kernels  25.2 us (15%)
  between operations  14.5 us (9%)
  blocking collectives  13.9 us (8%)
  local copies, waits for them, and re-layouts  10.2 us (6%)
  other arithmetic  5.06 us (3%)
    all_to_all x5, starting transfers between devices, exchange(): lax.all_to_all(value, axis, 0, 0, axis_index_groups=groups, tiled=True)  42.9 us
    all_to_all x5, waiting for transfers between devices, exchange(): lax.all_to_all(value, axis, 0, 0, axis_index_groups=groups, tiled=True)  27.1 us
    ppermute x9, starting transfers between devices, partner(): return lax.ppermute(value, 'pw', [(i, i ^ turn) for i in range(size)])  26 us
    pallas_call x3, Pallas kernels, vmem_call(): pl.pallas_call(kernel, out_shape=out_shape, in_specs=specs or [vmem] * le...  25.2 us
    all_to_all x1, blocking collectives, exchange(): lax.all_to_all(value, axis, 0, 0, axis_index_groups=groups, tiled=True)  13.9 us
  transfers between devices with their start and end apart: 15, of which 5 were waited for; matrix products, arithmetic and copies ran while one was open for 2% of the time, Pallas kernels for 15%

profile of v4, /device:TPU:1, one launch (start us, length us, event | category | flops | bytes accessed | tf_op | source)
XLA Modules:
  0.0 168.9 jit_solution(16830086909356999386)
XLA Ops:
  7.2 0.7 and_select_fusion.1
  7.9 0.7 convert_element_type.16
  8.6 1.0 broadcast_multiply_fusion.1
  9.7 13.9 %all_to_all.30.part_ref = bf16[4,5,40,128]{3,2,1,0:T(8,128)(2,1)S(1)} all-to-all(bf16[4,5,40,128]{3,2,1,0:T(8,128)(2,1)S(1)} %pad_maximum_fusion.1), channel_id=1, replica_groups={{0,1,2,3},{4,5,6,7},{8,9,10,11},{12,13,14,15},{16,17,18,19},{20,21,22,2..., dimensions={0} | all-to-all | bytes 409600 | tf_op jit(solution)/shard_map/all_to_all | solution.py:373
  23.7 0.7 pad_maximum_fusion
  24.5 2.7 %collective-permute-start.2 = (bf16[512,128]{1,0:T(8,128)(2,1)S(1)}, bf16[512,128]{1,0:T(8,128)(2,1)S(1)}, u32[]{:S(2)}, u32[]{:S(2)}) collective-permute-start(bf16[512,128]{1,0:T(8,128)(2,1)S(1)} %bitcast.171), channel_id=1, source_target_pairs={{0,3},{1,2},{2,1},{3,0},{4,7},{5,6},{6,5},{7,4},{8,11},{9,10},{10,... | collective-permute-start | bytes 393224 | tf_op jit(solution)/shard_map/ppermute | solution.py:362
  27.2 3.3 %collective-permute-start.1 = (bf16[512,128]{1,0:T(8,128)(2,1)S(1)}, bf16[512,128]{1,0:T(8,128)(2,1)S(1)}, u32[]{:S(2)}, u32[]{:S(2)}) collective-permute-start(bf16[512,128]{1,0:T(8,128)(2,1)S(1)} %bitcast.172), channel_id=1, source_target_pairs={{0,2},{1,3},{2,0},{3,1},{4,6},{5,7},{6,4},{7,5},{8,10},{9,11},{10,... | collective-permute-start | bytes 393224 | tf_op jit(solution)/shard_map/ppermute | solution.py:362
  30.5 1.9 %collective-permute-start = (bf16[512,128]{1,0:T(8,128)(2,1)S(1)}, bf16[512,128]{1,0:T(8,128)(2,1)S(1)}, u32[]{:S(2)}, u32[]{:S(2)}) collective-permute-start(bf16[512,128]{1,0:T(8,128)(2,1)S(1)} %bitcast.173), channel_id=1, source_target_pairs={{0,1},{1,0},{2,3},{3,2},{4,5},{5,4},{6,7},{7,6},{8,9},{9,8},{10,11... | collective-permute-start | bytes 393224 | tf_op jit(solution)/shard_map/ppermute | solution.py:362
  32.4 2.3 %shard_map.175 = s16[16,48,128]{2,1,0:T(8,128)(2,1)} custom-call(bf16[4,5,40,128]{3,2,1,0:T(8,128)(2,1)} %copy-done, bf16[256,256]{1,0:T(8,128)(2,1)} %constant.71.clone.high_ref, bf16[256,256]{1,0:T(8,128)(2,1)} %constant.72.clone.low_ref), custom_call_target="tpu_custom_call" | custom-call | tf_op jit(solution)/shard_map/pallas_call | solution.py:289
  34.7 9.7 %all-to-all-start.1 = ((s16[16,48,128]{2,1,0:T(8,128)(2,1)}), s16[16,48,128]{2,1,0:T(8,128)(2,1)S(1)}, u32[]{:S(2)}, u32[]{:S(2)}) async-start(s16[16,48,128]{2,1,0:T(8,128)(2,1)} %shard_map.175), calls=%async_computation.1 | async-start | bytes 393216 | tf_op jit(solution)/shard_map/all_to_all | solution.py:373
  44.5 0.3 fusion.13
  44.8 0.3 fusion.6
  45.1 1.0 copy.80
  46.2 10.8 %all-to-all-done.1.recv_ref = s16[16,48,128]{2,1,0:T(8,128)(2,1)S(1)} async-done(((s16[16,48,128]{2,1,0:T(8,128)(2,1)}), s16[16,48,128]{2,1,0:T(8,128)(2,1)S(1)}, u32[]{:S(2)}, u32[]{:S(2)}) %all-to-all-start.1) | async-done | bytes 196640 | tf_op jit(solution)/shard_map/all_to_all | solution.py:373
  57.0 0.7 copy-done.2
  57.7 20.2 %shard_map.176 = (s16[16,48,128]{2,1,0:T(8,128)(2,1)}, bf16[1280,128]{1,0:T(8,128)(2,1)}) custom-call(s32[1]{0:T(128)} %bitcast.me_ref, s16[16,48,128]{2,1,0:T(8,128)(2,1)} %copy-done.2, bf16[512,128]{1,0:T(8,128)(2,1)} %bitcast.174, bf16[512,128]{1,0:T(8,128)(2,1)} %copy-done.9, bf16[512,128]{1,0:T(8,128)(2,1)} %copy-done.8, ...), custom_call_target="tpu_custom_call", output_to_operand_aliasing={{1}: (13, {})} | custom-call | tf_op jit(solution)/shard_map/pallas_call | solution.py:289
  77.9 8.9 %all-to-all-start.2 = ((s16[16,48,128]{2,1,0:T(8,128)(2,1)}), s16[16,48,128]{2,1,0:T(8,128)(2,1)S(1)}, u32[]{:S(2)}, u32[]{:S(2)}) async-start(s16[16,48,128]{2,1,0:T(8,128)(2,1)} %get-tuple-element.7), calls=%async_computation.2 | async-start | bytes 393216 | tf_op jit(solution)/shard_map/all_to_all | solution.py:373
  86.9 2.8 %collective-permute-start.8 = (bf16[1280,128]{1,0:T(8,128)(2,1)}, bf16[1280,128]{1,0:T(8,128)(2,1)S(1)}, u32[]{:S(2)}, u32[]{:S(2)}) collective-permute-start(bf16[1280,128]{1,0:T(8,128)(2,1)} %get-tuple-element.9), channel_id=1, source_target_pairs={{0,1},{1,0},{2,3},{3,2},{4,5},{5,4},{6,7},{7,6},{8,9},{9,8},{10,11... | collective-permute-start | bytes 983048 | tf_op jit(solution)/shard_map/ppermute | solution.py:362
  89.8 2.3 %collective-permute-start.7 = (bf16[1280,128]{1,0:T(8,128)(2,1)}, bf16[1280,128]{1,0:T(8,128)(2,1)S(1)}, u32[]{:S(2)}, u32[]{:S(2)}) collective-permute-start(bf16[1280,128]{1,0:T(8,128)(2,1)} %get-tuple-element.9), channel_id=1, source_target_pairs={{0,2},{1,3},{2,0},{3,1},{4,6},{5,7},{6,4},{7,5},{8,10},{9,11},{10,... | collective-permute-start | bytes 983048 | tf_op jit(solution)/shard_map/ppermute | solution.py:362
  92.1 3.2 %collective-permute-start.6 = (bf16[1280,128]{1,0:T(8,128)(2,1)}, bf16[1280,128]{1,0:T(8,128)(2,1)S(1)}, u32[]{:S(2)}, u32[]{:S(2)}) collective-permute-start(bf16[1280,128]{1,0:T(8,128)(2,1)} %get-tuple-element.9), channel_id=1, source_target_pairs={{0,3},{1,2},{2,1},{3,0},{4,7},{5,6},{6,5},{7,4},{8,11},{9,10},{10,... | collective-permute-start | bytes 983048 | tf_op jit(solution)/shard_map/ppermute | solution.py:362
  95.2 4.2 %all-to-all-done.2.recv_ref = s16[16,48,128]{2,1,0:T(8,128)(2,1)S(1)} async-done(((s16[16,48,128]{2,1,0:T(8,128)(2,1)}), s16[16,48,128]{2,1,0:T(8,128)(2,1)S(1)}, u32[]{:S(2)}, u32[]{:S(2)}) %all-to-all-start.2) | async-done | bytes 196640 | tf_op jit(solution)/shard_map/all_to_all | solution.py:373
  99.5 0.7 copy-done.3
  100.1 2.7 %shard_map.177 = (bf16[4,4,40,128]{3,2,1,0:T(8,128)(2,1)}, bf16[8,320,128]{2,1,0:T(8,128)(2,1)}) custom-call(s16[16,48,128]{2,1,0:T(8,128)(2,1)} %copy-done.3, bf16[4,5,40,128]{3,2,1,0:T(8,128)(2,1)} %copy-done, bf16[256,256]{1,0:T(8,128)(2,1)} %constant.71.clone.high_ref, bf16[256,256]{1,0:T(8,128)(2,1)} %constant.72.clone.low_ref), custom_call_target="tpu_custom_call" | custom-call | tf_op jit(solution)/shard_map/pallas_call | solution.py:289
  102.9 6.5 %all-to-all-start.3 = ((bf16[8,320,128]{2,1,0:T(8,128)(2,1)}), bf16[8,320,128]{2,1,0:T(8,128)(2,1)S(1)}, u32[]{:S(2)}, u32[]{:S(2)}) async-start(bf16[8,320,128]{2,1,0:T(8,128)(2,1)} %get-tuple-element.10), calls=%async_computation.3 | async-start | bytes 1310720 | tf_op jit(solution)/shard_map/all_to_all | solution.py:373
  109.5 9.6 %all-to-all-done.3 = bf16[8,320,128]{2,1,0:T(8,128)(2,1)S(1)} async-done(((bf16[8,320,128]{2,1,0:T(8,128)(2,1)}), bf16[8,320,128]{2,1,0:T(8,128)(2,1)S(1)}, u32[]{:S(2)}, u32[]{:S(2)}) %all-to-all-start.3) | async-done | bytes 655392 | tf_op jit(solution)/shard_map/all_to_all | solution.py:373
  119.1 0.4 copy.90
  119.7 0.2 fusion.2
  120.7 1.4 slice_bitcast_fusion
  122.1 0.3 fusion.10
  122.4 0.5 slice_add_fusion
  122.9 0.5 fusion.12
  124.6 0.3 copy.98
  124.9 0.3 broadcast_in_dim.65
  125.1 0.7 broadcast_in_dim.66
  125.8 10.8 %all-to-all-start.4 = ((f32[16,16,128]{2,1,0:T(8,128)}), f32[16,16,128]{2,1,0:T(8,128)S(1)}, u32[]{:S(2)}, u32[]{:S(2)}) async-start(f32[16,16,128]{2,1,0:T(8,128)} %broadcast_in_dim.66), calls=%async_computation.4 | async-start | bytes 262144 | tf_op jit(solution)/shard_map/all_to_all | solution.py:373
  136.7 4.3 %collective-permute-start.5 = (bf16[4,40,128]{2,1,0:T(8,128)(2,1)S(1)}, bf16[4,40,128]{2,1,0:T(8,128)(2,1)S(1)}, u32[]{:S(2)}, u32[]{:S(2)}) collective-permute-start(bf16[4,40,128]{2,1,0:T(8,128)(2,1)S(1)} %get-tuple-element.38), channel_id=1, source_target_pairs={{0,1},{1,0},{2,3},{3,2},{4,5},{5,4},{6,7},{7,6},{8,9},{9,8},{10,11... | collective-permute-start | bytes 122888 | tf_op jit(solution)/shard_map/ppermute | solution.py:362
  141.0 2.0 %collective-permute-start.4 = (bf16[4,40,128]{2,1,0:T(8,128)(2,1)S(1)}, bf16[4,40,128]{2,1,0:T(8,128)(2,1)S(1)}, u32[]{:S(2)}, u32[]{:S(2)}) collective-permute-start(bf16[4,40,128]{2,1,0:T(8,128)(2,1)S(1)} %get-tuple-element.39), channel_id=1, source_target_pairs={{0,2},{1,3},{2,0},{3,1},{4,6},{5,7},{6,4},{7,5},{8,10},{9,11},{10,... | collective-permute-start | bytes 122888 | tf_op jit(solution)/shard_map/ppermute | solution.py:362
  143.0 3.5 %collective-permute-start.3 = (bf16[4,40,128]{2,1,0:T(8,128)(2,1)S(1)}, bf16[4,40,128]{2,1,0:T(8,128)(2,1)S(1)}, u32[]{:S(2)}, u32[]{:S(2)}) collective-permute-start(bf16[4,40,128]{2,1,0:T(8,128)(2,1)S(1)} %get-tuple-element.40), channel_id=1, source_target_pairs={{0,3},{1,2},{2,1},{3,0},{4,7},{5,6},{6,5},{7,4},{8,11},{9,10},{10,... | collective-permute-start | bytes 122888 | tf_op jit(solution)/shard_map/ppermute | solution.py:362
  146.5 2.2 %collective-permute-done.3 = bf16[4,40,128]{2,1,0:T(8,128)(2,1)S(1)} collective-permute-done((bf16[4,40,128]{2,1,0:T(8,128)(2,1)S(1)}, bf16[4,40,128]{2,1,0:T(8,128)(2,1)S(1)}, u32[]{:S(2)}, u32[]{:S(2)}) %collective-permute-start.3) | collective-permute-done | bytes 40992 | tf_op jit(solution)/shard_map/ppermute | solution.py:362
  148.8 0.6 broadcast_in_dim.67
  149.4 7.0 %all-to-all-start.5 = ((f32[4,16,128]{2,1,0:T(8,128)}), f32[4,16,128]{2,1,0:T(8,128)S(1)}, u32[]{:S(2)}, u32[]{:S(2)}) async-start(f32[4,16,128]{2,1,0:T(8,128)} %broadcast_in_dim.67), calls=%async_computation.5 | async-start | bytes 65536 | tf_op jit(solution)/shard_map/all_to_all | solution.py:373
  156.3 0.7 pad_maximum_fusion.2
  157.0 2.5 %all-to-all-done.5 = f32[4,16,128]{2,1,0:T(8,128)S(1)} async-done(((f32[4,16,128]{2,1,0:T(8,128)}), f32[4,16,128]{2,1,0:T(8,128)S(1)}, u32[]{:S(2)}, u32[]{:S(2)}) %all-to-all-start.5) | async-done | bytes 32800 | tf_op jit(solution)/shard_map/all_to_all | solution.py:373
  159.5 0.4 copy.99
  160.0 0.3 copy.101
  160.3 0.7 copy.103
  161.0 0.3 copy.100
  161.3 0.7 copy.102
  (64 shorter events, 2.7 us)
Async XLA Ops:
  7.2 113.6 %all-gather.2.cloned.1.call-start = ((), (), s32[]{:S(2)}) async-start(), calls=%async_computation.6 | async-start | bytes 2949120 | tf_op jit(solution)/shard_map/all_gather | solution.py:408
  8.6 15.8 %copy-start.10 = (f32[2,128,128]{2,1,0:T(8,128)S(1)}, f32[2,128,128]{2,1,0:T(8,128)}, u32[]{:S(2)}) copy-start(f32[2,128,128]{2,1,0:T(8,128)} %param.18) | copy-start | bytes 393220
  23.6 8.8 %copy-start = (bf16[4,5,40,128]{3,2,1,0:T(8,128)(2,1)}, bf16[4,5,40,128]{3,2,1,0:T(8,128)(2,1)S(1)}, u32[]{:S(2)}) copy-start(bf16[4,5,40,128]{3,2,1,0:T(8,128)(2,1)S(1)} %all_to_all.30.part_ref) | copy-start | bytes 614404
  23.6 20.8 %copy-start.4 = (bf16[32,2,40,128]{3,2,1,0:T(8,128)(2,1)S(1)}, bf16[32,2,40,128]{3,2,1,0:T(8,128)(2,1)}, u32[]{:S(2)}) copy-start(bf16[32,2,40,128]{3,2,1,0:T(8,128)(2,1)} %param.17) | copy-start | bytes 1966084
  24.5 20.3 %copy-start.5 = (bf16[2,2,128,128]{3,2,1,0:T(8,128)(2,1)}, bf16[2,2,128,128]{3,2,1,0:T(8,128)(2,1)S(1)}, u32[]{:S(2)}) copy-start(bf16[2,2,128,128]{3,2,1,0:T(8,128)(2,1)S(1)} %pad_maximum_fusion.3) | copy-start | bytes 393220
  24.5 21.7 %collective-permute-start.2 = (bf16[512,128]{1,0:T(8,128)(2,1)S(1)}, bf16[512,128]{1,0:T(8,128)(2,1)S(1)}, u32[]{:S(2)}, u32[]{:S(2)}) collective-permute-start(bf16[512,128]{1,0:T(8,128)(2,1)S(1)} %bitcast.171), channel_id=1, source_target_pairs={{0,3},{1,2},{2,1},{3,0},{4,7},{5,6},{6,5},{7,4},{8,11},{9,10},{10,... | collective-permute-start | bytes 393224 | tf_op jit(solution)/shard_map/ppermute | solution.py:362
  27.2 19.0 %collective-permute-start.1 = (bf16[512,128]{1,0:T(8,128)(2,1)S(1)}, bf16[512,128]{1,0:T(8,128)(2,1)S(1)}, u32[]{:S(2)}, u32[]{:S(2)}) collective-permute-start(bf16[512,128]{1,0:T(8,128)(2,1)S(1)} %bitcast.172), channel_id=1, source_target_pairs={{0,2},{1,3},{2,0},{3,1},{4,6},{5,7},{6,4},{7,5},{8,10},{9,11},{10,... | collective-permute-start | bytes 393224 | tf_op jit(solution)/shard_map/ppermute | solution.py:362
  30.5 15.7 %collective-permute-start = (bf16[512,128]{1,0:T(8,128)(2,1)S(1)}, bf16[512,128]{1,0:T(8,128)(2,1)S(1)}, u32[]{:S(2)}, u32[]{:S(2)}) collective-permute-start(bf16[512,128]{1,0:T(8,128)(2,1)S(1)} %bitcast.173), channel_id=1, source_target_pairs={{0,1},{1,0},{2,3},{3,2},{4,5},{5,4},{6,7},{7,6},{8,9},{9,8},{10,11... | collective-permute-start | bytes 393224 | tf_op jit(solution)/shard_map/ppermute | solution.py:362
  34.7 22.3 %all-to-all-start.1 = ((s16[16,48,128]{2,1,0:T(8,128)(2,1)}), s16[16,48,128]{2,1,0:T(8,128)(2,1)S(1)}, u32[]{:S(2)}, u32[]{:S(2)}) async-start(s16[16,48,128]{2,1,0:T(8,128)(2,1)} %shard_map.175), calls=%async_computation.1 | async-start | bytes 393216 | tf_op jit(solution)/shard_map/all_to_all | solution.py:373
  46.2 10.8 %copy-start.7 = (bf16[512,128]{1,0:T(8,128)(2,1)}, bf16[512,128]{1,0:T(8,128)(2,1)S(1)}, u32[]{:S(2)}) copy-start(bf16[512,128]{1,0:T(8,128)(2,1)S(1)} %collective-permute-done.2.v3_ref) | copy-start | bytes 393220
  46.2 10.8 %copy-start.8 = (bf16[512,128]{1,0:T(8,128)(2,1)}, bf16[512,128]{1,0:T(8,128)(2,1)S(1)}, u32[]{:S(2)}) copy-start(bf16[512,128]{1,0:T(8,128)(2,1)S(1)} %collective-permute-done.1.v2_ref) | copy-start | bytes 393220
  46.2 10.8 %copy-start.9 = (bf16[512,128]{1,0:T(8,128)(2,1)}, bf16[512,128]{1,0:T(8,128)(2,1)S(1)}, u32[]{:S(2)}) copy-start(bf16[512,128]{1,0:T(8,128)(2,1)S(1)} %collective-permute-done.v1_ref) | copy-start | bytes 393220
  57.0 0.7 copy-start.2
  77.9 31.4 %copy-start.1 = (bf16[1280,128]{1,0:T(8,128)(2,1)S(1)}, bf16[1280,128]{1,0:T(8,128)(2,1)}, u32[]{:S(2)}) copy-start(bf16[1280,128]{1,0:T(8,128)(2,1)} %get-tuple-element.9) | copy-start | bytes 983044
  77.9 21.5 %all-to-all-start.2 = ((s16[16,48,128]{2,1,0:T(8,128)(2,1)}), s16[16,48,128]{2,1,0:T(8,128)(2,1)S(1)}, u32[]{:S(2)}, u32[]{:S(2)}) async-start(s16[16,48,128]{2,1,0:T(8,128)(2,1)} %get-tuple-element.7), calls=%async_computation.2 | async-start | bytes 393216 | tf_op jit(solution)/shard_map/all_to_all | solution.py:373
  86.9 22.4 %collective-permute-start.8 = (bf16[1280,128]{1,0:T(8,128)(2,1)}, bf16[1280,128]{1,0:T(8,128)(2,1)S(1)}, u32[]{:S(2)}, u32[]{:S(2)}) collective-permute-start(bf16[1280,128]{1,0:T(8,128)(2,1)} %get-tuple-element.9), channel_id=1, source_target_pairs={{0,1},{1,0},{2,3},{3,2},{4,5},{5,4},{6,7},{7,6},{8,9},{9,8},{10,11... | collective-permute-start | bytes 983048 | tf_op jit(solution)/shard_map/ppermute | solution.py:362
  89.8 19.6 %collective-permute-start.7 = (bf16[1280,128]{1,0:T(8,128)(2,1)}, bf16[1280,128]{1,0:T(8,128)(2,1)S(1)}, u32[]{:S(2)}, u32[]{:S(2)}) collective-permute-start(bf16[1280,128]{1,0:T(8,128)(2,1)} %get-tuple-element.9), channel_id=1, source_target_pairs={{0,2},{1,3},{2,0},{3,1},{4,6},{5,7},{6,4},{7,5},{8,10},{9,11},{10,... | collective-permute-start | bytes 983048 | tf_op jit(solution)/shard_map/ppermute | solution.py:362
  92.1 17.3 %collective-permute-start.6 = (bf16[1280,128]{1,0:T(8,128)(2,1)}, bf16[1280,128]{1,0:T(8,128)(2,1)S(1)}, u32[]{:S(2)}, u32[]{:S(2)}) collective-permute-start(bf16[1280,128]{1,0:T(8,128)(2,1)} %get-tuple-element.9), channel_id=1, source_target_pairs={{0,3},{1,2},{2,1},{3,0},{4,7},{5,6},{6,5},{7,4},{8,11},{9,10},{10,... | collective-permute-start | bytes 983048 | tf_op jit(solution)/shard_map/ppermute | solution.py:362
  99.5 0.7 copy-start.3
  102.9 16.2 %all-to-all-start.3 = ((bf16[8,320,128]{2,1,0:T(8,128)(2,1)}), bf16[8,320,128]{2,1,0:T(8,128)(2,1)S(1)}, u32[]{:S(2)}, u32[]{:S(2)}) async-start(bf16[8,320,128]{2,1,0:T(8,128)(2,1)} %get-tuple-element.10), calls=%async_computation.3 | async-start | bytes 1310720 | tf_op jit(solution)/shard_map/all_to_all | solution.py:373
  124.0 12.7 %copy-start.6 = (bf16[4,4,40,128]{3,2,1,0:T(8,128)(2,1)S(1)}, bf16[4,4,40,128]{3,2,1,0:T(8,128)(2,1)}, u32[]{:S(2)}) copy-start(bf16[4,4,40,128]{3,2,1,0:T(8,128)(2,1)} %get-tuple-element.8) | copy-start | bytes 491524
  125.8 22.9 %all-to-all-start.4 = ((f32[16,16,128]{2,1,0:T(8,128)}), f32[16,16,128]{2,1,0:T(8,128)S(1)}, u32[]{:S(2)}, u32[]{:S(2)}) async-start(f32[16,16,128]{2,1,0:T(8,128)} %broadcast_in_dim.66), calls=%async_computation.4 | async-start | bytes 262144 | tf_op jit(solution)/shard_map/all_to_all | solution.py:373
  136.7 9.8 %collective-permute-start.5 = (bf16[4,40,128]{2,1,0:T(8,128)(2,1)S(1)}, bf16[4,40,128]{2,1,0:T(8,128)(2,1)S(1)}, u32[]{:S(2)}, u32[]{:S(2)}) collective-permute-start(bf16[4,40,128]{2,1,0:T(8,128)(2,1)S(1)} %get-tuple-element.38), channel_id=1, source_target_pairs={{0,1},{1,0},{2,3},{3,2},{4,5},{5,4},{6,7},{7,6},{8,9},{9,8},{10,11... | collective-permute-start | bytes 122888 | tf_op jit(solution)/shard_map/ppermute | solution.py:362
  141.0 5.5 %collective-permute-start.4 = (bf16[4,40,128]{2,1,0:T(8,128)(2,1)S(1)}, bf16[4,40,128]{2,1,0:T(8,128)(2,1)S(1)}, u32[]{:S(2)}, u32[]{:S(2)}) collective-permute-start(bf16[4,40,128]{2,1,0:T(8,128)(2,1)S(1)} %get-tuple-element.39), channel_id=1, source_target_pairs={{0,2},{1,3},{2,0},{3,1},{4,6},{5,7},{6,4},{7,5},{8,10},{9,11},{10,... | collective-permute-start | bytes 122888 | tf_op jit(solution)/shard_map/ppermute | solution.py:362
  143.0 5.7 %collective-permute-start.3 = (bf16[4,40,128]{2,1,0:T(8,128)(2,1)S(1)}, bf16[4,40,128]{2,1,0:T(8,128)(2,1)S(1)}, u32[]{:S(2)}, u32[]{:S(2)}) collective-permute-start(bf16[4,40,128]{2,1,0:T(8,128)(2,1)S(1)} %get-tuple-element.40), channel_id=1, source_target_pairs={{0,3},{1,2},{2,1},{3,0},{4,7},{5,6},{6,5},{7,4},{8,11},{9,10},{10,... | collective-permute-start | bytes 122888 | tf_op jit(solution)/shard_map/ppermute | solution.py:362
  149.4 10.1 %all-to-all-start.5 = ((f32[4,16,128]{2,1,0:T(8,128)}), f32[4,16,128]{2,1,0:T(8,128)S(1)}, u32[]{:S(2)}, u32[]{:S(2)}) async-start(f32[4,16,128]{2,1,0:T(8,128)} %broadcast_in_dim.67), calls=%async_computation.5 | async-start | bytes 65536 | tf_op jit(solution)/shard_map/all_to_all | solution.py:373
Sparse Core Ops, SparseCore 0:
  24.6 73.2 all-gather.1

commit v5 on v4

--- a/solution.py
+++ b/solution.py
@@ -102,7 +102,27 @@
     return value.astype(jnp.int32).astype(F32)
 
 
-def spread_kernel(part_ref, high_ref, low_ref, out_ref):
+def group_kernel(cells_ref, block_ref, mask_ref, out_ref, column_ref):
+    sticks = mask_ref.shape[0]
+    inside = jnp.where(mask_ref[...] > 0, 1.0, 0.0)
+    lane = lax.broadcasted_iota(jnp.int32, (1, NG), 1)
+    for s in range(sticks):
+        cell = cells_ref[s]
+        x, y = lax.shift_right_logical(cell, 7), jnp.bitwise_and(cell, NG - 1)
+        column_ref[s : s + 1, :] = jnp.where(lane == 0, x, jnp.where(lane == 1, y, 0)).astype(F32)
+    column = column_ref[...].astype(BF16)
+    for group in range(GROUP):
+        for line in range(2 * BANDS):
+            value = block_ref[BANDS * group + line // 2, line % 2].astype(F32) * inside
+            out_ref[group, line] = value.astype(BF16)
+        out_ref[group, 2 * BANDS] = column
+
+
+def spread_kernel(part_ref, high_ref, low_ref, rows_ref, out_ref, vectors_ref, same_rows_ref):
+    for src in range(GROUP):
+        for band in range(BANDS):
+            for copy in range(vectors_ref.shape[0]):
+                vectors_ref[copy, BANDS * src + band] = part_ref[src, 2 * band : 2 * band + 2]
     powers, tails = [], []
     for band in range(BANDS):
         real = part_ref[:, 2 * band].reshape(STICKS, NG)
@@ -247,7 +267,9 @@
     out_ref[:, 32:48, :] = to_short(tail_ref[...])
 
 
-def finish_kernel(recv_ref, part_ref, high_ref, low_ref, out_ref, copies_ref, line_ref, pack_ref):
+def finish_kernel(
+    recv_ref, part_ref, high_ref, low_ref, rows_ref, out_ref, copies_ref, same_rows_ref, line_ref, pack_ref
+):
     squares = part_ref[:, 2 * BANDS].reshape(STICKS, NG).astype(F32)
     signed = jnp.where(squares < NG // 2, squares, squares - NG)
     across = signed * signed
@@ -297,10 +319,25 @@
     )(*inputs)
 
 
-def spread(part):
+def group(stick_cells, block, sphere_mask):
+    sticks = block.shape[2]
+    shape = jax.ShapeDtypeStruct((GROUP, 2 * BANDS + 1, sticks, NG), BF16)
+    whole = pl.BlockSpec(memory_space=pltpu.VMEM)
+    specs = [pl.BlockSpec(memory_space=pltpu.SMEM), whole, whole]
+    inputs = (stick_cells, block, sphere_mask)
+    return vmem_call(group_kernel, shape, inputs, (pltpu.VMEM((sticks, NG), F32),), specs)
+
+
+def spread(part, rows):
     (high, low), _ = depth_tables()
-    shape = jax.ShapeDtypeStruct((RING, ROWS, NG), jnp.int16)
-    return vmem_call(spread_kernel, shape, (part, high, low))
+    shape = (
+        jax.ShapeDtypeStruct((RING, ROWS, NG), jnp.int16),
+        jax.ShapeDtypeStruct((2, GROUP * BANDS, 2, *part.shape[2:]), BF16),
+        jax.ShapeDtypeStruct(rows.shape, rows.dtype),
+    )
+    whole, place = pl.BlockSpec(memory_space=pltpu.VMEM), pl.BlockSpec(memory_space=pl.ANY)
+    inputs = (part, high, low, rows)
+    return vmem_call(spread_kernel, shape, inputs, (), [whole] * 3 + [place], (whole, whole, place), {3: 2})
 
 
 def planes(me, recv, potentials, rows):
@@ -331,15 +368,18 @@
     return vmem_call(plane_kernel, shape, inputs, scratch, specs, outs, {len(inputs) - 1: 1})
 
 
-def finish(recv, part, copies):
+def finish(recv, part, copies, other):
     _, (high, low) = depth_tables()
     rows = BANDS * STICKS
     shape = (
         jax.ShapeDtypeStruct((GROUP, 2 * BANDS, STICKS // GROUP, NG), BF16),
         jax.ShapeDtypeStruct((copies, rows, NG), BF16),
+        jax.ShapeDtypeStruct(other.shape, other.dtype),
     )
     scratch = (pltpu.VMEM((2 * NG, 2 * NG), F32), pltpu.VMEM((rows, NG), F32))
-    return vmem_call(finish_kernel, shape, (recv, part, high, low), scratch)
+    whole, place = pl.BlockSpec(memory_space=pltpu.VMEM), pl.BlockSpec(memory_space=pl.ANY)
+    inputs = (recv, part, high, low, other)
+    return vmem_call(finish_kernel, shape, inputs, scratch, [whole] * 4 + [place], (whole, whole, place), {4: 2})
 
 
 def pack(value):
@@ -385,31 +425,25 @@
     fours = [[i * GROUP + j for j in range(GROUP)] for i in range(size // GROUP)]
     rings = [[i * GROUP + j for i in range(size // GROUP)] for j in range(GROUP)]
 
-    inside = sphere_mask.astype(BF16)[None, None]
-    masked = block * inside
-    lane = jnp.arange(NG, dtype=jnp.int32)[None, :]
-    column = jnp.where(lane == 0, stick_cells[:, None] // NG, jnp.where(lane == 1, stick_cells[:, None] % NG, 0))
-    grouped = masked.reshape(GROUP, 2 * BANDS, sticks, NG)
-    column = jnp.broadcast_to(column.astype(BF16)[None, None], (GROUP, 1, sticks, NG))
-    part = exchange(jnp.concatenate([grouped, column], axis=1), "pw", fours)
-    sent = spread(part)
-    recv = exchange(sent, "pw", rings)
-
-    bands_rows = jnp.transpose(pack(bands * inside), (2, 0, 1, 3)).reshape(-1, NG)
+    part = exchange(group(stick_cells, block, sphere_mask), "pw", fours)
     v_high = lax.reduce_precision(potential, 8, 7)
     v_low = (potential - v_high).astype(BF16)
     potential_rows = jnp.stack([v_high.astype(BF16), v_low]).reshape(-1, NG)
+    sent, vectors, potential_rows = spread(part, potential_rows)
+    recv = exchange(sent, "pw", rings)
+
+    inside = sphere_mask.astype(BF16)[None, None]
+    bands_rows = jnp.transpose(pack(bands * inside), (2, 0, 1, 3)).reshape(-1, NG)
     potentials = [potential_rows] + [partner(potential_rows, turn, size) for turn in range(1, GROUP)]
     back, bands_rows = planes(me.reshape(1), recv, potentials, bands_rows)
     back = exchange(back, "pw", rings)
     bands_all = place([bands_rows] + [partner(bands_rows, turn, size) for turn in range(1, GROUP)], me)
     bands_all = [piece.reshape(sticks // 2, 2 * rows, NG) for piece in bands_all]
-    vectors = part[:, : 2 * BANDS].reshape(GROUP * BANDS, 2, sticks, NG)
-    masked_all = lax.all_gather(jnp.stack([vectors, vectors]), "band", axis=1, tiled=True)[0]
+    masked_all = lax.all_gather(vectors, "band", axis=1, tiled=True)[0]
     masked_all = pack(masked_all.reshape(teams * GROUP * BANDS, 2, sticks, NG))
     masked_all = masked_all.reshape(teams, GROUP, BANDS, 2, sticks // 2, NG)
 
-    result, copies = finish(back, part, teams)
+    result, copies, masked_all = finish(back, part, teams, masked_all)
     applied_all = exchange(copies, "band").reshape(teams, BANDS, 2, GROUP, sticks // 2, NG)
     pieces = [lax.dynamic_index_in_dim(result, jnp.bitwise_xor(me, turn), 0, False) for turn in range(GROUP)]
     pieces = pieces[:1] + [partner(pieces[turn], turn, size) for turn in range(1, GROUP)]

time: 170 us -> 189 us (1.11)
  waiting for transfers between devices: 29.3 us -> 47.3 us
  blocking collectives: 13.9 us -> 0 us
  starting transfers between devices: 68.9 us -> 79.9 us
  local copies, waits for them, and re-layouts: 10.2 us -> 12.2 us
    ppermute x9, waiting for transfers between devices: 2.18 us -> 22 us  [partner(): return lax.ppermute(value, 'pw', [(i, i ^ turn) for i in range(size)])]
    all_to_all x1 -> x0, blocking collectives: 13.9 us -> none  [exchange(): lax.all_to_all(value, axis, 0, 0, axis_index_groups=groups, tiled=True)]
    all_to_all x5 -> x6, starting transfers between devices: 42.9 us -> 54.4 us  [exchange(): lax.all_to_all(value, axis, 0, 0, axis_index_groups=groups, tiled=True)]
    all_to_all x5 -> x6, waiting for transfers between devices: 27.1 us -> 17.2 us  [exchange(): lax.all_to_all(value, axis, 0, 0, axis_index_groups=groups, tiled=True)]
    all_gather x1, waiting for transfers between devices: 0.01 us -> 8.09 us  [per_device(): masked_all = lax.all_gather(vectors, 'band', axis=1, tiled=True)[0]]
    pallas_call x3 -> x4, Pallas kernels: 25.2 us -> 27 us  [vmem_call(): pl.pallas_call(kernel, out_shape=out_shape, in_specs=specs or [vmem] * le...]
  transfers between devices with their start and end apart: 15 -> 16, of which waited for: 5 -> 10; matrix products, arithmetic and copies ran while one was open for 2% -> 5% of each run, Pallas kernels for 15% -> 11%
where the time goes in v5:
time: 189 us; the launch traced here: 188 us
  starting transfers between devices  79.9 us (42%)
  waiting for transfers between devices  47.3 us (25%)
  Pallas kernels  27 us (14%)
  between operations  14.4 us (8%)
  local copies, waits for them, and re-layouts  12.2 us (6%)
  other arithmetic  5.38 us (3%)
    all_to_all x6, starting transfers between devices, exchange(): lax.all_to_all(value, axis, 0, 0, axis_index_groups=groups, tiled=True)  54.4 us
    pallas_call x4, Pallas kernels, vmem_call(): pl.pallas_call(kernel, out_shape=out_shape, in_specs=specs or [vmem] * le...  27 us
    ppermute x9, starting transfers between devices, partner(): return lax.ppermute(value, 'pw', [(i, i ^ turn) for i in range(size)])  25.5 us
    ppermute x9, waiting for transfers between devices, partner(): return lax.ppermute(value, 'pw', [(i, i ^ turn) for i in range(size)])  22 us
    all_to_all x6, waiting for transfers between devices, exchange(): lax.all_to_all(value, axis, 0, 0, axis_index_groups=groups, tiled=True)  17.2 us
    all_gather x1, waiting for transfers between devices, per_device(): masked_all = lax.all_gather(vectors, 'band', axis=1, tiled=True)[0]  8.09 us
  transfers between devices with their start and end apart: 16, of which 10 were waited for; matrix products, arithmetic and copies ran while one was open for 5% of the time, Pallas kernels for 11%

profile of v5, /device:TPU:1, one launch (start us, length us, event | category | flops | bytes accessed | tf_op | source)
XLA Modules:
  0.0 187.9 jit_solution(11864789614206413780)
XLA Ops:
  7.2 1.7 shard_map.175
  8.9 10.2 %all-to-all-start = ((bf16[4,5,40,128]{3,2,1,0:T(8,128)(2,1)}), bf16[4,5,40,128]{3,2,1,0:T(8,128)(2,1)S(1)}, u32[]{:S(2)}, u32[]{:S(2)}) async-start(bf16[4,5,40,128]{3,2,1,0:T(8,128)(2,1)} %shard_map.175), calls=%async_computation | async-start | bytes 409600 | tf_op jit(solution)/shard_map/all_to_all | solution.py:413
  19.1 0.9 fusion.13
  20.1 0.7 pad_maximum_fusion.1
  20.7 3.0 %all-to-all-done.part_ref = bf16[4,5,40,128]{3,2,1,0:T(8,128)(2,1)S(1)} async-done(((bf16[4,5,40,128]{3,2,1,0:T(8,128)(2,1)}), bf16[4,5,40,128]{3,2,1,0:T(8,128)(2,1)S(1)}, u32[]{:S(2)}, u32[]{:S(2)}) %all-to-all-start) | async-done | bytes 204832 | tf_op jit(solution)/shard_map/all_to_all | solution.py:413
  23.7 0.7 copy-done
  24.4 2.3 %shard_map.176 = (s16[16,48,128]{2,1,0:T(8,128)(2,1)}, bf16[2,8,2,40,128]{4,3,2,1,0:T(8,128)(2,1)}, bf16[512,128]{1,0:T(8,128)(2,1)}) custom-call(bf16[4,5,40,128]{3,2,1,0:T(8,128)(2,1)} %copy-done, bf16[256,256]{1,0:T(8,128)(2,1)} %constant.43.clone.high_ref, bf16[256,256]{1,0:T(8,128)(2,1)} %constant.44.clone.low_ref, ...), custom_call_target="tpu_custom_call", output_to_operand_aliasing={{2}: (3, {})} | custom-call | tf_op jit(solution)/shard_map/pallas_call | solution.py:311
  26.7 9.7 %all-to-all-start.1 = ((s16[16,48,128]{2,1,0:T(8,128)(2,1)}), s16[16,48,128]{2,1,0:T(8,128)(2,1)S(1)}, u32[]{:S(2)}, u32[]{:S(2)}) async-start(s16[16,48,128]{2,1,0:T(8,128)(2,1)} %get-tuple-element.11), calls=%async_computation.1 | async-start | bytes 393216 | tf_op jit(solution)/shard_map/all_to_all | solution.py:413
  36.8 3.1 %collective-permute-start = (bf16[512,128]{1,0:T(8,128)(2,1)S(1)}, bf16[512,128]{1,0:T(8,128)(2,1)S(1)}, u32[]{:S(2)}, u32[]{:S(2)}) collective-permute-start(bf16[512,128]{1,0:T(8,128)(2,1)S(1)} %copy-done.1), channel_id=1, source_target_pairs={{0,1},{1,0},{2,3},{3,2},{4,5},{5,4},{6,7},{7,6},{8,9},{9,8},{10,11... | collective-permute-start | bytes 393224 | tf_op jit(solution)/shard_map/ppermute | solution.py:402
  39.9 2.0 %collective-permute-start.1 = (bf16[512,128]{1,0:T(8,128)(2,1)S(1)}, bf16[512,128]{1,0:T(8,128)(2,1)S(1)}, u32[]{:S(2)}, u32[]{:S(2)}) collective-permute-start(bf16[512,128]{1,0:T(8,128)(2,1)S(1)} %copy-done.1), channel_id=1, source_target_pairs={{0,2},{1,3},{2,0},{3,1},{4,6},{5,7},{6,4},{7,5},{8,10},{9,11},{10,... | collective-permute-start | bytes 393224 | tf_op jit(solution)/shard_map/ppermute | solution.py:402
  41.9 3.5 %collective-permute-start.2 = (bf16[512,128]{1,0:T(8,128)(2,1)S(1)}, bf16[512,128]{1,0:T(8,128)(2,1)S(1)}, u32[]{:S(2)}, u32[]{:S(2)}) collective-permute-start(bf16[512,128]{1,0:T(8,128)(2,1)S(1)} %copy-done.1), channel_id=1, source_target_pairs={{0,3},{1,2},{2,1},{3,0},{4,7},{5,6},{6,5},{7,4},{8,11},{9,10},{10,... | collective-permute-start | bytes 393224 | tf_op jit(solution)/shard_map/ppermute | solution.py:402
  45.7 1.0 copy.82
  46.9 6.8 %collective-permute-done.2.v3_ref = bf16[512,128]{1,0:T(8,128)(2,1)S(1)} collective-permute-done((bf16[512,128]{1,0:T(8,128)(2,1)S(1)}, bf16[512,128]{1,0:T(8,128)(2,1)S(1)}, u32[]{:S(2)}, u32[]{:S(2)}) %collective-permute-start.2) | collective-permute-done | bytes 131104 | tf_op jit(solution)/shard_map/ppermute | solution.py:402
  53.8 0.6 copy-done.8
  54.5 20.2 %shard_map.177 = (s16[16,48,128]{2,1,0:T(8,128)(2,1)}, bf16[1280,128]{1,0:T(8,128)(2,1)}) custom-call(s32[1]{0:T(128)} %bitcast.me_ref, s16[16,48,128]{2,1,0:T(8,128)(2,1)} %copy-done.2, bf16[512,128]{1,0:T(8,128)(2,1)} %get-tuple-element.12.v0_ref, bf16[512,128]{1,0:T(8,128)(2,1)} %copy-done.6, ...), custom_call_target="tpu_custom_call", output_to_operand_aliasing={{1}: (13, {})} | custom-call | tf_op jit(solution)/shard_map/pallas_call | solution.py:311
  74.7 1.9 %collective-permute-start.7 = (bf16[1280,128]{1,0:T(8,128)(2,1)}, bf16[1280,128]{1,0:T(8,128)(2,1)S(1)}, u32[]{:S(2)}, u32[]{:S(2)}) collective-permute-start(bf16[1280,128]{1,0:T(8,128)(2,1)} %get-tuple-element.16), channel_id=1, source_target_pairs={{0,2},{1,3},{2,0},{3,1},{4,6},{5,7},{6,4},{7,5},{8,10},{9,11},{10,... | collective-permute-start | bytes 983048 | tf_op jit(solution)/shard_map/ppermute | solution.py:402
  76.6 3.5 %collective-permute-start.6 = (bf16[1280,128]{1,0:T(8,128)(2,1)}, bf16[1280,128]{1,0:T(8,128)(2,1)S(1)}, u32[]{:S(2)}, u32[]{:S(2)}) collective-permute-start(bf16[1280,128]{1,0:T(8,128)(2,1)} %get-tuple-element.16), channel_id=1, source_target_pairs={{0,3},{1,2},{2,1},{3,0},{4,7},{5,6},{6,5},{7,4},{8,11},{9,10},{10,... | collective-permute-start | bytes 983048 | tf_op jit(solution)/shard_map/ppermute | solution.py:402
  80.2 2.1 %collective-permute-start.8 = (bf16[1280,128]{1,0:T(8,128)(2,1)}, bf16[1280,128]{1,0:T(8,128)(2,1)S(1)}, u32[]{:S(2)}, u32[]{:S(2)}) collective-permute-start(bf16[1280,128]{1,0:T(8,128)(2,1)} %get-tuple-element.16), channel_id=1, source_target_pairs={{0,1},{1,0},{2,3},{3,2},{4,5},{5,4},{6,7},{7,6},{8,9},{9,8},{10,11... | collective-permute-start | bytes 983048 | tf_op jit(solution)/shard_map/ppermute | solution.py:402
  82.3 11.6 %all-to-all-start.2 = ((s16[16,48,128]{2,1,0:T(8,128)(2,1)}), s16[16,48,128]{2,1,0:T(8,128)(2,1)S(1)}, u32[]{:S(2)}, u32[]{:S(2)}) async-start(s16[16,48,128]{2,1,0:T(8,128)(2,1)} %get-tuple-element.13), calls=%async_computation.2 | async-start | bytes 393216 | tf_op jit(solution)/shard_map/all_to_all | solution.py:413
  93.9 13.8 %collective-permute-done.6 = bf16[1280,128]{1,0:T(8,128)(2,1)S(1)} collective-permute-done((bf16[1280,128]{1,0:T(8,128)(2,1)}, bf16[1280,128]{1,0:T(8,128)(2,1)S(1)}, u32[]{:S(2)}, u32[]{:S(2)}) %collective-permute-start.6) | collective-permute-done | bytes 327712 | tf_op jit(solution)/shard_map/ppermute | solution.py:402
  107.7 1.1 broadcast_select_fusion.4
  108.8 8.1 %all-gather.2.cloned.1.call-done = bf16[2,64,2,40,128]{4,3,2,1,0:T(8,128)(2,1)} async-done(((bf16[2,8,2,40,128]{4,3,2,1,0:T(8,128)(2,1)}), bf16[2,64,2,40,128]{4,3,2,1,0:T(8,128)(2,1)}) %all-gather.2.cloned.1.call-update) | async-done | bytes 2621456 | tf_op jit(solution)/shard_map/all_gather | solution.py:442
  116.9 1.4 slice_bitcast_fusion
  118.3 0.8 fusion.14
  119.1 1.5 slice_add_fusion
  120.6 0.7 copy-done.3
  121.3 2.7 %shard_map.178 = (bf16[4,4,40,128]{3,2,1,0:T(8,128)(2,1)}, bf16[8,320,128]{2,1,0:T(8,128)(2,1)}, bf16[8,4,2,2,20,128]{5,4,3,2,1,0:T(8,128)(2,1)}) custom-call(s16[16,48,128]{2,1,0:T(8,128)(2,1)} %copy-done.3, bf16[4,5,40,128]{3,2,1,0:T(8,128)(2,1)} %copy-done, bf16[256,256]{1,0:T(8,128)(2,1)} %constant.43.clone.high_ref, ...), custom_call_target="tpu_custom_call", output_to_operand_aliasing={{2}: (4, {})} | custom-call | tf_op jit(solution)/shard_map/pallas_call | solution.py:311
  124.0 1.3 slice_bitcast_fusion.1
  125.3 3.7 %all-to-all-start.3 = ((bf16[8,320,128]{2,1,0:T(8,128)(2,1)}), bf16[8,320,128]{2,1,0:T(8,128)(2,1)S(1)}, u32[]{:S(2)}, u32[]{:S(2)}) async-start(bf16[8,320,128]{2,1,0:T(8,128)(2,1)} %get-tuple-element.18), calls=%async_computation.3 | async-start | bytes 1310720 | tf_op jit(solution)/shard_map/all_to_all | solution.py:413
  130.2 10.5 %all-to-all-done.3 = bf16[8,320,128]{2,1,0:T(8,128)(2,1)S(1)} async-done(((bf16[8,320,128]{2,1,0:T(8,128)(2,1)}), bf16[8,320,128]{2,1,0:T(8,128)(2,1)S(1)}, u32[]{:S(2)}, u32[]{:S(2)}) %all-to-all-start.3) | async-done | bytes 655392 | tf_op jit(solution)/shard_map/all_to_all | solution.py:413
  140.7 0.4 copy.90
  142.9 0.7 broadcast_in_dim.7
  143.6 11.8 %all-to-all-start.4 = ((f32[16,16,128]{2,1,0:T(8,128)}), f32[16,16,128]{2,1,0:T(8,128)S(1)}, u32[]{:S(2)}, u32[]{:S(2)}) async-start(f32[16,16,128]{2,1,0:T(8,128)} %broadcast_in_dim.7), calls=%async_computation.4 | async-start | bytes 262144 | tf_op jit(solution)/shard_map/all_to_all | solution.py:413
  155.4 4.9 %collective-permute-start.3 = (bf16[4,40,128]{2,1,0:T(8,128)(2,1)S(1)}, bf16[4,40,128]{2,1,0:T(8,128)(2,1)S(1)}, u32[]{:S(2)}, u32[]{:S(2)}) collective-permute-start(bf16[4,40,128]{2,1,0:T(8,128)(2,1)S(1)} %get-tuple-element.48), channel_id=1, source_target_pairs={{0,3},{1,2},{2,1},{3,0},{4,7},{5,6},{6,5},{7,4},{8,11},{9,10},{10,... | collective-permute-start | bytes 122888 | tf_op jit(solution)/shard_map/ppermute | solution.py:402
  160.3 2.5 %collective-permute-start.4 = (bf16[4,40,128]{2,1,0:T(8,128)(2,1)S(1)}, bf16[4,40,128]{2,1,0:T(8,128)(2,1)S(1)}, u32[]{:S(2)}, u32[]{:S(2)}) collective-permute-start(bf16[4,40,128]{2,1,0:T(8,128)(2,1)S(1)} %get-tuple-element.47), channel_id=1, source_target_pairs={{0,2},{1,3},{2,0},{3,1},{4,6},{5,7},{6,4},{7,5},{8,10},{9,11},{10,... | collective-permute-start | bytes 122888 | tf_op jit(solution)/shard_map/ppermute | solution.py:402
  162.9 1.9 %collective-permute-start.5 = (bf16[4,40,128]{2,1,0:T(8,128)(2,1)S(1)}, bf16[4,40,128]{2,1,0:T(8,128)(2,1)S(1)}, u32[]{:S(2)}, u32[]{:S(2)}) collective-permute-start(bf16[4,40,128]{2,1,0:T(8,128)(2,1)S(1)} %get-tuple-element.46), channel_id=1, source_target_pairs={{0,1},{1,0},{2,3},{3,2},{4,5},{5,4},{6,7},{7,6},{8,9},{9,8},{10,11... | collective-permute-start | bytes 122888 | tf_op jit(solution)/shard_map/ppermute | solution.py:402
  164.8 0.7 collective-permute-done.4
  165.6 0.4 collective-permute-done.5
  166.0 1.3 all-to-all-done.4
  167.4 0.6 broadcast_in_dim.16
  168.0 7.4 %all-to-all-start.5 = ((f32[4,16,128]{2,1,0:T(8,128)}), f32[4,16,128]{2,1,0:T(8,128)S(1)}, u32[]{:S(2)}, u32[]{:S(2)}) async-start(f32[4,16,128]{2,1,0:T(8,128)} %broadcast_in_dim.16), calls=%async_computation.5 | async-start | bytes 65536 | tf_op jit(solution)/shard_map/all_to_all | solution.py:413
  175.4 0.7 pad_maximum_fusion
  176.0 2.5 %all-to-all-done.5 = f32[4,16,128]{2,1,0:T(8,128)S(1)} async-done(((f32[4,16,128]{2,1,0:T(8,128)}), f32[4,16,128]{2,1,0:T(8,128)S(1)}, u32[]{:S(2)}, u32[]{:S(2)}) %all-to-all-start.5) | async-done | bytes 32800 | tf_op jit(solution)/shard_map/all_to_all | solution.py:413
  178.5 0.4 copy.99
  179.0 0.3 copy.100
  179.3 0.7 copy.102
  180.0 0.3 copy.101
  180.3 0.7 copy.103
  (54 shorter events, 4.0 us)
Async XLA Ops:
  7.2 19.5 %copy-start.9 = (s32[40,128]{1,0:T(8,128)S(1)}, s32[40,128]{1,0:T(8,128)}, u32[]{:S(2)}) copy-start(s32[40,128]{1,0:T(8,128)} %mask_ref.1) | copy-start | bytes 61444
  7.2 29.3 %copy-start.4 = (bf16[32,2,40,128]{3,2,1,0:T(8,128)(2,1)S(1)}, bf16[32,2,40,128]{3,2,1,0:T(8,128)(2,1)}, u32[]{:S(2)}) copy-start(bf16[32,2,40,128]{3,2,1,0:T(8,128)(2,1)} %param.17) | copy-start | bytes 1966084
  8.9 14.8 %all-to-all-start = ((bf16[4,5,40,128]{3,2,1,0:T(8,128)(2,1)}), bf16[4,5,40,128]{3,2,1,0:T(8,128)(2,1)S(1)}, u32[]{:S(2)}, u32[]{:S(2)}) async-start(bf16[4,5,40,128]{3,2,1,0:T(8,128)(2,1)} %shard_map.175), calls=%async_computation | async-start | bytes 409600 | tf_op jit(solution)/shard_map/all_to_all | solution.py:413
  19.1 97.7 %all-gather.2.cloned.1.call-start = ((), (), s32[]{:S(2)}) async-start(), calls=%async_computation.6 | async-start | bytes 2949120 | tf_op jit(solution)/shard_map/all_gather | solution.py:442
  23.7 0.7 copy-start
  26.7 10.1 %copy-start.1 = (bf16[512,128]{1,0:T(8,128)(2,1)S(1)}, bf16[512,128]{1,0:T(8,128)(2,1)}, u32[]{:S(2)}) copy-start(bf16[512,128]{1,0:T(8,128)(2,1)} %get-tuple-element.12.v0_ref) | copy-start | bytes 393220
  26.7 27.0 %all-to-all-start.1 = ((s16[16,48,128]{2,1,0:T(8,128)(2,1)}), s16[16,48,128]{2,1,0:T(8,128)(2,1)S(1)}, u32[]{:S(2)}, u32[]{:S(2)}) async-start(s16[16,48,128]{2,1,0:T(8,128)(2,1)} %get-tuple-element.11), calls=%async_computation.1 | async-start | bytes 393216 | tf_op jit(solution)/shard_map/all_to_all | solution.py:413
  36.8 9.9 %collective-permute-start = (bf16[512,128]{1,0:T(8,128)(2,1)S(1)}, bf16[512,128]{1,0:T(8,128)(2,1)S(1)}, u32[]{:S(2)}, u32[]{:S(2)}) collective-permute-start(bf16[512,128]{1,0:T(8,128)(2,1)S(1)} %copy-done.1), channel_id=1, source_target_pairs={{0,1},{1,0},{2,3},{3,2},{4,5},{5,4},{6,7},{7,6},{8,9},{9,8},{10,11... | collective-permute-start | bytes 393224 | tf_op jit(solution)/shard_map/ppermute | solution.py:402
  39.9 7.0 %collective-permute-start.1 = (bf16[512,128]{1,0:T(8,128)(2,1)S(1)}, bf16[512,128]{1,0:T(8,128)(2,1)S(1)}, u32[]{:S(2)}, u32[]{:S(2)}) collective-permute-start(bf16[512,128]{1,0:T(8,128)(2,1)S(1)} %copy-done.1), channel_id=1, source_target_pairs={{0,2},{1,3},{2,0},{3,1},{4,6},{5,7},{6,4},{7,5},{8,10},{9,11},{10,... | collective-permute-start | bytes 393224 | tf_op jit(solution)/shard_map/ppermute | solution.py:402
  41.9 11.8 %collective-permute-start.2 = (bf16[512,128]{1,0:T(8,128)(2,1)S(1)}, bf16[512,128]{1,0:T(8,128)(2,1)S(1)}, u32[]{:S(2)}, u32[]{:S(2)}) collective-permute-start(bf16[512,128]{1,0:T(8,128)(2,1)S(1)} %copy-done.1), channel_id=1, source_target_pairs={{0,3},{1,2},{2,1},{3,0},{4,7},{5,6},{6,5},{7,4},{8,11},{9,10},{10,... | collective-permute-start | bytes 393224 | tf_op jit(solution)/shard_map/ppermute | solution.py:402
  46.7 7.0 %copy-start.6 = (bf16[512,128]{1,0:T(8,128)(2,1)}, bf16[512,128]{1,0:T(8,128)(2,1)S(1)}, u32[]{:S(2)}) copy-start(bf16[512,128]{1,0:T(8,128)(2,1)S(1)} %collective-permute-done.v1_ref) | copy-start | bytes 393220
  46.9 6.8 %copy-start.7 = (bf16[512,128]{1,0:T(8,128)(2,1)}, bf16[512,128]{1,0:T(8,128)(2,1)S(1)}, u32[]{:S(2)}) copy-start(bf16[512,128]{1,0:T(8,128)(2,1)S(1)} %collective-permute-done.1.v2_ref) | copy-start | bytes 393220
  53.7 0.6 copy-start.8
  53.7 0.7 copy-start.2
  74.7 19.2 %collective-permute-start.7 = (bf16[1280,128]{1,0:T(8,128)(2,1)}, bf16[1280,128]{1,0:T(8,128)(2,1)S(1)}, u32[]{:S(2)}, u32[]{:S(2)}) collective-permute-start(bf16[1280,128]{1,0:T(8,128)(2,1)} %get-tuple-element.16), channel_id=1, source_target_pairs={{0,2},{1,3},{2,0},{3,1},{4,6},{5,7},{6,4},{7,5},{8,10},{9,11},{10,... | collective-permute-start | bytes 983048 | tf_op jit(solution)/shard_map/ppermute | solution.py:402
  76.6 31.1 %collective-permute-start.6 = (bf16[1280,128]{1,0:T(8,128)(2,1)}, bf16[1280,128]{1,0:T(8,128)(2,1)S(1)}, u32[]{:S(2)}, u32[]{:S(2)}) collective-permute-start(bf16[1280,128]{1,0:T(8,128)(2,1)} %get-tuple-element.16), channel_id=1, source_target_pairs={{0,3},{1,2},{2,1},{3,0},{4,7},{5,6},{6,5},{7,4},{8,11},{9,10},{10,... | collective-permute-start | bytes 983048 | tf_op jit(solution)/shard_map/ppermute | solution.py:402
  80.2 27.5 %collective-permute-start.8 = (bf16[1280,128]{1,0:T(8,128)(2,1)}, bf16[1280,128]{1,0:T(8,128)(2,1)S(1)}, u32[]{:S(2)}, u32[]{:S(2)}) collective-permute-start(bf16[1280,128]{1,0:T(8,128)(2,1)} %get-tuple-element.16), channel_id=1, source_target_pairs={{0,1},{1,0},{2,3},{3,2},{4,5},{5,4},{6,7},{7,6},{8,9},{9,8},{10,11... | collective-permute-start | bytes 983048 | tf_op jit(solution)/shard_map/ppermute | solution.py:402
  82.3 38.3 %all-to-all-start.2 = ((s16[16,48,128]{2,1,0:T(8,128)(2,1)}), s16[16,48,128]{2,1,0:T(8,128)(2,1)S(1)}, u32[]{:S(2)}, u32[]{:S(2)}) async-start(s16[16,48,128]{2,1,0:T(8,128)(2,1)} %get-tuple-element.13), calls=%async_computation.2 | async-start | bytes 393216 | tf_op jit(solution)/shard_map/all_to_all | solution.py:413
  120.6 0.7 copy-start.3
  125.3 15.4 %all-to-all-start.3 = ((bf16[8,320,128]{2,1,0:T(8,128)(2,1)}), bf16[8,320,128]{2,1,0:T(8,128)(2,1)S(1)}, u32[]{:S(2)}, u32[]{:S(2)}) async-start(bf16[8,320,128]{2,1,0:T(8,128)(2,1)} %get-tuple-element.18), calls=%async_computation.3 | async-start | bytes 1310720 | tf_op jit(solution)/shard_map/all_to_all | solution.py:413
  141.6 13.8 %copy-start.5 = (bf16[4,4,40,128]{3,2,1,0:T(8,128)(2,1)S(1)}, bf16[4,4,40,128]{3,2,1,0:T(8,128)(2,1)}, u32[]{:S(2)}) copy-start(bf16[4,4,40,128]{3,2,1,0:T(8,128)(2,1)} %get-tuple-element.15) | copy-start | bytes 491524
  143.6 23.8 %all-to-all-start.4 = ((f32[16,16,128]{2,1,0:T(8,128)}), f32[16,16,128]{2,1,0:T(8,128)S(1)}, u32[]{:S(2)}, u32[]{:S(2)}) async-start(f32[16,16,128]{2,1,0:T(8,128)} %broadcast_in_dim.7), calls=%async_computation.4 | async-start | bytes 262144 | tf_op jit(solution)/shard_map/all_to_all | solution.py:413
  155.4 9.4 %collective-permute-start.3 = (bf16[4,40,128]{2,1,0:T(8,128)(2,1)S(1)}, bf16[4,40,128]{2,1,0:T(8,128)(2,1)S(1)}, u32[]{:S(2)}, u32[]{:S(2)}) collective-permute-start(bf16[4,40,128]{2,1,0:T(8,128)(2,1)S(1)} %get-tuple-element.48), channel_id=1, source_target_pairs={{0,3},{1,2},{2,1},{3,0},{4,7},{5,6},{6,5},{7,4},{8,11},{9,10},{10,... | collective-permute-start | bytes 122888 | tf_op jit(solution)/shard_map/ppermute | solution.py:402
  160.3 5.2 %collective-permute-start.4 = (bf16[4,40,128]{2,1,0:T(8,128)(2,1)S(1)}, bf16[4,40,128]{2,1,0:T(8,128)(2,1)S(1)}, u32[]{:S(2)}, u32[]{:S(2)}) collective-permute-start(bf16[4,40,128]{2,1,0:T(8,128)(2,1)S(1)} %get-tuple-element.47), channel_id=1, source_target_pairs={{0,2},{1,3},{2,0},{3,1},{4,6},{5,7},{6,4},{7,5},{8,10},{9,11},{10,... | collective-permute-start | bytes 122888 | tf_op jit(solution)/shard_map/ppermute | solution.py:402
  162.9 3.1 %collective-permute-start.5 = (bf16[4,40,128]{2,1,0:T(8,128)(2,1)S(1)}, bf16[4,40,128]{2,1,0:T(8,128)(2,1)S(1)}, u32[]{:S(2)}, u32[]{:S(2)}) collective-permute-start(bf16[4,40,128]{2,1,0:T(8,128)(2,1)S(1)} %get-tuple-element.46), channel_id=1, source_target_pairs={{0,1},{1,0},{2,3},{3,2},{4,5},{5,4},{6,7},{7,6},{8,9},{9,8},{10,11... | collective-permute-start | bytes 122888 | tf_op jit(solution)/shard_map/ppermute | solution.py:402
  168.0 10.6 %all-to-all-start.5 = ((f32[4,16,128]{2,1,0:T(8,128)}), f32[4,16,128]{2,1,0:T(8,128)S(1)}, u32[]{:S(2)}, u32[]{:S(2)}) async-start(f32[4,16,128]{2,1,0:T(8,128)} %broadcast_in_dim.16), calls=%async_computation.5 | async-start | bytes 65536 | tf_op jit(solution)/shard_map/all_to_all | solution.py:413
Sparse Core Ops, SparseCore 0:
  26.8 89.9 all-gather.1

commit v6 on v5

--- a/solution.py
+++ b/solution.py
@@ -118,11 +118,7 @@
         out_ref[group, 2 * BANDS] = column
 
 
-def spread_kernel(part_ref, high_ref, low_ref, rows_ref, out_ref, vectors_ref, same_rows_ref):
-    for src in range(GROUP):
-        for band in range(BANDS):
-            for copy in range(vectors_ref.shape[0]):
-                vectors_ref[copy, BANDS * src + band] = part_ref[src, 2 * band : 2 * band + 2]
+def spread_kernel(part_ref, high_ref, low_ref, rows_ref, out_ref, same_rows_ref):
     powers, tails = [], []
     for band in range(BANDS):
         real = part_ref[:, 2 * band].reshape(STICKS, NG)
@@ -267,9 +263,7 @@
     out_ref[:, 32:48, :] = to_short(tail_ref[...])
 
 
-def finish_kernel(
-    recv_ref, part_ref, high_ref, low_ref, rows_ref, out_ref, copies_ref, same_rows_ref, line_ref, pack_ref
-):
+def finish_kernel(recv_ref, part_ref, high_ref, low_ref, out_ref, copies_ref, line_ref, pack_ref):
     squares = part_ref[:, 2 * BANDS].reshape(STICKS, NG).astype(F32)
     signed = jnp.where(squares < NG // 2, squares, squares - NG)
     across = signed * signed
@@ -332,12 +326,11 @@
     (high, low), _ = depth_tables()
     shape = (
         jax.ShapeDtypeStruct((RING, ROWS, NG), jnp.int16),
-        jax.ShapeDtypeStruct((2, GROUP * BANDS, 2, *part.shape[2:]), BF16),
         jax.ShapeDtypeStruct(rows.shape, rows.dtype),
     )
     whole, place = pl.BlockSpec(memory_space=pltpu.VMEM), pl.BlockSpec(memory_space=pl.ANY)
     inputs = (part, high, low, rows)
-    return vmem_call(spread_kernel, shape, inputs, (), [whole] * 3 + [place], (whole, whole, place), {3: 2})
+    return vmem_call(spread_kernel, shape, inputs, (), [whole] * 3 + [place], (whole, place), {3: 1})
 
 
 def planes(me, recv, potentials, rows):
@@ -368,18 +361,15 @@
     return vmem_call(plane_kernel, shape, inputs, scratch, specs, outs, {len(inputs) - 1: 1})
 
 
-def finish(recv, part, copies, other):
+def finish(recv, part, copies):
     _, (high, low) = depth_tables()
     rows = BANDS * STICKS
     shape = (
         jax.ShapeDtypeStruct((GROUP, 2 * BANDS, STICKS // GROUP, NG), BF16),
         jax.ShapeDtypeStruct((copies, rows, NG), BF16),
-        jax.ShapeDtypeStruct(other.shape, other.dtype),
     )
     scratch = (pltpu.VMEM((2 * NG, 2 * NG), F32), pltpu.VMEM((rows, NG), F32))
-    whole, place = pl.BlockSpec(memory_space=pltpu.VMEM), pl.BlockSpec(memory_space=pl.ANY)
-    inputs = (recv, part, high, low, other)
-    return vmem_call(finish_kernel, shape, inputs, scratch, [whole] * 4 + [place], (whole, whole, place), {4: 2})
+    return vmem_call(finish_kernel, shape, (recv, part, high, low), scratch)
 
 
 def pack(value):
@@ -429,7 +419,7 @@
     v_high = lax.reduce_precision(potential, 8, 7)
     v_low = (potential - v_high).astype(BF16)
     potential_rows = jnp.stack([v_high.astype(BF16), v_low]).reshape(-1, NG)
-    sent, vectors, potential_rows = spread(part, potential_rows)
+    sent, potential_rows = spread(part, potential_rows)
     recv = exchange(sent, "pw", rings)
 
     inside = sphere_mask.astype(BF16)[None, None]
@@ -439,11 +429,12 @@
     back = exchange(back, "pw", rings)
     bands_all = place([bands_rows] + [partner(bands_rows, turn, size) for turn in range(1, GROUP)], me)
     bands_all = [piece.reshape(sticks // 2, 2 * rows, NG) for piece in bands_all]
-    masked_all = lax.all_gather(vectors, "band", axis=1, tiled=True)[0]
+    vectors = part[:, : 2 * BANDS].reshape(GROUP * BANDS, 2, sticks, NG)
+    masked_all = lax.all_gather(jnp.stack([vectors, vectors]), "band", axis=1, tiled=True)[0]
     masked_all = pack(masked_all.reshape(teams * GROUP * BANDS, 2, sticks, NG))
     masked_all = masked_all.reshape(teams, GROUP, BANDS, 2, sticks // 2, NG)
 
-    result, copies, masked_all = finish(back, part, teams, masked_all)
+    result, copies = finish(back, part, teams)
     applied_all = exchange(copies, "band").reshape(teams, BANDS, 2, GROUP, sticks // 2, NG)
     pieces = [lax.dynamic_index_in_dim(result, jnp.bitwise_xor(me, turn), 0, False) for turn in range(GROUP)]
     pieces = pieces[:1] + [partner(pieces[turn], turn, size) for turn in range(1, GROUP)]

time: 189 us -> 169 us (0.89)
  waiting for transfers between devices: 47.3 us -> 25.6 us
  blocking collectives: 0 us -> 14.8 us
  starting transfers between devices: 79.9 us -> 70 us
  other arithmetic: 5.38 us -> 3.25 us
    all_to_all x0 -> x1, blocking collectives: none -> 14.8 us  [exchange(): lax.all_to_all(value, axis, 0, 0, axis_index_groups=groups, tiled=True)]
    ppermute x9, waiting for transfers between devices: 22 us -> 7.26 us  [partner(): return lax.ppermute(value, 'pw', [(i, i ^ turn) for i in range(size)])]
    all_to_all x6 -> x5, starting transfers between devices: 54.4 us -> 44.5 us  [exchange(): lax.all_to_all(value, axis, 0, 0, axis_index_groups=groups, tiled=True)]
    all_gather x1, waiting for transfers between devices: 8.09 us -> 0.01 us  [per_device(): lax.all_gather(jnp.stack([vectors, vectors]), 'band', axis=1, tiled=True)[0]]
    all_to_all x6 -> x5, waiting for transfers between devices: 17.2 us -> 18.4 us  [exchange(): lax.all_to_all(value, axis, 0, 0, axis_index_groups=groups, tiled=True)]
  transfers between devices with their start and end apart: 16 -> 15, of which waited for: 10 -> 5; matrix products, arithmetic and copies ran while one was open for 5% -> 3% of each run, Pallas kernels for 11% -> 15%
where the time goes in v6:
time: 169 us; the launch traced here: 168 us
  starting transfers between devices  70 us (41%)
  Pallas kernels  26.9 us (16%)
  waiting for transfers between devices  25.6 us (15%)
  blocking collectives  14.8 us (9%)
  between operations  14.5 us (9%)
  local copies, waits for them, and re-layouts  10.8 us (6%)
  other arithmetic  3.25 us (2%)
    all_to_all x5, starting transfers between devices, exchange(): lax.all_to_all(value, axis, 0, 0, axis_index_groups=groups, tiled=True)  44.5 us
    pallas_call x4, Pallas kernels, vmem_call(): pl.pallas_call(kernel, out_shape=out_shape, in_specs=specs or [vmem] * le...  26.9 us
    ppermute x9, starting transfers between devices, partner(): return lax.ppermute(value, 'pw', [(i, i ^ turn) for i in range(size)])  25.5 us
    all_to_all x5, waiting for transfers between devices, exchange(): lax.all_to_all(value, axis, 0, 0, axis_index_groups=groups, tiled=True)  18.4 us
    all_to_all x1, blocking collectives, exchange(): lax.all_to_all(value, axis, 0, 0, axis_index_groups=groups, tiled=True)  14.8 us
    ppermute x9, waiting for transfers between devices, partner(): return lax.ppermute(value, 'pw', [(i, i ^ turn) for i in range(size)])  7.26 us
    unnamed x26, local copies, waits for them, and re-layouts  3.4 us
  transfers between devices with their start and end apart: 15, of which 5 were waited for; matrix products, arithmetic and copies ran while one was open for 3% of the time, Pallas kernels for 15%

profile of v6, /device:TPU:1, one launch (start us, length us, event | category | flops | bytes accessed | tf_op | source)
XLA Modules:
  0.0 167.7 jit_solution(16709549232455892046)
XLA Ops:
  7.2 1.7 %shard_map.175 = bf16[4,5,40,128]{3,2,1,0:T(8,128)(2,1)} custom-call(s32[40]{0:T(128)} %cells_ref.1, bf16[8,2,40,128]{3,2,1,0:T(8,128)(2,1)} %block_ref.1, s32[40,128]{1,0:T(8,128)} %mask_ref.1), custom_call_target="tpu_custom_call" | custom-call | tf_op jit(solution)/shard_map/pallas_call | solution.py:305
  8.9 14.8 %all_to_all.30.part_ref = bf16[4,5,40,128]{3,2,1,0:T(8,128)(2,1)S(1)} all-to-all(bf16[4,5,40,128]{3,2,1,0:T(8,128)(2,1)} %shard_map.175), channel_id=1, replica_groups={{0,1,2,3},{4,5,6,7},{8,9,10,11},{12,13,14,15},{16,17,18,19},{20,21,22,2..., dimensions={0} | all-to-all | bytes 409600 | tf_op jit(solution)/shard_map/all_to_all | solution.py:403
  23.9 0.7 pad_maximum_fusion
  24.7 0.7 pad_maximum_fusion.2
  25.4 2.3 %shard_map.176 = (s16[16,48,128]{2,1,0:T(8,128)(2,1)}, bf16[512,128]{1,0:T(8,128)(2,1)}) custom-call(bf16[4,5,40,128]{3,2,1,0:T(8,128)(2,1)} %copy-done, bf16[256,256]{1,0:T(8,128)(2,1)} %constant.43.clone.high_ref, bf16[256,256]{1,0:T(8,128)(2,1)} %constant.44.clone.low_ref, bf16[512,128]{1,0:T(8,128)(2,1)} %bitcast.168), custom_call_target="tpu_custom_call", output_to_operand_aliasing={{1}: (3, {})} | custom-call | tf_op jit(solution)/shard_map/pallas_call | solution.py:305
  27.6 9.5 %all-to-all-start.1 = ((s16[16,48,128]{2,1,0:T(8,128)(2,1)}), s16[16,48,128]{2,1,0:T(8,128)(2,1)S(1)}, u32[]{:S(2)}, u32[]{:S(2)}) async-start(s16[16,48,128]{2,1,0:T(8,128)(2,1)} %get-tuple-element.9), calls=%async_computation.1 | async-start | bytes 393216 | tf_op jit(solution)/shard_map/all_to_all | solution.py:403
  37.3 0.3 fusion.13
  37.6 0.5 copy-done.2
  38.1 2.9 %collective-permute-start.2 = (bf16[512,128]{1,0:T(8,128)(2,1)S(1)}, bf16[512,128]{1,0:T(8,128)(2,1)S(1)}, u32[]{:S(2)}, u32[]{:S(2)}) collective-permute-start(bf16[512,128]{1,0:T(8,128)(2,1)S(1)} %copy-done.2), channel_id=1, source_target_pairs={{0,3},{1,2},{2,1},{3,0},{4,7},{5,6},{6,5},{7,4},{8,11},{9,10},{10,... | collective-permute-start | bytes 393224 | tf_op jit(solution)/shard_map/ppermute | solution.py:392
  41.0 3.3 %collective-permute-start.1 = (bf16[512,128]{1,0:T(8,128)(2,1)S(1)}, bf16[512,128]{1,0:T(8,128)(2,1)S(1)}, u32[]{:S(2)}, u32[]{:S(2)}) collective-permute-start(bf16[512,128]{1,0:T(8,128)(2,1)S(1)} %copy-done.2), channel_id=1, source_target_pairs={{0,2},{1,3},{2,0},{3,1},{4,6},{5,7},{6,4},{7,5},{8,10},{9,11},{10,... | collective-permute-start | bytes 393224 | tf_op jit(solution)/shard_map/ppermute | solution.py:392
  44.4 1.9 %collective-permute-start = (bf16[512,128]{1,0:T(8,128)(2,1)S(1)}, bf16[512,128]{1,0:T(8,128)(2,1)S(1)}, u32[]{:S(2)}, u32[]{:S(2)}) collective-permute-start(bf16[512,128]{1,0:T(8,128)(2,1)S(1)} %copy-done.2), channel_id=1, source_target_pairs={{0,1},{1,0},{2,3},{3,2},{4,5},{5,4},{6,7},{7,6},{8,9},{9,8},{10,11... | collective-permute-start | bytes 393224 | tf_op jit(solution)/shard_map/ppermute | solution.py:392
  46.3 0.3 fusion.6
  46.6 1.0 copy.81
  47.6 4.9 %collective-permute-done.1.v2_ref = bf16[512,128]{1,0:T(8,128)(2,1)S(1)} collective-permute-done((bf16[512,128]{1,0:T(8,128)(2,1)S(1)}, bf16[512,128]{1,0:T(8,128)(2,1)S(1)}, u32[]{:S(2)}, u32[]{:S(2)}) %collective-permute-start.1) | collective-permute-done | bytes 131104 | tf_op jit(solution)/shard_map/ppermute | solution.py:392
  52.5 0.6 copy-done.8
  53.3 20.2 %shard_map.177 = (s16[16,48,128]{2,1,0:T(8,128)(2,1)}, bf16[1280,128]{1,0:T(8,128)(2,1)}) custom-call(s32[1]{0:T(128)} %bitcast.me_ref, s16[16,48,128]{2,1,0:T(8,128)(2,1)} %copy-done.3, bf16[512,128]{1,0:T(8,128)(2,1)} %get-tuple-element.10.v0_ref, bf16[512,128]{1,0:T(8,128)(2,1)} %copy-done.9, ...), custom_call_target="tpu_custom_call", output_to_operand_aliasing={{1}: (13, {})} | custom-call | tf_op jit(solution)/shard_map/pallas_call | solution.py:305
  73.5 11.6 %all-to-all-start.2 = ((s16[16,48,128]{2,1,0:T(8,128)(2,1)}), s16[16,48,128]{2,1,0:T(8,128)(2,1)S(1)}, u32[]{:S(2)}, u32[]{:S(2)}) async-start(s16[16,48,128]{2,1,0:T(8,128)(2,1)} %get-tuple-element.11), calls=%async_computation.2 | async-start | bytes 393216 | tf_op jit(solution)/shard_map/all_to_all | solution.py:403
  85.1 1.9 %collective-permute-start.8 = (bf16[1280,128]{1,0:T(8,128)(2,1)}, bf16[1280,128]{1,0:T(8,128)(2,1)S(1)}, u32[]{:S(2)}, u32[]{:S(2)}) collective-permute-start(bf16[1280,128]{1,0:T(8,128)(2,1)} %get-tuple-element.13), channel_id=1, source_target_pairs={{0,1},{1,0},{2,3},{3,2},{4,5},{5,4},{6,7},{7,6},{8,9},{9,8},{10,11... | collective-permute-start | bytes 983048 | tf_op jit(solution)/shard_map/ppermute | solution.py:392
  87.1 3.2 %collective-permute-start.7 = (bf16[1280,128]{1,0:T(8,128)(2,1)}, bf16[1280,128]{1,0:T(8,128)(2,1)S(1)}, u32[]{:S(2)}, u32[]{:S(2)}) collective-permute-start(bf16[1280,128]{1,0:T(8,128)(2,1)} %get-tuple-element.13), channel_id=1, source_target_pairs={{0,2},{1,3},{2,0},{3,1},{4,6},{5,7},{6,4},{7,5},{8,10},{9,11},{10,... | collective-permute-start | bytes 983048 | tf_op jit(solution)/shard_map/ppermute | solution.py:392
  90.3 2.8 %collective-permute-start.6 = (bf16[1280,128]{1,0:T(8,128)(2,1)}, bf16[1280,128]{1,0:T(8,128)(2,1)S(1)}, u32[]{:S(2)}, u32[]{:S(2)}) collective-permute-start(bf16[1280,128]{1,0:T(8,128)(2,1)} %get-tuple-element.13), channel_id=1, source_target_pairs={{0,3},{1,2},{2,1},{3,0},{4,7},{5,6},{6,5},{7,4},{8,11},{9,10},{10,... | collective-permute-start | bytes 983048 | tf_op jit(solution)/shard_map/ppermute | solution.py:392
  93.0 6.1 %all-to-all-done.2.recv_ref = s16[16,48,128]{2,1,0:T(8,128)(2,1)S(1)} async-done(((s16[16,48,128]{2,1,0:T(8,128)(2,1)}), s16[16,48,128]{2,1,0:T(8,128)(2,1)S(1)}, u32[]{:S(2)}, u32[]{:S(2)}) %all-to-all-start.2) | async-done | bytes 196640 | tf_op jit(solution)/shard_map/all_to_all | solution.py:403
  99.2 0.7 copy-done.4
  99.9 2.7 %shard_map.178 = (bf16[4,4,40,128]{3,2,1,0:T(8,128)(2,1)}, bf16[8,320,128]{2,1,0:T(8,128)(2,1)}) custom-call(s16[16,48,128]{2,1,0:T(8,128)(2,1)} %copy-done.4, bf16[4,5,40,128]{3,2,1,0:T(8,128)(2,1)} %copy-done, bf16[256,256]{1,0:T(8,128)(2,1)} %constant.43.clone.high_ref, bf16[256,256]{1,0:T(8,128)(2,1)} %constant.44.clone.low_ref), custom_call_target="tpu_custom_call" | custom-call | tf_op jit(solution)/shard_map/pallas_call | solution.py:305
  102.6 5.5 %all-to-all-start.3 = ((bf16[8,320,128]{2,1,0:T(8,128)(2,1)}), bf16[8,320,128]{2,1,0:T(8,128)(2,1)S(1)}, u32[]{:S(2)}, u32[]{:S(2)}) async-start(bf16[8,320,128]{2,1,0:T(8,128)(2,1)} %get-tuple-element.14), calls=%async_computation.3 | async-start | bytes 1310720 | tf_op jit(solution)/shard_map/all_to_all | solution.py:403
  108.2 9.7 %all-to-all-done.3 = bf16[8,320,128]{2,1,0:T(8,128)(2,1)S(1)} async-done(((bf16[8,320,128]{2,1,0:T(8,128)(2,1)}), bf16[8,320,128]{2,1,0:T(8,128)(2,1)S(1)}, u32[]{:S(2)}, u32[]{:S(2)}) %all-to-all-start.3) | async-done | bytes 655392 | tf_op jit(solution)/shard_map/all_to_all | solution.py:403
  118.0 0.4 copy.91
  118.6 0.2 fusion.2
  119.6 1.4 slice_bitcast_fusion
  121.0 0.3 fusion.10
  121.3 0.5 slice_add_fusion
  121.8 0.5 fusion.12
  123.4 0.3 copy.99
  123.7 0.3 broadcast_in_dim.6
  124.0 0.7 broadcast_in_dim.7
  124.6 10.5 %all-to-all-start.4 = ((f32[16,16,128]{2,1,0:T(8,128)}), f32[16,16,128]{2,1,0:T(8,128)S(1)}, u32[]{:S(2)}, u32[]{:S(2)}) async-start(f32[16,16,128]{2,1,0:T(8,128)} %broadcast_in_dim.7), calls=%async_computation.4 | async-start | bytes 262144 | tf_op jit(solution)/shard_map/all_to_all | solution.py:403
  135.2 4.1 %collective-permute-start.5 = (bf16[4,40,128]{2,1,0:T(8,128)(2,1)S(1)}, bf16[4,40,128]{2,1,0:T(8,128)(2,1)S(1)}, u32[]{:S(2)}, u32[]{:S(2)}) collective-permute-start(bf16[4,40,128]{2,1,0:T(8,128)(2,1)S(1)} %get-tuple-element.42), channel_id=1, source_target_pairs={{0,1},{1,0},{2,3},{3,2},{4,5},{5,4},{6,7},{7,6},{8,9},{9,8},{10,11... | collective-permute-start | bytes 122888 | tf_op jit(solution)/shard_map/ppermute | solution.py:392
  139.3 2.2 %collective-permute-start.4 = (bf16[4,40,128]{2,1,0:T(8,128)(2,1)S(1)}, bf16[4,40,128]{2,1,0:T(8,128)(2,1)S(1)}, u32[]{:S(2)}, u32[]{:S(2)}) collective-permute-start(bf16[4,40,128]{2,1,0:T(8,128)(2,1)S(1)} %get-tuple-element.43), channel_id=1, source_target_pairs={{0,2},{1,3},{2,0},{3,1},{4,6},{5,7},{6,4},{7,5},{8,10},{9,11},{10,... | collective-permute-start | bytes 122888 | tf_op jit(solution)/shard_map/ppermute | solution.py:392
  141.5 3.3 %collective-permute-start.3 = (bf16[4,40,128]{2,1,0:T(8,128)(2,1)S(1)}, bf16[4,40,128]{2,1,0:T(8,128)(2,1)S(1)}, u32[]{:S(2)}, u32[]{:S(2)}) collective-permute-start(bf16[4,40,128]{2,1,0:T(8,128)(2,1)S(1)} %get-tuple-element.44), channel_id=1, source_target_pairs={{0,3},{1,2},{2,1},{3,0},{4,7},{5,6},{6,5},{7,4},{8,11},{9,10},{10,... | collective-permute-start | bytes 122888 | tf_op jit(solution)/shard_map/ppermute | solution.py:392
  144.8 2.4 %collective-permute-done.3 = bf16[4,40,128]{2,1,0:T(8,128)(2,1)S(1)} collective-permute-done((bf16[4,40,128]{2,1,0:T(8,128)(2,1)S(1)}, bf16[4,40,128]{2,1,0:T(8,128)(2,1)S(1)}, u32[]{:S(2)}, u32[]{:S(2)}) %collective-permute-start.3) | collective-permute-done | bytes 40992 | tf_op jit(solution)/shard_map/ppermute | solution.py:392
  147.2 0.6 broadcast_in_dim.16
  147.9 7.3 %all-to-all-start.5 = ((f32[4,16,128]{2,1,0:T(8,128)}), f32[4,16,128]{2,1,0:T(8,128)S(1)}, u32[]{:S(2)}, u32[]{:S(2)}) async-start(f32[4,16,128]{2,1,0:T(8,128)} %broadcast_in_dim.16), calls=%async_computation.5 | async-start | bytes 65536 | tf_op jit(solution)/shard_map/all_to_all | solution.py:403
  155.2 0.7 pad_maximum_fusion.1
  155.9 2.5 %all-to-all-done.5 = f32[4,16,128]{2,1,0:T(8,128)S(1)} async-done(((f32[4,16,128]{2,1,0:T(8,128)}), f32[4,16,128]{2,1,0:T(8,128)S(1)}, u32[]{:S(2)}, u32[]{:S(2)}) %all-to-all-start.5) | async-done | bytes 32800 | tf_op jit(solution)/shard_map/all_to_all | solution.py:403
  158.4 0.4 copy.100
  158.8 0.3 copy.102
  159.1 0.7 copy.104
  159.8 0.3 copy.101
  160.2 0.7 copy.103
  (60 shorter events, 2.7 us)
Async XLA Ops:
  7.2 17.5 %copy-start.11 = (s32[40,128]{1,0:T(8,128)S(1)}, s32[40,128]{1,0:T(8,128)}, u32[]{:S(2)}) copy-start(s32[40,128]{1,0:T(8,128)} %mask_ref.1) | copy-start | bytes 61444
  7.2 17.5 %copy-start.10 = (f32[2,128,128]{2,1,0:T(8,128)S(1)}, f32[2,128,128]{2,1,0:T(8,128)}, u32[]{:S(2)}) copy-start(f32[2,128,128]{2,1,0:T(8,128)} %param.18) | copy-start | bytes 393220
  7.2 112.4 %all-gather.2.cloned.1.call-start = ((), (), s32[]{:S(2)}) async-start(), calls=%async_computation.6 | async-start | bytes 2949120 | tf_op jit(solution)/shard_map/all_gather | solution.py:433
  23.8 1.6 copy-start
  23.8 13.4 %copy-start.5 = (bf16[32,2,40,128]{3,2,1,0:T(8,128)(2,1)S(1)}, bf16[32,2,40,128]{3,2,1,0:T(8,128)(2,1)}, u32[]{:S(2)}) copy-start(bf16[32,2,40,128]{3,2,1,0:T(8,128)(2,1)} %param.17) | copy-start | bytes 1966084
  27.6 24.9 %all-to-all-start.1 = ((s16[16,48,128]{2,1,0:T(8,128)(2,1)}), s16[16,48,128]{2,1,0:T(8,128)(2,1)S(1)}, u32[]{:S(2)}, u32[]{:S(2)}) async-start(s16[16,48,128]{2,1,0:T(8,128)(2,1)} %get-tuple-element.9), calls=%async_computation.1 | async-start | bytes 393216 | tf_op jit(solution)/shard_map/all_to_all | solution.py:403
  37.2 0.9 copy-start.2
  38.1 9.5 %collective-permute-start.2 = (bf16[512,128]{1,0:T(8,128)(2,1)S(1)}, bf16[512,128]{1,0:T(8,128)(2,1)S(1)}, u32[]{:S(2)}, u32[]{:S(2)}) collective-permute-start(bf16[512,128]{1,0:T(8,128)(2,1)S(1)} %copy-done.2), channel_id=1, source_target_pairs={{0,3},{1,2},{2,1},{3,0},{4,7},{5,6},{6,5},{7,4},{8,11},{9,10},{10,... | collective-permute-start | bytes 393224 | tf_op jit(solution)/shard_map/ppermute | solution.py:392
  41.0 11.5 %collective-permute-start.1 = (bf16[512,128]{1,0:T(8,128)(2,1)S(1)}, bf16[512,128]{1,0:T(8,128)(2,1)S(1)}, u32[]{:S(2)}, u32[]{:S(2)}) collective-permute-start(bf16[512,128]{1,0:T(8,128)(2,1)S(1)} %copy-done.2), channel_id=1, source_target_pairs={{0,2},{1,3},{2,0},{3,1},{4,6},{5,7},{6,4},{7,5},{8,10},{9,11},{10,... | collective-permute-start | bytes 393224 | tf_op jit(solution)/shard_map/ppermute | solution.py:392
  44.4 8.2 %collective-permute-start = (bf16[512,128]{1,0:T(8,128)(2,1)S(1)}, bf16[512,128]{1,0:T(8,128)(2,1)S(1)}, u32[]{:S(2)}, u32[]{:S(2)}) collective-permute-start(bf16[512,128]{1,0:T(8,128)(2,1)S(1)} %copy-done.2), channel_id=1, source_target_pairs={{0,1},{1,0},{2,3},{3,2},{4,5},{5,4},{6,7},{7,6},{8,9},{9,8},{10,11... | collective-permute-start | bytes 393224 | tf_op jit(solution)/shard_map/ppermute | solution.py:392
  47.6 4.9 %copy-start.7 = (bf16[512,128]{1,0:T(8,128)(2,1)}, bf16[512,128]{1,0:T(8,128)(2,1)S(1)}, u32[]{:S(2)}) copy-start(bf16[512,128]{1,0:T(8,128)(2,1)S(1)} %collective-permute-done.2.v3_ref) | copy-start | bytes 393220
  52.5 0.6 copy-start.8
  52.5 0.7 copy-start.9
  52.5 0.8 copy-start.3
  73.5 34.6 %copy-start.1 = (bf16[1280,128]{1,0:T(8,128)(2,1)S(1)}, bf16[1280,128]{1,0:T(8,128)(2,1)}, u32[]{:S(2)}) copy-start(bf16[1280,128]{1,0:T(8,128)(2,1)} %get-tuple-element.13) | copy-start | bytes 983044
  73.5 25.6 %all-to-all-start.2 = ((s16[16,48,128]{2,1,0:T(8,128)(2,1)}), s16[16,48,128]{2,1,0:T(8,128)(2,1)S(1)}, u32[]{:S(2)}, u32[]{:S(2)}) async-start(s16[16,48,128]{2,1,0:T(8,128)(2,1)} %get-tuple-element.11), calls=%async_computation.2 | async-start | bytes 393216 | tf_op jit(solution)/shard_map/all_to_all | solution.py:403
  85.1 22.9 %collective-permute-start.8 = (bf16[1280,128]{1,0:T(8,128)(2,1)}, bf16[1280,128]{1,0:T(8,128)(2,1)S(1)}, u32[]{:S(2)}, u32[]{:S(2)}) collective-permute-start(bf16[1280,128]{1,0:T(8,128)(2,1)} %get-tuple-element.13), channel_id=1, source_target_pairs={{0,1},{1,0},{2,3},{3,2},{4,5},{5,4},{6,7},{7,6},{8,9},{9,8},{10,11... | collective-permute-start | bytes 983048 | tf_op jit(solution)/shard_map/ppermute | solution.py:392
  87.1 21.0 %collective-permute-start.7 = (bf16[1280,128]{1,0:T(8,128)(2,1)}, bf16[1280,128]{1,0:T(8,128)(2,1)S(1)}, u32[]{:S(2)}, u32[]{:S(2)}) collective-permute-start(bf16[1280,128]{1,0:T(8,128)(2,1)} %get-tuple-element.13), channel_id=1, source_target_pairs={{0,2},{1,3},{2,0},{3,1},{4,6},{5,7},{6,4},{7,5},{8,10},{9,11},{10,... | collective-permute-start | bytes 983048 | tf_op jit(solution)/shard_map/ppermute | solution.py:392
  90.3 17.8 %collective-permute-start.6 = (bf16[1280,128]{1,0:T(8,128)(2,1)}, bf16[1280,128]{1,0:T(8,128)(2,1)S(1)}, u32[]{:S(2)}, u32[]{:S(2)}) collective-permute-start(bf16[1280,128]{1,0:T(8,128)(2,1)} %get-tuple-element.13), channel_id=1, source_target_pairs={{0,3},{1,2},{2,1},{3,0},{4,7},{5,6},{6,5},{7,4},{8,11},{9,10},{10,... | collective-permute-start | bytes 983048 | tf_op jit(solution)/shard_map/ppermute | solution.py:392
  99.2 0.7 copy-start.4
  102.6 15.4 %all-to-all-start.3 = ((bf16[8,320,128]{2,1,0:T(8,128)(2,1)}), bf16[8,320,128]{2,1,0:T(8,128)(2,1)S(1)}, u32[]{:S(2)}, u32[]{:S(2)}) async-start(bf16[8,320,128]{2,1,0:T(8,128)(2,1)} %get-tuple-element.14), calls=%async_computation.3 | async-start | bytes 1310720 | tf_op jit(solution)/shard_map/all_to_all | solution.py:403
  122.9 12.3 %copy-start.6 = (bf16[4,4,40,128]{3,2,1,0:T(8,128)(2,1)S(1)}, bf16[4,4,40,128]{3,2,1,0:T(8,128)(2,1)}, u32[]{:S(2)}) copy-start(bf16[4,4,40,128]{3,2,1,0:T(8,128)(2,1)} %get-tuple-element.12) | copy-start | bytes 491524
  124.6 22.6 %all-to-all-start.4 = ((f32[16,16,128]{2,1,0:T(8,128)}), f32[16,16,128]{2,1,0:T(8,128)S(1)}, u32[]{:S(2)}, u32[]{:S(2)}) async-start(f32[16,16,128]{2,1,0:T(8,128)} %broadcast_in_dim.7), calls=%async_computation.4 | async-start | bytes 262144 | tf_op jit(solution)/shard_map/all_to_all | solution.py:403
  135.2 9.6 %collective-permute-start.5 = (bf16[4,40,128]{2,1,0:T(8,128)(2,1)S(1)}, bf16[4,40,128]{2,1,0:T(8,128)(2,1)S(1)}, u32[]{:S(2)}, u32[]{:S(2)}) collective-permute-start(bf16[4,40,128]{2,1,0:T(8,128)(2,1)S(1)} %get-tuple-element.42), channel_id=1, source_target_pairs={{0,1},{1,0},{2,3},{3,2},{4,5},{5,4},{6,7},{7,6},{8,9},{9,8},{10,11... | collective-permute-start | bytes 122888 | tf_op jit(solution)/shard_map/ppermute | solution.py:392
  139.3 5.5 %collective-permute-start.4 = (bf16[4,40,128]{2,1,0:T(8,128)(2,1)S(1)}, bf16[4,40,128]{2,1,0:T(8,128)(2,1)S(1)}, u32[]{:S(2)}, u32[]{:S(2)}) collective-permute-start(bf16[4,40,128]{2,1,0:T(8,128)(2,1)S(1)} %get-tuple-element.43), channel_id=1, source_target_pairs={{0,2},{1,3},{2,0},{3,1},{4,6},{5,7},{6,4},{7,5},{8,10},{9,11},{10,... | collective-permute-start | bytes 122888 | tf_op jit(solution)/shard_map/ppermute | solution.py:392
  141.5 5.7 %collective-permute-start.3 = (bf16[4,40,128]{2,1,0:T(8,128)(2,1)S(1)}, bf16[4,40,128]{2,1,0:T(8,128)(2,1)S(1)}, u32[]{:S(2)}, u32[]{:S(2)}) collective-permute-start(bf16[4,40,128]{2,1,0:T(8,128)(2,1)S(1)} %get-tuple-element.44), channel_id=1, source_target_pairs={{0,3},{1,2},{2,1},{3,0},{4,7},{5,6},{6,5},{7,4},{8,11},{9,10},{10,... | collective-permute-start | bytes 122888 | tf_op jit(solution)/shard_map/ppermute | solution.py:392
  147.9 10.5 %all-to-all-start.5 = ((f32[4,16,128]{2,1,0:T(8,128)}), f32[4,16,128]{2,1,0:T(8,128)S(1)}, u32[]{:S(2)}, u32[]{:S(2)}) async-start(f32[4,16,128]{2,1,0:T(8,128)} %broadcast_in_dim.16), calls=%async_computation.5 | async-start | bytes 65536 | tf_op jit(solution)/shard_map/all_to_all | solution.py:403
Sparse Core Ops, SparseCore 0:
  24.8 76.9 all-gather.1

commit v7 on v6

--- a/solution.py
+++ b/solution.py
@@ -214,9 +214,10 @@
     me = me_ref[0]
     for copy in copies:
         copy.wait()
-    for turn in range(GROUP):
+    for owner in range(GROUP):
+        turn = jnp.bitwise_xor(me, owner)
         for i in range(2):
-            z = 2 * jnp.bitwise_xor(me, turn) + i
+            z = 2 * owner + i
             at = i * NG
             potential = dot(v_ref[turn, at : at + NG, :], order_ref[...])
             potential += dot(v_ref[turn, at + 2 * NG : at + 3 * NG, :], order_ref[...])

time: 169 us -> 169 us (level)
  no operation moved by 1% of the time
where the time goes in v7:
time: 169 us; the launch traced here: 168 us
  starting transfers between devices  70.1 us (41%)
  Pallas kernels  26.9 us (16%)
  waiting for transfers between devices  25.6 us (15%)
  blocking collectives  14.8 us (9%)
  between operations  14.5 us (9%)
  local copies, waits for them, and re-layouts  10.8 us (6%)
  other arithmetic  3.25 us (2%)
    all_to_all x5, starting transfers between devices, exchange(): lax.all_to_all(value, axis, 0, 0, axis_index_groups=groups, tiled=True)  44.5 us
    pallas_call x4, Pallas kernels, vmem_call(): pl.pallas_call(kernel, out_shape=out_shape, in_specs=specs or [vmem] * le...  26.9 us
    ppermute x9, starting transfers between devices, partner(): return lax.ppermute(value, 'pw', [(i, i ^ turn) for i in range(size)])  25.6 us
    all_to_all x5, waiting for transfers between devices, exchange(): lax.all_to_all(value, axis, 0, 0, axis_index_groups=groups, tiled=True)  18.3 us
    all_to_all x1, blocking collectives, exchange(): lax.all_to_all(value, axis, 0, 0, axis_index_groups=groups, tiled=True)  14.8 us
    ppermute x9, waiting for transfers between devices, partner(): return lax.ppermute(value, 'pw', [(i, i ^ turn) for i in range(size)])  7.26 us
    unnamed x26, local copies, waits for them, and re-layouts  3.4 us
  transfers between devices with their start and end apart: 15, of which 5 were waited for; matrix products, arithmetic and copies ran while one was open for 3% of the time, Pallas kernels for 15%

profile of v7, /device:TPU:1, one launch (start us, length us, event | category | flops | bytes accessed | tf_op | source)
XLA Modules:
  0.0 167.7 jit_solution(4612463306590046116)
XLA Ops:
  7.2 1.7 %shard_map.175 = bf16[4,5,40,128]{3,2,1,0:T(8,128)(2,1)} custom-call(s32[40]{0:T(128)} %cells_ref.1, bf16[8,2,40,128]{3,2,1,0:T(8,128)(2,1)} %block_ref.1, s32[40,128]{1,0:T(8,128)} %mask_ref.1), custom_call_target="tpu_custom_call" | custom-call | tf_op jit(solution)/shard_map/pallas_call | solution.py:306
  8.9 14.8 %all_to_all.30.part_ref = bf16[4,5,40,128]{3,2,1,0:T(8,128)(2,1)S(1)} all-to-all(bf16[4,5,40,128]{3,2,1,0:T(8,128)(2,1)} %shard_map.175), channel_id=1, replica_groups={{0,1,2,3},{4,5,6,7},{8,9,10,11},{12,13,14,15},{16,17,18,19},{20,21,22,2..., dimensions={0} | all-to-all | bytes 409600 | tf_op jit(solution)/shard_map/all_to_all | solution.py:404
  23.9 0.7 pad_maximum_fusion
  24.7 0.7 pad_maximum_fusion.2
  25.4 2.3 %shard_map.176 = (s16[16,48,128]{2,1,0:T(8,128)(2,1)}, bf16[512,128]{1,0:T(8,128)(2,1)}) custom-call(bf16[4,5,40,128]{3,2,1,0:T(8,128)(2,1)} %copy-done, bf16[256,256]{1,0:T(8,128)(2,1)} %constant.43.clone.high_ref, bf16[256,256]{1,0:T(8,128)(2,1)} %constant.44.clone.low_ref, bf16[512,128]{1,0:T(8,128)(2,1)} %bitcast.168), custom_call_target="tpu_custom_call", output_to_operand_aliasing={{1}: (3, {})} | custom-call | tf_op jit(solution)/shard_map/pallas_call | solution.py:306
  27.6 9.5 %all-to-all-start.1 = ((s16[16,48,128]{2,1,0:T(8,128)(2,1)}), s16[16,48,128]{2,1,0:T(8,128)(2,1)S(1)}, u32[]{:S(2)}, u32[]{:S(2)}) async-start(s16[16,48,128]{2,1,0:T(8,128)(2,1)} %get-tuple-element.9), calls=%async_computation.1 | async-start | bytes 393216 | tf_op jit(solution)/shard_map/all_to_all | solution.py:404
  37.3 0.3 fusion.13
  37.6 0.5 copy-done.2
  38.1 2.9 %collective-permute-start.2 = (bf16[512,128]{1,0:T(8,128)(2,1)S(1)}, bf16[512,128]{1,0:T(8,128)(2,1)S(1)}, u32[]{:S(2)}, u32[]{:S(2)}) collective-permute-start(bf16[512,128]{1,0:T(8,128)(2,1)S(1)} %copy-done.2), channel_id=1, source_target_pairs={{0,3},{1,2},{2,1},{3,0},{4,7},{5,6},{6,5},{7,4},{8,11},{9,10},{10,... | collective-permute-start | bytes 393224 | tf_op jit(solution)/shard_map/ppermute | solution.py:393
  41.0 3.3 %collective-permute-start.1 = (bf16[512,128]{1,0:T(8,128)(2,1)S(1)}, bf16[512,128]{1,0:T(8,128)(2,1)S(1)}, u32[]{:S(2)}, u32[]{:S(2)}) collective-permute-start(bf16[512,128]{1,0:T(8,128)(2,1)S(1)} %copy-done.2), channel_id=1, source_target_pairs={{0,2},{1,3},{2,0},{3,1},{4,6},{5,7},{6,4},{7,5},{8,10},{9,11},{10,... | collective-permute-start | bytes 393224 | tf_op jit(solution)/shard_map/ppermute | solution.py:393
  44.4 1.9 %collective-permute-start = (bf16[512,128]{1,0:T(8,128)(2,1)S(1)}, bf16[512,128]{1,0:T(8,128)(2,1)S(1)}, u32[]{:S(2)}, u32[]{:S(2)}) collective-permute-start(bf16[512,128]{1,0:T(8,128)(2,1)S(1)} %copy-done.2), channel_id=1, source_target_pairs={{0,1},{1,0},{2,3},{3,2},{4,5},{5,4},{6,7},{7,6},{8,9},{9,8},{10,11... | collective-permute-start | bytes 393224 | tf_op jit(solution)/shard_map/ppermute | solution.py:393
  46.3 0.3 fusion.6
  46.6 1.0 copy.81
  47.6 4.9 %collective-permute-done.1.v2_ref = bf16[512,128]{1,0:T(8,128)(2,1)S(1)} collective-permute-done((bf16[512,128]{1,0:T(8,128)(2,1)S(1)}, bf16[512,128]{1,0:T(8,128)(2,1)S(1)}, u32[]{:S(2)}, u32[]{:S(2)}) %collective-permute-start.1) | collective-permute-done | bytes 131104 | tf_op jit(solution)/shard_map/ppermute | solution.py:393
  52.5 0.6 copy-done.8
  53.3 20.2 %shard_map.177 = (s16[16,48,128]{2,1,0:T(8,128)(2,1)}, bf16[1280,128]{1,0:T(8,128)(2,1)}) custom-call(s32[1]{0:T(128)} %bitcast.me_ref, s16[16,48,128]{2,1,0:T(8,128)(2,1)} %copy-done.3, bf16[512,128]{1,0:T(8,128)(2,1)} %get-tuple-element.10.v0_ref, bf16[512,128]{1,0:T(8,128)(2,1)} %copy-done.9, ...), custom_call_target="tpu_custom_call", output_to_operand_aliasing={{1}: (13, {})} | custom-call | tf_op jit(solution)/shard_map/pallas_call | solution.py:306
  73.5 11.6 %all-to-all-start.2 = ((s16[16,48,128]{2,1,0:T(8,128)(2,1)}), s16[16,48,128]{2,1,0:T(8,128)(2,1)S(1)}, u32[]{:S(2)}, u32[]{:S(2)}) async-start(s16[16,48,128]{2,1,0:T(8,128)(2,1)} %get-tuple-element.11), calls=%async_computation.2 | async-start | bytes 393216 | tf_op jit(solution)/shard_map/all_to_all | solution.py:404
  85.1 1.9 %collective-permute-start.8 = (bf16[1280,128]{1,0:T(8,128)(2,1)}, bf16[1280,128]{1,0:T(8,128)(2,1)S(1)}, u32[]{:S(2)}, u32[]{:S(2)}) collective-permute-start(bf16[1280,128]{1,0:T(8,128)(2,1)} %get-tuple-element.13), channel_id=1, source_target_pairs={{0,1},{1,0},{2,3},{3,2},{4,5},{5,4},{6,7},{7,6},{8,9},{9,8},{10,11... | collective-permute-start | bytes 983048 | tf_op jit(solution)/shard_map/ppermute | solution.py:393
  87.1 3.2 %collective-permute-start.7 = (bf16[1280,128]{1,0:T(8,128)(2,1)}, bf16[1280,128]{1,0:T(8,128)(2,1)S(1)}, u32[]{:S(2)}, u32[]{:S(2)}) collective-permute-start(bf16[1280,128]{1,0:T(8,128)(2,1)} %get-tuple-element.13), channel_id=1, source_target_pairs={{0,2},{1,3},{2,0},{3,1},{4,6},{5,7},{6,4},{7,5},{8,10},{9,11},{10,... | collective-permute-start | bytes 983048 | tf_op jit(solution)/shard_map/ppermute | solution.py:393
  90.3 2.7 %collective-permute-start.6 = (bf16[1280,128]{1,0:T(8,128)(2,1)}, bf16[1280,128]{1,0:T(8,128)(2,1)S(1)}, u32[]{:S(2)}, u32[]{:S(2)}) collective-permute-start(bf16[1280,128]{1,0:T(8,128)(2,1)} %get-tuple-element.13), channel_id=1, source_target_pairs={{0,3},{1,2},{2,1},{3,0},{4,7},{5,6},{6,5},{7,4},{8,11},{9,10},{10,... | collective-permute-start | bytes 983048 | tf_op jit(solution)/shard_map/ppermute | solution.py:393
  93.0 6.1 %all-to-all-done.2.recv_ref = s16[16,48,128]{2,1,0:T(8,128)(2,1)S(1)} async-done(((s16[16,48,128]{2,1,0:T(8,128)(2,1)}), s16[16,48,128]{2,1,0:T(8,128)(2,1)S(1)}, u32[]{:S(2)}, u32[]{:S(2)}) %all-to-all-start.2) | async-done | bytes 196640 | tf_op jit(solution)/shard_map/all_to_all | solution.py:404
  99.1 0.7 copy-done.4
  99.8 2.7 %shard_map.178 = (bf16[4,4,40,128]{3,2,1,0:T(8,128)(2,1)}, bf16[8,320,128]{2,1,0:T(8,128)(2,1)}) custom-call(s16[16,48,128]{2,1,0:T(8,128)(2,1)} %copy-done.4, bf16[4,5,40,128]{3,2,1,0:T(8,128)(2,1)} %copy-done, bf16[256,256]{1,0:T(8,128)(2,1)} %constant.43.clone.high_ref, bf16[256,256]{1,0:T(8,128)(2,1)} %constant.44.clone.low_ref), custom_call_target="tpu_custom_call" | custom-call | tf_op jit(solution)/shard_map/pallas_call | solution.py:306
  102.6 5.5 %all-to-all-start.3 = ((bf16[8,320,128]{2,1,0:T(8,128)(2,1)}), bf16[8,320,128]{2,1,0:T(8,128)(2,1)S(1)}, u32[]{:S(2)}, u32[]{:S(2)}) async-start(bf16[8,320,128]{2,1,0:T(8,128)(2,1)} %get-tuple-element.14), calls=%async_computation.3 | async-start | bytes 1310720 | tf_op jit(solution)/shard_map/all_to_all | solution.py:404
  108.2 9.7 %all-to-all-done.3 = bf16[8,320,128]{2,1,0:T(8,128)(2,1)S(1)} async-done(((bf16[8,320,128]{2,1,0:T(8,128)(2,1)}), bf16[8,320,128]{2,1,0:T(8,128)(2,1)S(1)}, u32[]{:S(2)}, u32[]{:S(2)}) %all-to-all-start.3) | async-done | bytes 655392 | tf_op jit(solution)/shard_map/all_to_all | solution.py:404
  118.0 0.4 copy.91
  118.6 0.2 fusion.2
  119.6 1.4 slice_bitcast_fusion
  121.0 0.3 fusion.10
  121.3 0.5 slice_add_fusion
  121.8 0.5 fusion.12
  123.4 0.3 copy.99
  123.7 0.3 broadcast_in_dim.6
  124.0 0.7 broadcast_in_dim.7
  124.7 10.5 %all-to-all-start.4 = ((f32[16,16,128]{2,1,0:T(8,128)}), f32[16,16,128]{2,1,0:T(8,128)S(1)}, u32[]{:S(2)}, u32[]{:S(2)}) async-start(f32[16,16,128]{2,1,0:T(8,128)} %broadcast_in_dim.7), calls=%async_computation.4 | async-start | bytes 262144 | tf_op jit(solution)/shard_map/all_to_all | solution.py:404
  135.2 4.1 %collective-permute-start.5 = (bf16[4,40,128]{2,1,0:T(8,128)(2,1)S(1)}, bf16[4,40,128]{2,1,0:T(8,128)(2,1)S(1)}, u32[]{:S(2)}, u32[]{:S(2)}) collective-permute-start(bf16[4,40,128]{2,1,0:T(8,128)(2,1)S(1)} %get-tuple-element.42), channel_id=1, source_target_pairs={{0,1},{1,0},{2,3},{3,2},{4,5},{5,4},{6,7},{7,6},{8,9},{9,8},{10,11... | collective-permute-start | bytes 122888 | tf_op jit(solution)/shard_map/ppermute | solution.py:393
  139.3 2.2 %collective-permute-start.4 = (bf16[4,40,128]{2,1,0:T(8,128)(2,1)S(1)}, bf16[4,40,128]{2,1,0:T(8,128)(2,1)S(1)}, u32[]{:S(2)}, u32[]{:S(2)}) collective-permute-start(bf16[4,40,128]{2,1,0:T(8,128)(2,1)S(1)} %get-tuple-element.43), channel_id=1, source_target_pairs={{0,2},{1,3},{2,0},{3,1},{4,6},{5,7},{6,4},{7,5},{8,10},{9,11},{10,... | collective-permute-start | bytes 122888 | tf_op jit(solution)/shard_map/ppermute | solution.py:393
  141.5 3.3 %collective-permute-start.3 = (bf16[4,40,128]{2,1,0:T(8,128)(2,1)S(1)}, bf16[4,40,128]{2,1,0:T(8,128)(2,1)S(1)}, u32[]{:S(2)}, u32[]{:S(2)}) collective-permute-start(bf16[4,40,128]{2,1,0:T(8,128)(2,1)S(1)} %get-tuple-element.44), channel_id=1, source_target_pairs={{0,3},{1,2},{2,1},{3,0},{4,7},{5,6},{6,5},{7,4},{8,11},{9,10},{10,... | collective-permute-start | bytes 122888 | tf_op jit(solution)/shard_map/ppermute | solution.py:393
  144.8 2.4 %collective-permute-done.3 = bf16[4,40,128]{2,1,0:T(8,128)(2,1)S(1)} collective-permute-done((bf16[4,40,128]{2,1,0:T(8,128)(2,1)S(1)}, bf16[4,40,128]{2,1,0:T(8,128)(2,1)S(1)}, u32[]{:S(2)}, u32[]{:S(2)}) %collective-permute-start.3) | collective-permute-done | bytes 40992 | tf_op jit(solution)/shard_map/ppermute | solution.py:393
  147.2 0.6 broadcast_in_dim.16
  147.9 7.3 %all-to-all-start.5 = ((f32[4,16,128]{2,1,0:T(8,128)}), f32[4,16,128]{2,1,0:T(8,128)S(1)}, u32[]{:S(2)}, u32[]{:S(2)}) async-start(f32[4,16,128]{2,1,0:T(8,128)} %broadcast_in_dim.16), calls=%async_computation.5 | async-start | bytes 65536 | tf_op jit(solution)/shard_map/all_to_all | solution.py:404
  155.2 0.7 pad_maximum_fusion.1
  155.9 2.5 %all-to-all-done.5 = f32[4,16,128]{2,1,0:T(8,128)S(1)} async-done(((f32[4,16,128]{2,1,0:T(8,128)}), f32[4,16,128]{2,1,0:T(8,128)S(1)}, u32[]{:S(2)}, u32[]{:S(2)}) %all-to-all-start.5) | async-done | bytes 32800 | tf_op jit(solution)/shard_map/all_to_all | solution.py:404
  158.3 0.4 copy.100
  158.8 0.3 copy.102
  159.1 0.7 copy.104
  159.8 0.3 copy.101
  160.2 0.7 copy.103
  (60 shorter events, 2.7 us)
Async XLA Ops:
  7.2 17.5 %copy-start.11 = (s32[40,128]{1,0:T(8,128)S(1)}, s32[40,128]{1,0:T(8,128)}, u32[]{:S(2)}) copy-start(s32[40,128]{1,0:T(8,128)} %mask_ref.1) | copy-start | bytes 61444
  7.2 17.5 %copy-start.10 = (f32[2,128,128]{2,1,0:T(8,128)S(1)}, f32[2,128,128]{2,1,0:T(8,128)}, u32[]{:S(2)}) copy-start(f32[2,128,128]{2,1,0:T(8,128)} %param.18) | copy-start | bytes 393220
  7.2 112.4 %all-gather.2.cloned.1.call-start = ((), (), s32[]{:S(2)}) async-start(), calls=%async_computation.6 | async-start | bytes 2949120 | tf_op jit(solution)/shard_map/all_gather | solution.py:434
  23.8 1.6 copy-start
  23.8 13.4 %copy-start.5 = (bf16[32,2,40,128]{3,2,1,0:T(8,128)(2,1)S(1)}, bf16[32,2,40,128]{3,2,1,0:T(8,128)(2,1)}, u32[]{:S(2)}) copy-start(bf16[32,2,40,128]{3,2,1,0:T(8,128)(2,1)} %param.17) | copy-start | bytes 1966084
  27.6 24.9 %all-to-all-start.1 = ((s16[16,48,128]{2,1,0:T(8,128)(2,1)}), s16[16,48,128]{2,1,0:T(8,128)(2,1)S(1)}, u32[]{:S(2)}, u32[]{:S(2)}) async-start(s16[16,48,128]{2,1,0:T(8,128)(2,1)} %get-tuple-element.9), calls=%async_computation.1 | async-start | bytes 393216 | tf_op jit(solution)/shard_map/all_to_all | solution.py:404
  37.2 0.9 copy-start.2
  38.1 9.5 %collective-permute-start.2 = (bf16[512,128]{1,0:T(8,128)(2,1)S(1)}, bf16[512,128]{1,0:T(8,128)(2,1)S(1)}, u32[]{:S(2)}, u32[]{:S(2)}) collective-permute-start(bf16[512,128]{1,0:T(8,128)(2,1)S(1)} %copy-done.2), channel_id=1, source_target_pairs={{0,3},{1,2},{2,1},{3,0},{4,7},{5,6},{6,5},{7,4},{8,11},{9,10},{10,... | collective-permute-start | bytes 393224 | tf_op jit(solution)/shard_map/ppermute | solution.py:393
  41.0 11.5 %collective-permute-start.1 = (bf16[512,128]{1,0:T(8,128)(2,1)S(1)}, bf16[512,128]{1,0:T(8,128)(2,1)S(1)}, u32[]{:S(2)}, u32[]{:S(2)}) collective-permute-start(bf16[512,128]{1,0:T(8,128)(2,1)S(1)} %copy-done.2), channel_id=1, source_target_pairs={{0,2},{1,3},{2,0},{3,1},{4,6},{5,7},{6,4},{7,5},{8,10},{9,11},{10,... | collective-permute-start | bytes 393224 | tf_op jit(solution)/shard_map/ppermute | solution.py:393
  44.4 8.2 %collective-permute-start = (bf16[512,128]{1,0:T(8,128)(2,1)S(1)}, bf16[512,128]{1,0:T(8,128)(2,1)S(1)}, u32[]{:S(2)}, u32[]{:S(2)}) collective-permute-start(bf16[512,128]{1,0:T(8,128)(2,1)S(1)} %copy-done.2), channel_id=1, source_target_pairs={{0,1},{1,0},{2,3},{3,2},{4,5},{5,4},{6,7},{7,6},{8,9},{9,8},{10,11... | collective-permute-start | bytes 393224 | tf_op jit(solution)/shard_map/ppermute | solution.py:393
  47.6 4.9 %copy-start.7 = (bf16[512,128]{1,0:T(8,128)(2,1)}, bf16[512,128]{1,0:T(8,128)(2,1)S(1)}, u32[]{:S(2)}) copy-start(bf16[512,128]{1,0:T(8,128)(2,1)S(1)} %collective-permute-done.2.v3_ref) | copy-start | bytes 393220
  52.5 0.6 copy-start.8
  52.5 0.7 copy-start.9
  52.5 0.8 copy-start.3
  73.5 34.6 %copy-start.1 = (bf16[1280,128]{1,0:T(8,128)(2,1)S(1)}, bf16[1280,128]{1,0:T(8,128)(2,1)}, u32[]{:S(2)}) copy-start(bf16[1280,128]{1,0:T(8,128)(2,1)} %get-tuple-element.13) | copy-start | bytes 983044
  73.5 25.6 %all-to-all-start.2 = ((s16[16,48,128]{2,1,0:T(8,128)(2,1)}), s16[16,48,128]{2,1,0:T(8,128)(2,1)S(1)}, u32[]{:S(2)}, u32[]{:S(2)}) async-start(s16[16,48,128]{2,1,0:T(8,128)(2,1)} %get-tuple-element.11), calls=%async_computation.2 | async-start | bytes 393216 | tf_op jit(solution)/shard_map/all_to_all | solution.py:404
  85.1 22.9 %collective-permute-start.8 = (bf16[1280,128]{1,0:T(8,128)(2,1)}, bf16[1280,128]{1,0:T(8,128)(2,1)S(1)}, u32[]{:S(2)}, u32[]{:S(2)}) collective-permute-start(bf16[1280,128]{1,0:T(8,128)(2,1)} %get-tuple-element.13), channel_id=1, source_target_pairs={{0,1},{1,0},{2,3},{3,2},{4,5},{5,4},{6,7},{7,6},{8,9},{9,8},{10,11... | collective-permute-start | bytes 983048 | tf_op jit(solution)/shard_map/ppermute | solution.py:393
  87.1 21.0 %collective-permute-start.7 = (bf16[1280,128]{1,0:T(8,128)(2,1)}, bf16[1280,128]{1,0:T(8,128)(2,1)S(1)}, u32[]{:S(2)}, u32[]{:S(2)}) collective-permute-start(bf16[1280,128]{1,0:T(8,128)(2,1)} %get-tuple-element.13), channel_id=1, source_target_pairs={{0,2},{1,3},{2,0},{3,1},{4,6},{5,7},{6,4},{7,5},{8,10},{9,11},{10,... | collective-permute-start | bytes 983048 | tf_op jit(solution)/shard_map/ppermute | solution.py:393
  90.3 17.8 %collective-permute-start.6 = (bf16[1280,128]{1,0:T(8,128)(2,1)}, bf16[1280,128]{1,0:T(8,128)(2,1)S(1)}, u32[]{:S(2)}, u32[]{:S(2)}) collective-permute-start(bf16[1280,128]{1,0:T(8,128)(2,1)} %get-tuple-element.13), channel_id=1, source_target_pairs={{0,3},{1,2},{2,1},{3,0},{4,7},{5,6},{6,5},{7,4},{8,11},{9,10},{10,... | collective-permute-start | bytes 983048 | tf_op jit(solution)/shard_map/ppermute | solution.py:393
  99.1 0.7 copy-start.4
  102.6 15.4 %all-to-all-start.3 = ((bf16[8,320,128]{2,1,0:T(8,128)(2,1)}), bf16[8,320,128]{2,1,0:T(8,128)(2,1)S(1)}, u32[]{:S(2)}, u32[]{:S(2)}) async-start(bf16[8,320,128]{2,1,0:T(8,128)(2,1)} %get-tuple-element.14), calls=%async_computation.3 | async-start | bytes 1310720 | tf_op jit(solution)/shard_map/all_to_all | solution.py:404
  122.9 12.3 %copy-start.6 = (bf16[4,4,40,128]{3,2,1,0:T(8,128)(2,1)S(1)}, bf16[4,4,40,128]{3,2,1,0:T(8,128)(2,1)}, u32[]{:S(2)}) copy-start(bf16[4,4,40,128]{3,2,1,0:T(8,128)(2,1)} %get-tuple-element.12) | copy-start | bytes 491524
  124.7 22.6 %all-to-all-start.4 = ((f32[16,16,128]{2,1,0:T(8,128)}), f32[16,16,128]{2,1,0:T(8,128)S(1)}, u32[]{:S(2)}, u32[]{:S(2)}) async-start(f32[16,16,128]{2,1,0:T(8,128)} %broadcast_in_dim.7), calls=%async_computation.4 | async-start | bytes 262144 | tf_op jit(solution)/shard_map/all_to_all | solution.py:404
  135.2 9.6 %collective-permute-start.5 = (bf16[4,40,128]{2,1,0:T(8,128)(2,1)S(1)}, bf16[4,40,128]{2,1,0:T(8,128)(2,1)S(1)}, u32[]{:S(2)}, u32[]{:S(2)}) collective-permute-start(bf16[4,40,128]{2,1,0:T(8,128)(2,1)S(1)} %get-tuple-element.42), channel_id=1, source_target_pairs={{0,1},{1,0},{2,3},{3,2},{4,5},{5,4},{6,7},{7,6},{8,9},{9,8},{10,11... | collective-permute-start | bytes 122888 | tf_op jit(solution)/shard_map/ppermute | solution.py:393
  139.3 5.5 %collective-permute-start.4 = (bf16[4,40,128]{2,1,0:T(8,128)(2,1)S(1)}, bf16[4,40,128]{2,1,0:T(8,128)(2,1)S(1)}, u32[]{:S(2)}, u32[]{:S(2)}) collective-permute-start(bf16[4,40,128]{2,1,0:T(8,128)(2,1)S(1)} %get-tuple-element.43), channel_id=1, source_target_pairs={{0,2},{1,3},{2,0},{3,1},{4,6},{5,7},{6,4},{7,5},{8,10},{9,11},{10,... | collective-permute-start | bytes 122888 | tf_op jit(solution)/shard_map/ppermute | solution.py:393
  141.5 5.7 %collective-permute-start.3 = (bf16[4,40,128]{2,1,0:T(8,128)(2,1)S(1)}, bf16[4,40,128]{2,1,0:T(8,128)(2,1)S(1)}, u32[]{:S(2)}, u32[]{:S(2)}) collective-permute-start(bf16[4,40,128]{2,1,0:T(8,128)(2,1)S(1)} %get-tuple-element.44), channel_id=1, source_target_pairs={{0,3},{1,2},{2,1},{3,0},{4,7},{5,6},{6,5},{7,4},{8,11},{9,10},{10,... | collective-permute-start | bytes 122888 | tf_op jit(solution)/shard_map/ppermute | solution.py:393
  147.9 10.5 %all-to-all-start.5 = ((f32[4,16,128]{2,1,0:T(8,128)}), f32[4,16,128]{2,1,0:T(8,128)S(1)}, u32[]{:S(2)}, u32[]{:S(2)}) async-start(f32[4,16,128]{2,1,0:T(8,128)} %broadcast_in_dim.16), calls=%async_computation.5 | async-start | bytes 65536 | tf_op jit(solution)/shard_map/all_to_all | solution.py:404
Sparse Core Ops, SparseCore 0:
  24.8 76.9 all-gather.1
